TPU v7x, 32 devices: a whole 2x2x4 slice. The times are simulated.
32 devices in a mesh: groups: 2 (over x), dp: 16 (over z, y, core).
Axes of the slice: x: 2, y: 2, z: 4, core: 2. Of those that a mesh axis runs over, the one named last changes fastest.
Arguments:
- train_features: bfloat16 [4096, 4096], P(None, ('groups', 'dp')), parts along dimension 1, may hold values from -0.099609375 to 0.099609375
- query_gradients: bfloat16 [4096, 32768], P(None, ('groups', 'dp')), parts along dimension 1, may hold values from -6 to 6
- block_pairs: int32 [64, 2], P(('groups', 'dp')), parts along dimension 0, may hold values from 0 to 127, as said below
- basis_out: float32 [128, 64], P('groups'), parts along dimension 0, may hold values from -0.75 to 0.75
- basis_in: float32 [128, 64], P('groups'), parts along dimension 0, may hold values from -0.75 to 0.75
- eigen_out: float32 [128], P('groups'), parts along dimension 0, may hold values from 0.1 to 2
- eigen_in: float32 [128], P('groups'), parts along dimension 0, may hold values from 0.1 to 2
- damping: float32 [2], P('groups'), parts along dimension 0, may hold values from 0.2 to 1
Outputs:
- scores: float32 [64, 128, 128], P(('groups', 'dp')), parts along dimension 0
There are 2 independent parts, one for each index of `groups`. A program takes and returns all parts, laid end to end along the dimension named above; each array names one. Nothing has to cross between parts.
Inputs may be any that keep to these rules, and one draw needn't show every extreme that they name: `block_pairs`: each row is a pair (training block t, query block u); block b means examples b * 128 to (b + 1) * 128 - 1. The first column is below 16 and every training block appears in it. Of the 8 query blocks of one device, exactly 4 appear in the second column on 2 of the devices and exactly one on each other device.
All inputs are finite; a program needn't handle non-finite values.
Results may differ from a plain program's by a relative error of at most 0.0029.
Values may be sent and summed in bfloat16 or wider, within the bound.
No kernel may reach another device: no remote copies, remote signals or barrier semaphores. Data moves between devices by JAX's collectives and lax.ppermute only.
A program may use at most 128 MiB of HBM per device.

v0:
```python
import jax
import jax.numpy as jnp
from jax import lax
from jax.sharding import PartitionSpec as P

PROJ_OUT = 64
PROJ_IN = 64
BLOCK_ROWS = 128


def precondition(gradients, basis_out, basis_in, eigen_out, eigen_in, damping):
    highest = lax.Precision.HIGHEST
    rotated = jnp.einsum("bi,abq->iaq", basis_in, gradients, precision=highest)
    spectral = jnp.einsum("ao,iaq->oiq", basis_out, rotated, precision=highest)
    scaled = spectral / (eigen_out[:, None, None] * eigen_in[None, :, None] + damping[0])
    partway = jnp.einsum("bi,oiq->boq", basis_in, scaled, precision=highest)
    return jnp.einsum("ao,boq->abq", basis_out, partway, precision=highest)


def body(
    train_features, query_gradients, block_pairs, basis_out, basis_in, eigen_out, eigen_in, damping
):
    feature_count = query_gradients.shape[0]
    local_columns = query_gradients.shape[1]
    local_blocks = local_columns // BLOCK_ROWS
    pair_lists = lax.all_gather(block_pairs, "dp", axis=0, tiled=True)
    train_share = lax.all_to_all(train_features, "dp", split_axis=0, concat_axis=1, tiled=True)
    share_width = train_share.shape[0]

    def one_block(block_index, buffer):
        first = (block_index * BLOCK_ROWS).astype(jnp.int32)
        columns = lax.dynamic_slice_in_dim(query_gradients, first, BLOCK_ROWS, 1)
        gradients = columns.astype(jnp.float32).reshape(PROJ_OUT, PROJ_IN, BLOCK_ROWS)
        result = precondition(gradients, basis_out, basis_in, eigen_out, eigen_in, damping)
        result = result.astype(jnp.bfloat16).reshape(feature_count, BLOCK_ROWS)
        return lax.dynamic_update_slice_in_dim(buffer, result, first, 1)

    outgoing = lax.fori_loop(
        0, local_blocks, one_block, jnp.zeros((feature_count, local_columns), jnp.bfloat16)
    )
    query_share = lax.all_to_all(outgoing, "dp", split_axis=0, concat_axis=1, tiled=True)
    positions = pair_lists[:, 1]
    train_tiles = train_share.reshape(share_width, -1, BLOCK_ROWS)
    query_tiles = query_share.reshape(share_width, -1, BLOCK_ROWS)
    left_blocks = jnp.take(train_tiles, pair_lists[:, 0], axis=1)
    right_blocks = jnp.take(query_tiles, positions, axis=1)
    return lax.psum_scatter(
        jnp.einsum("fpx,fpy->pxy", left_blocks, right_blocks, preferred_element_type=jnp.float32),
        "dp",
        scatter_dimension=0,
        tiled=True,
    )


def solution(mesh):
    placed = (
        P(None, ("groups", "dp")),
        P(None, ("groups", "dp")),
        P(("groups", "dp"), None),
        P("groups", None),
        P("groups", None),
        P("groups"),
        P("groups"),
        P("groups"),
    )
    return jax.shard_map(
        body, mesh=mesh, in_specs=placed, out_specs=P(("groups", "dp"), None, None), check_vma=False
    )
```

profile of v0, /device:TPU:0, one launch (start us, length us, event | category | flops | bytes accessed | tf_op | source)
XLA Modules:
  0.0 445.1 jit_solution(186866385729107794)
XLA Ops:
  6.5 7.4 %all-to-all-start = ((bf16[16,256,128]{2,1,0:T(8,128)(2,1)}), bf16[16,256,128]{2,1,0:T(8,128)(2,1)S(1)}, u32[]{:S(2)}, u32[]{:S(2)}) async-start(bf16[16,256,128]{2,1,0:T(8,128)(2,1)} %bitcast.74), calls=%async_computation | async-start | bytes 2097152 | tf_op jit(solution)/shard_map/all_to_all | solution.py:27
  14.0 4.3 broadcast_in_dim.30
  18.3 125.2 %while.13 = (s32[]{:T(128)}, bf16[4096,1024]{1,0:T(8,128)(2,1)}, bf16[4096,1024]{1,0:T(8,128)(2,1)}, f32[64,64]{1,0:T(8,128)S(1)}, f32[64,64]{1,0:T(8,128)S(1)},...) while((s32[]{:T(128)}, bf16[4096,1024]{1,0:T(8,128)(2,1)}, ...), condition=%wide.region_1.0_spmd, body=%wide.region_0.0_spmd.sunk | while | flops 1611669504 | bytes 21070520 | solution.py:38
  18.3 1.3 constant_dynamic-slice_fusion.2
  21.4 4.2 bitcast_divide_fusion.2
  25.6 3.3 fusion.52
  28.9 3.3 fusion.53
  32.8 1.2 constant_dynamic-update-slice_fusion.2
  34.0 1.3 constant_dynamic-slice_fusion.2
  37.1 4.2 bitcast_divide_fusion.2
  41.2 3.3 fusion.52
  44.5 3.3 fusion.53
  48.5 1.2 constant_dynamic-update-slice_fusion.2
  49.7 1.3 constant_dynamic-slice_fusion.2
  52.8 4.2 bitcast_divide_fusion.2
  56.9 3.3 fusion.52
  60.2 3.3 fusion.53
  65.3 1.3 constant_dynamic-slice_fusion.2
  68.4 4.2 bitcast_divide_fusion.2
  72.6 3.3 fusion.52
  75.8 3.3 fusion.53
  79.8 1.1 constant_dynamic-update-slice_fusion.2
  80.9 1.3 constant_dynamic-slice_fusion.2
  84.0 4.2 bitcast_divide_fusion.2
  88.2 3.3 fusion.52
  91.5 3.3 fusion.53
  96.5 1.3 constant_dynamic-slice_fusion.2
  99.6 4.2 bitcast_divide_fusion.2
  103.8 3.3 fusion.52
  107.1 3.3 fusion.53
  111.0 1.1 constant_dynamic-update-slice_fusion.2
  112.2 1.3 constant_dynamic-slice_fusion.2
  115.3 4.2 bitcast_divide_fusion.2
  119.4 3.3 fusion.52
  122.7 3.3 fusion.53
  126.7 1.1 constant_dynamic-update-slice_fusion.2
  127.8 1.3 constant_dynamic-slice_fusion.2
  130.9 4.2 bitcast_divide_fusion.2
  135.1 3.3 fusion.52
  138.3 3.3 fusion.53
  142.3 1.1 constant_dynamic-update-slice_fusion.2
  143.5 6.2 %all-to-all-start.1 = ((bf16[16,256,1024]{2,1,0:T(8,128)(2,1)}), bf16[16,256,1024]{2,1,0:T(8,128)(2,1)}, u32[]{:S(2)}, u32[]{:S(2)}) async-start(bf16[16,256,1024]{2,1,0:T(8,128)(2,1)} %bitcast.71), calls=%async_computation.1 | async-start | bytes 16777216 | tf_op jit(solution)/shard_map/all_to_all | solution.py:41
  149.7 151.4 %all-gather = s32[16,2,2]{2,1,0:T(2,128)S(1)} all-gather(s32[1,2,2]{2,1,0:T(2,128)S(1)} %bitcast.76), channel_id=1, replica_groups=mesh['groups'=2,'dp'=16] {'dp'}, dimensions={0}, use_global_device_ids=true | all-gather | bytes 272 | tf_op jit(solution)/shard_map/all_gather | solution.py:26
  302.3 12.3 %copy.32 = bf16[256,16,1024]{0,2,1:T(8,128)(2,1)} copy(bf16[256,16,1024]{2,0,1:T(8,128)(2,1)} %bitcast.20) | data formatting | bytes 16777216 | tf_op jit(solution)/shard_map/all_to_all | solution.py:41
  314.6 12.0 %copy.33 = bf16[256,128,128]{2,0,1:T(8,128)(2,1)} copy(bf16[256,128,128]{0,2,1:T(8,128)(2,1)} %bitcast.72) | data formatting | bytes 16777216 | tf_op jit(solution)/shard_map/reshape | solution.py:44
  326.6 5.6 %gather_fusion.1 = bf16[32,256,128]{2,1,0:T(8,128)(2,1)} fusion(bf16[256,128,128]{2,0,1:T(8,128)(2,1)} %copy.33, s32[1024]{0:T(1024)S(1)} %pad_clamp_fusion), kind=kCustom, calls=%fused_computation.1 | custom fusion | bytes 4194432 | tf_op jit(solution)/shard_map/jit(_take)/gather | solution.py:46
  332.2 3.8 fusion.21
  336.0 102.2 %reduce-scatter.2.cloned.1.call-done = f32[2,128,128]{2,1,0:T(8,128)} async-done(((f32[32,128,128]{2,1,0:T(8,128)}), f32[2,128,128]{2,1,0:T(8,128)}) %reduce-scatter.2.cloned.1.call-update) | async-done | bytes 131088 | tf_op jit(solution)/shard_map/reduce_scatter | solution.py:47
  (49 shorter events, 23.1 us)
Async XLA Ops:
  6.5 136.9 %all-to-all-start = ((bf16[16,256,128]{2,1,0:T(8,128)(2,1)}), bf16[16,256,128]{2,1,0:T(8,128)(2,1)S(1)}, u32[]{:S(2)}, u32[]{:S(2)}) async-start(bf16[16,256,128]{2,1,0:T(8,128)(2,1)} %bitcast.74), calls=%async_computation | async-start | bytes 2097152 | tf_op jit(solution)/shard_map/all_to_all | solution.py:27
  13.9 4.4 copy-start
  13.9 4.3 copy-start.1
  14.0 4.3 copy-start.2
  14.0 4.3 copy-start.3
  143.5 6.2 %copy-start.4 = (s32[2,2]{1,0:T(2,128)S(1)}, s32[2,2]{1,0:T(2,128)}, u32[]{:S(2)}) copy-start(s32[2,2]{1,0:T(2,128)} %param.12) | copy-start | bytes 52
  143.5 158.9 %all-to-all-start.1 = ((bf16[16,256,1024]{2,1,0:T(8,128)(2,1)}), bf16[16,256,1024]{2,1,0:T(8,128)(2,1)}, u32[]{:S(2)}, u32[]{:S(2)}) async-start(bf16[16,256,1024]{2,1,0:T(8,128)(2,1)} %bitcast.71), calls=%async_computation.1 | async-start | bytes 16777216 | tf_op jit(solution)/shard_map/all_to_all | solution.py:41
  149.7 288.6 %reduce-scatter.2.cloned.1.call-start = ((), (), s32[]{:S(2)}) async-start(), calls=%async_computation.3 | async-start | bytes 2228224 | tf_op jit(solution)/shard_map/reduce_scatter | solution.py:47
Sparse Core Ops, SparseCore 0:
  336.1 102.0 reduce-scatter.1
where the time goes:
time: 446 us; the launch traced here: 445 us
  blocking collectives  151 us (34%)
  waiting for transfers between devices  102 us (23%)
  matrix products  98 us (22%)
  local copies, waits for them, and re-layouts  60.2 us (13%)
  starting transfers between devices  13.6 us (3%)
  between operations  13.5 us (3%)
  other arithmetic  5.79 us (1%)
    all_gather x1, blocking collectives, body(): pair_lists = lax.all_gather(block_pairs, 'dp', axis=0, tiled=True)  151 us
    reduce_scatter x1, waiting for transfers between devices, body(): lax.psum_scatter(jnp.einsum('fpx,fpy->pxy', left_blocks, right_blocks, pr...  102 us
    dot_general x8, matrix products, precondition(): spectral = jnp.einsum('ao,iaq->oiq', basis_out, rotated, precision=highest)  33.3 us
    dot_general x8, matrix products, precondition(): partway = jnp.einsum('bi,oiq->boq', basis_in, scaled, precision=highest)  26.3 us
    dot_general x8, matrix products, precondition(): return jnp.einsum('ao,boq->abq', basis_out, partway, precision=highest)  26.1 us
    all_to_all x1, local copies, waits for them, and re-layouts, body(): lax.all_to_all(outgoing, 'dp', split_axis=0, concat_axis=1, tiled=True)  12.3 us
    reshape x1, local copies, waits for them, and re-layouts, body(): query_tiles = query_share.reshape(share_width, -1, BLOCK_ROWS)  12 us
    dynamic_slice x8, local copies, waits for them, and re-layouts, one_block(): columns = lax.dynamic_slice_in_dim(query_gradients, first, BLOCK_ROWS, 1)  10.3 us
  transfers between devices with their start and end apart: 3, of which 1 were waited for; matrix products, arithmetic and copies ran while one was open for 29% of the time, Pallas kernels for 0%

commit v1 on v0

v1 whole, which is shorter than its diff:
```python
import functools

import jax
import jax.numpy as jnp
from jax import lax
from jax.experimental import pallas as pl
from jax.experimental.pallas import tpu as pltpu
from jax.sharding import PartitionSpec as P

SIDE = 64
COLS = 128
NAMED_MOST = 4
EXTRA = NAMED_MOST - 1
GROUPED = 4
WIDE = GROUPED * SIDE
TILES = SIDE // GROUPED
VMEM_LIMIT = 40 * 1024 * 1024
f32, bf16 = jnp.float32, jnp.bfloat16


def split(x):
    high = x.astype(bf16)
    return high, (x - high.astype(f32)).astype(bf16)


def mm(a, b):
    return jnp.dot(a, b, preferred_element_type=f32)


def mm_nt(a, b):
    return lax.dot_general(a, b, (((1,), (1,)), ((), ())), preferred_element_type=f32)


def mm3(a, b):
    return mm(a[0], b[0]) + (mm(a[0], b[1]) + mm(a[1], b[0]))


def iota(shape, axis):
    return lax.broadcasted_iota(jnp.int32, shape, axis)


def chosen(cond):
    return jnp.where(cond, 1.0, 0.0).astype(bf16)


def precondition_kernel(train, basis_in, basis_out, inverse, out, y_high, y_low, z_high, z_low):
    tall, flat, square = (WIDE, SIDE), (SIDE, WIDE), (WIDE, WIDE)
    pick_i = chosen(iota(tall, 0) // GROUPED == iota(tall, 1))
    pick_i_t = chosen(iota(flat, 1) // GROUPED == iota(flat, 0))
    pick_low = chosen(iota(tall, 0) % SIDE == iota(tall, 1))
    pick_low_t = chosen(iota(flat, 1) % SIDE == iota(flat, 0))
    row_a = iota(tall, 0) // (GROUPED * GROUPED) * GROUPED + iota(tall, 0) % GROUPED
    pick_a = chosen(row_a == iota(tall, 1))
    col_a = iota(flat, 1) // (GROUPED * GROUPED) * GROUPED + iota(flat, 1) % GROUPED
    pick_a_t = chosen(col_a == iota(flat, 0))
    r, c = iota(square, 0), iota(square, 1)
    same_in = r % GROUPED == c // SIDE
    same_in_t = c % GROUPED == r // SIDE
    same_out = r // GROUPED % GROUPED == c // SIDE
    same_out_t = c // GROUPED % GROUPED == r // SIDE

    def masked(cond, x):
        return jnp.where(cond, x, 0.0).astype(bf16)

    in_parts, out_parts = split(basis_in[...]), split(basis_out[...])
    w_in = [masked(same_in, mm(mm_nt(pick_i, b).astype(bf16), pick_low_t)) for b in in_parts]
    w_in_t = [masked(same_in_t, mm(mm(pick_low, b).astype(bf16), pick_i_t)) for b in in_parts]
    w_out = [masked(same_out, mm(mm(pick_a, b).astype(bf16), pick_low_t)) for b in out_parts]
    w_out_t = [masked(same_out_t, mm(mm_nt(pick_low, b).astype(bf16), pick_a_t)) for b in out_parts]

    for A in range(0, TILES, 2):
        x = jnp.concatenate([train[pl.ds((A + k) * WIDE, WIDE), :] for k in range(2)], axis=1)
        high, low = split(mm(w_in[0], x) + mm(w_in[1], x))
        for k in range(2):
            y_high[A + k] = high[:, k * COLS : (k + 1) * COLS].reshape(TILES, -1, COLS)
            y_low[A + k] = low[:, k * COLS : (k + 1) * COLS].reshape(TILES, -1, COLS)
    for g in range(0, TILES, 2):
        y = [jnp.concatenate([ref[:, g + k].reshape(WIDE, COLS) for k in range(2)], axis=1) for ref in (y_high, y_low)]
        s = mm3(w_out_t, y)
        factor = [jnp.broadcast_to(inverse[:, g + k : g + k + 1], (WIDE, COLS)) for k in range(2)]
        high, low = split(mm3(w_out, split(s * jnp.concatenate(factor, axis=1))))
        for k in range(2):
            z_high[:, g + k] = high[:, k * COLS : (k + 1) * COLS].reshape(TILES, -1, COLS)
            z_low[:, g + k] = low[:, k * COLS : (k + 1) * COLS].reshape(TILES, -1, COLS)
    share = out.shape[2]
    for A in range(0, TILES, 2):
        z = [jnp.concatenate([ref[A + k].reshape(WIDE, COLS) for k in range(2)], axis=1) for ref in (z_high, z_low)]
        result = mm3(w_in_t, z)
        for k in range(2):
            turned = result[:, k * COLS : (k + 1) * COLS].T.astype(bf16)
            for part in range(WIDE // share):
                out[(A + k) * (WIDE // share) + part] = turned[:, part * share : (part + 1) * share]


def precondition(train, basis_in, basis_out, inverse, chunks):
    features = train.shape[0]
    tiled = pltpu.VMEM((TILES, TILES, WIDE // TILES, COLS), bf16)
    return pl.pallas_call(
        precondition_kernel,
        out_shape=jax.ShapeDtypeStruct((chunks, COLS, features // chunks), bf16),
        in_specs=[pl.BlockSpec(memory_space=pltpu.VMEM)] * 4,
        out_specs=pl.BlockSpec(memory_space=pltpu.VMEM),
        scratch_shapes=[tiled] * 4,
        compiler_params=pltpu.CompilerParams(vmem_limit_bytes=VMEM_LIMIT),
        cost_estimate=pl.CostEstimate(flops=3_000_000_000, bytes_accessed=4 * features * COLS, transcendentals=0),
        name="precondition",
    )(train, basis_in, basis_out, inverse)


def score_kernel(per_device, rows, train, first, extra, keep, send):
    core = rows[2, 0]
    devices = first.shape[0]

    def tile(pair):
        slot = rows[1, pair]
        a = first[jnp.minimum(slot, devices - 1)]
        b = extra[jnp.maximum(slot - devices, 0)]
        q = jnp.where(slot < devices, a.astype(f32), b.astype(f32)).astype(bf16)
        return mm(train[rows[0, pair]], q)

    def step(h, carry):
        base = h // per_device * (2 * per_device) + h % per_device
        keep[h] = tile(base + core * per_device)
        send[h] = tile(base + (1 - core) * per_device)
        return carry

    lax.fori_loop(0, keep.shape[0], step, 0, unroll=4)


def partial_scores(rows, per_device, train, first, extra):
    half = rows.shape[1] // 2
    tiles = jax.ShapeDtypeStruct((half, COLS, COLS), f32)
    whole = pl.BlockSpec(memory_space=pltpu.VMEM)
    return pl.pallas_call(
        functools.partial(score_kernel, per_device),
        out_shape=(tiles, tiles),
        in_specs=[pl.BlockSpec(memory_space=pltpu.SMEM), whole, whole, whole],
        out_specs=(whole, whole),
        compiler_params=pltpu.CompilerParams(vmem_limit_bytes=VMEM_LIMIT),
        name="partial_scores",
    )(rows, train, first, extra)


def body(devices, train_features, query_gradients, block_pairs, basis_out, basis_in, eigen_out, eigen_in, damping):
    bits = devices.bit_length() - 1
    me = lax.axis_index("dp")
    mine = [(me >> b) & 1 for b in range(bits)]
    features, local_columns = query_gradients.shape
    local_blocks = local_columns // COLS
    per_device = block_pairs.shape[0]
    share = features // devices
    hot_total = devices // 8

    def across(x, b):
        return lax.ppermute(x, "dp", [(d, d ^ (1 << b)) for d in range(devices)])

    pairs = block_pairs
    for b in range(bits):
        other = across(pairs, b)
        pairs = jnp.where(mine[b] == 0, jnp.concatenate([pairs, other]), jnp.concatenate([other, pairs]))

    inverse = 1.0 / (eigen_out[None, :, None] * eigen_in.reshape(TILES, GROUPED).T[:, None, :] + damping[0])
    conditioned = precondition(train_features, basis_in, basis_out, inverse.reshape(WIDE, TILES), devices)
    train_share = lax.all_to_all(conditioned, "dp", split_axis=0, concat_axis=0, tiled=True)

    blocks = jnp.arange(devices * local_blocks, dtype=jnp.int32)
    named = jnp.any(pairs[:, 1:2] == blocks[None, :], axis=0).reshape(devices, local_blocks)
    ahead = jnp.arange(local_blocks)[:, None] < jnp.arange(local_blocks)[None, :]
    order = jnp.sum(jnp.where(named[:, :, None] & ahead[None], 1, 0), axis=1)
    hot = jnp.sum(named.astype(jnp.int32), axis=1) > 1
    earlier = jnp.arange(devices)[:, None] < jnp.arange(devices)[None, :]
    hot_order = jnp.sum(jnp.where(hot[:, None] & earlier, 1, 0), axis=0)
    slot = jnp.where(
        order == 0, jnp.arange(devices)[:, None], devices + EXTRA * hot_order[:, None] + order - 1
    ).reshape(-1)
    pair_slot = jnp.sum(jnp.where(pairs[:, 1:2] == blocks[None, :], slot[None, :], 0), axis=1)
    rows = jnp.stack([pairs[:, 0], pair_slot, jnp.broadcast_to(mine[0], pair_slot.shape)]).astype(jnp.int32)

    own_named = lax.dynamic_index_in_dim(named, me, 0, False)
    own_order = lax.dynamic_index_in_dim(order, me, 0, False)
    local_ids = jnp.arange(local_blocks, dtype=jnp.int32)

    def named_block(k):
        which = jnp.sum(jnp.where(own_named & (own_order == k), local_ids, 0))
        return lax.dynamic_slice_in_dim(query_gradients, which * COLS, COLS, 1)

    own = jnp.stack([named_block(k) for k in range(1, NAMED_MOST)])
    own = own.reshape((EXTRA,) + (2,) * bits + (share, COLS))

    def halves(x, b, left):
        axis = 1 + [k for k in sorted(left, reverse=True)].index(b)
        keep = lax.dynamic_index_in_dim(x, mine[b], axis, False)
        return keep, lax.dynamic_index_in_dim(x, 1 - mine[b], axis, False)

    keep, send = halves(own, 0, list(range(bits)))
    other = across(send, 0)
    chains = []
    for rank in range(hot_total):
        is_rank = hot & (hot_order == rank)
        from_me = is_rank[me]
        from_other = is_rank[me ^ 1]
        x = jnp.where(from_me, keep, jnp.where(from_other, other, jnp.zeros_like(other)))
        rest = list(range(1, bits))
        turn = rank % 2
        chains.append([x, rest[turn : turn + 1] + rest[:turn] + rest[turn + 1 :], rest])

    first_share = lax.all_to_all(
        named_block(0).reshape(devices, share, COLS), "dp", split_axis=0, concat_axis=0, tiled=True
    )

    for _ in range(1, bits):
        for chain in chains:
            x, todo, left = chain
            b = todo.pop(0)
            keep, send = halves(x, b, left)
            left.remove(b)
            chain[0] = keep + across(send, b)
    extra_share = jnp.concatenate([chain[0] for chain in chains], axis=0)

    keep, send = partial_scores(rows, per_device, train_share, first_share, extra_share)
    tiles = keep + across(send, 0)
    tiles = tiles.reshape((2,) * (bits - 1) + (per_device, COLS, COLS))
    for b in range(1, bits):
        axis = bits - 1 - b
        keep = lax.dynamic_index_in_dim(tiles, mine[b], axis, False)
        send = lax.dynamic_index_in_dim(tiles, 1 - mine[b], axis, False)
        if b == 1:
            tiles = keep + across(send.astype(bf16), b).astype(f32)
        else:
            tiles = keep + across(send, b)
    return tiles


def solution(mesh):
    placed = (
        P(None, ("groups", "dp")),
        P(None, ("groups", "dp")),
        P(("groups", "dp"), None),
        P("groups", None),
        P("groups", None),
        P("groups"),
        P("groups"),
        P("groups"),
    )
    return jax.shard_map(
        functools.partial(body, mesh.shape["dp"]),
        mesh=mesh,
        in_specs=placed,
        out_specs=P(("groups", "dp"), None, None),
        check_vma=False,
    )
```

time: 446 us -> 156 us (0.35)
  blocking collectives: 151 us -> 0 us
  matrix products: 98 us -> 0 us
  local copies, waits for them, and re-layouts: 60.2 us -> 11.7 us
  starting transfers between devices: 13.6 us -> 32.9 us
  waiting for transfers between devices: 102 us -> 89 us
  between operations: 13.5 us -> 3.58 us
  Pallas kernels: 0 us -> 7.55 us
  other arithmetic: 5.79 us -> 11.3 us
    all_gather x1 -> x0, blocking collectives: 151 us -> none  [body(): pair_lists = lax.all_gather(block_pairs, 'dp', axis=0, tiled=True)]
    reduce_scatter x1 -> x0, waiting for transfers between devices: 102 us -> none  [body(): lax.psum_scatter(jnp.einsum('fpx,fpy->pxy', left_blocks, right_blocks, pr...]
    dot_general x33 -> x0, matrix products: 98 us -> none  [the longest x8 33.3 us: precondition(): spectral = jnp.einsum('ao,iaq->oiq', basis_out, rotated, precision=highest)]
    ppermute x0 -> x15, waiting for transfers between devices: none -> 89 us  [across(): return lax.ppermute(x, 'dp', [(d, d ^ 1 << b) for d in range(devices)])]
    ppermute x0 -> x15, starting transfers between devices: none -> 21.4 us  [across(): return lax.ppermute(x, 'dp', [(d, d ^ 1 << b) for d in range(devices)])]
    all_to_all x1 -> x0, local copies, waits for them, and re-layouts: 12.3 us -> none  [body(): lax.all_to_all(outgoing, 'dp', split_axis=0, concat_axis=1, tiled=True)]
    reshape x1, local copies, waits for them, and re-layouts: 12 us -> 0.08 us  [body(): eigen_in.reshape(TILES, GROUPED).T[:, None, :]]
    dynamic_update_slice x8 -> x0, local copies, waits for them, and re-layouts: 9.11 us -> none  [one_block(): return lax.dynamic_update_slice_in_dim(buffer, result, first, 1)]
  transfers between devices with their start and end apart: 3 -> 17, of which waited for: 1 -> 12; matrix products, arithmetic and copies ran while one was open for 29% -> 7% of each run, Pallas kernels for 0% -> 4%
where the time goes in v1:
time: 156 us
  waiting for transfers between devices  89 us (57%)
  starting transfers between devices  32.9 us (21%)
  local copies, waits for them, and re-layouts  11.7 us (8%)
  other arithmetic  11.3 us (7%)
  Pallas kernels  7.55 us (5%)
  between operations  3.58 us (2%)
    ppermute x15, waiting for transfers between devices, across(): return lax.ppermute(x, 'dp', [(d, d ^ 1 << b) for d in range(devices)])  89 us
    ppermute x15, starting transfers between devices, across(): return lax.ppermute(x, 'dp', [(d, d ^ 1 << b) for d in range(devices)])  21.4 us
    all_to_all x1, starting transfers between devices, body(): lax.all_to_all(conditioned, 'dp', split_axis=0, concat_axis=0, tiled=True)  6.34 us
    pallas_call x1, Pallas kernels, precondition(): pl.pallas_call(precondition_kernel, out_shape=jax.ShapeDtypeStruct((chunk...  5.65 us
    all_to_all x1, starting transfers between devices, body(): lax.all_to_all(named_block(0).reshape(devices, share, COLS), 'dp', split_...  5.17 us
    select_n x1, other arithmetic, body(): jnp.where(from_me, keep, jnp.where(from_other, other, jnp.zeros_like(othe...  4.51 us
    unnamed x21, local copies, waits for them, and re-layouts  3.88 us
    dynamic_slice x1, local copies, waits for them, and re-layouts, named_block(): return lax.dynamic_slice_in_dim(query_gradients, which * COLS, COLS, 1)  3.85 us
  transfers between devices with their start and end apart: 17, of which 12 were waited for; matrix products, arithmetic and copies ran while one was open for 7% of the time, Pallas kernels for 4%

profile of v1, /device:TPU:0, one launch (start us, length us, event | category | flops | bytes accessed | tf_op | source)
XLA Modules:
  0.0 156.0 jit_solution(1891171993458946105)
XLA Ops:
  0.0 0.8 copy.40
  0.8 0.5 collective-permute-start
  1.2 0.8 collective-permute-done
  2.1 2.8 %collective-permute-start.1 = (s32[4,2]{0,1:T(2,128)S(1)}, s32[4,2]{0,1:T(2,128)S(1)}, u32[]{:S(2)}, u32[]{:S(2)}) collective-permute-start(s32[4,2]{0,1:T(2,128)S(1)} %add_select_fusion.1), channel_id=1, source_target_pairs={{0,2},{1,3},{2,0},{3,1},{4,6},{5,7},{6,4},{7,5},{8,10},{9,11},{10,... | collective-permute-start | bytes 104 | tf_op jit(solution)/shard_map/ppermute | solution.py:155
  5.0 1.5 collective-permute-done.1
  6.6 2.1 %collective-permute-start.2 = (s32[8,2]{0,1:T(2,128)S(1)}, s32[8,2]{0,1:T(2,128)S(1)}, u32[]{:S(2)}, u32[]{:S(2)}) collective-permute-start(s32[8,2]{0,1:T(2,128)S(1)} %add_select_fusion.2), channel_id=1, source_target_pairs={{0,4},{1,5},{2,6},{3,7},{4,0},{5,1},{6,2},{7,3},{8,12},{9,13},{10,... | collective-permute-start | bytes 200 | tf_op jit(solution)/shard_map/ppermute | solution.py:155
  8.7 1.5 collective-permute-done.2
  10.3 3.0 %collective-permute-start.3 = (s32[16,2]{0,1:T(2,128)S(1)}, s32[16,2]{0,1:T(2,128)S(1)}, u32[]{:S(2)}, u32[]{:S(2)}) collective-permute-start(s32[16,2]{0,1:T(2,128)S(1)} %add_select_fusion.3), channel_id=1, source_target_pairs={{0,8},{1,9},{2,10},{3,11},{4,12},{5,13},{6,14},{7,15},{8,0},{9,1},... | collective-permute-start | bytes 392 | tf_op jit(solution)/shard_map/ppermute | solution.py:155
  13.3 1.5 collective-permute-done.3
  15.3 0.2 and_reduce_fusion.2
  15.5 0.7 select_reduce_fusion.5
  17.5 0.7 select_reduce_fusion.3
  19.5 3.8 %constant_dynamic-slice_fusion.6 = (bf16[4096,128]{1,0:T(8,128)(2,1)S(1)}, bf16[4096,128]{1,0:T(8,128)(2,1)}, bf16[4096,128]{1,0:T(8,128)(2,1)S(1)}, bf16[4096,128]{1,0:T(8,128)(2,1)S(1)}) fusion(bf16[4096,1024]{1,0:T(8,128)(2,1)} %param.9, s32[]{:T(128)S(6)} %select_n.180, s32[]{:T(128)S(6)} %select_n.177, s32[]{:T(128)S(6)} %select_n.184, s32[]{:T(128)S(6)} %select_n.182), kind=kLoop, calls=%fused_computation.41 | loop fusion | bytes 8388624 | tf_op jit(solution)/shard_map/dynamic_slice | solution.py:185
  23.4 0.3 pad_maximum_fusion
  23.8 1.3 dynamic-slice_bitcast_fusion
  25.1 0.8 copy-done.3
  26.8 0.1 fusion.2.inverse
  27.0 5.6 %precondition.1 = bf16[16,128,256]{2,1,0:T(8,128)(2,1)} custom-call(bf16[4096,128]{1,0:T(8,128)(2,1)S(1)} %copy-done, f32[64,64]{1,0:T(8,128)S(1)} %copy-done.1, f32[64,64]{1,0:T(8,128)S(1)} %copy-done.2, f32[256,16]{1,0:T(8,128)S(1)} %fusion.2.inverse), custom_call_target="tpu_custom_call" | custom-call | flops 3000000000 | bytes 2097152 | tf_op jit(solution)/shard_map/precondition/pallas_call | solution.py:98
  32.6 6.3 %all-to-all-start = ((bf16[16,128,256]{2,1,0:T(8,128)(2,1)}), bf16[16,128,256]{2,1,0:T(8,128)(2,1)S(1)}, u32[]{:S(2)}, u32[]{:S(2)}) async-start(bf16[16,128,256]{2,1,0:T(8,128)(2,1)} %precondition.1), calls=%async_computation | async-start | bytes 2097152 | tf_op jit(solution)/shard_map/all_to_all | solution.py:164
  39.0 0.1 convert_reduce_fusion
  39.2 0.7 fusion.5
  39.9 1.1 copy-done.7
  41.0 4.5 %bitcast_select_fusion.1 = (bf16[3,2,2,2,256,128]{5,4,3,2,1,0:T(8,128)(2,1)S(1)}, bf16[3,2,2,2,256,128]{5,4,3,2,1,0:T(8,128)(2,1)S(1)}) fusion(bf16[3,2,2,2,256,128]{5,4,3,2,1,0:T(8,128)(2,1)} %copy-done.7, pred[]{:T(512)} %bitcast.12, pred[]{:T(512)} %bitcast.7, bf16[3,2,2,2,2,256,128]{6,5,4,3,2,1,0:T(8,128)(2,1)} %copy-done.3, s32[]{:T(128)S(6)} %select_n.185, ...), kind=kLoop, calls=%fused_computation.2 | loop fusion | flops 3145728 | bytes 6291464 | tf_op jit(solution)/shard_map/jit(_where)/select_n | solution.py:202
  45.5 1.1 copy-done.6
  46.7 2.0 %collective-permute-start.5 = (bf16[3,2,2,256,128]{4,3,2,1,0:T(8,128)(2,1)S(1)}, bf16[3,2,2,256,128]{4,3,2,1,0:T(8,128)(2,1)}, u32[]{:S(2)}, u32[]{:S(2)}) collective-permute-start(bf16[3,2,2,256,128]{4,3,2,1,0:T(8,128)(2,1)S(1)} %dynamic-slice_bitcast_fusion.2), channel_id=1, source_target_pairs={{0,2},{1,3},{2,0},{3,1},{4,6},{5,7},{6,4},{7,5},{8,10},{9,11},{10,... | collective-permute-start | bytes 2359304 | tf_op jit(solution)/shard_map/ppermute | solution.py:155
  48.8 0.9 dynamic-slice_bitcast_fusion.1
  49.7 1.5 collective-permute-start.8
  51.4 0.2 select_reduce_fusion.1
  51.5 20.0 %collective-permute-done.5 = bf16[3,2,2,256,128]{4,3,2,1,0:T(8,128)(2,1)} collective-permute-done((bf16[3,2,2,256,128]{4,3,2,1,0:T(8,128)(2,1)S(1)}, bf16[3,2,2,256,128]{4,3,2,1,0:T(8,128)(2,1)}, u32[]{:S(2)}, u32[]{:S(2)}) %collective-permute-start.5) | collective-permute-done | bytes 786464 | tf_op jit(solution)/shard_map/ppermute | solution.py:155
  71.6 1.5 bitcast_add_fusion.1
  73.0 5.2 %all-to-all-start.1 = ((bf16[16,256,128]{2,1,0:T(8,128)(2,1)}), bf16[16,256,128]{2,1,0:T(8,128)(2,1)S(1)}, u32[]{:S(2)}, u32[]{:S(2)}) async-start(bf16[16,256,128]{2,1,0:T(8,128)(2,1)} %bitcast.6), calls=%async_computation.1 | async-start | bytes 2097152 | tf_op jit(solution)/shard_map/all_to_all | solution.py:207
  78.3 2.0 %collective-permute-start.6 = (bf16[3,2,256,128]{3,2,0,1:T(8,128)(2,1)S(1)}, bf16[3,2,256,128]{3,2,0,1:T(8,128)(2,1)S(1)}, u32[]{:S(2)}, u32[]{:S(2)}) collective-permute-start(bf16[3,2,256,128]{3,2,0,1:T(8,128)(2,1)S(1)} %bitcast.72), channel_id=1, source_target_pairs={{0,4},{1,5},{2,6},{3,7},{4,0},{5,1},{6,2},{7,3},{8,12},{9,13},{10,... | collective-permute-start | bytes 1179656 | tf_op jit(solution)/shard_map/ppermute | solution.py:155
  80.3 1.2 bitcast_add_fusion
  81.6 1.5 collective-permute-start.9
  83.2 23.4 %collective-permute-done.6 = bf16[3,2,256,128]{3,2,0,1:T(8,128)(2,1)S(1)} collective-permute-done((bf16[3,2,256,128]{3,2,0,1:T(8,128)(2,1)S(1)}, bf16[3,2,256,128]{3,2,0,1:T(8,128)(2,1)S(1)}, u32[]{:S(2)}, u32[]{:S(2)}) %collective-permute-start.6) | collective-permute-done | bytes 393248 | tf_op jit(solution)/shard_map/ppermute | solution.py:155
  106.7 2.6 %collective-permute-start.7 = (bf16[3,256,128]{2,1,0:T(8,128)(2,1)S(1)}, bf16[3,256,128]{2,1,0:T(8,128)(2,1)S(1)}, u32[]{:S(2)}, u32[]{:S(2)}) collective-permute-start(bf16[3,256,128]{2,1,0:T(8,128)(2,1)S(1)} %dynamic-slice_bitcast_fusion.5), channel_id=1, source_target_pairs={{0,8},{1,9},{2,10},{3,11},{4,12},{5,13},{6,14},{7,15},{8,0},{9,1},... | collective-permute-start | bytes 589832 | tf_op jit(solution)/shard_map/ppermute | solution.py:155
  109.4 0.5 collective-permute-start.10
  109.9 13.3 %collective-permute-done.7 = bf16[3,256,128]{2,1,0:T(8,128)(2,1)S(1)} collective-permute-done((bf16[3,256,128]{2,1,0:T(8,128)(2,1)S(1)}, bf16[3,256,128]{2,1,0:T(8,128)(2,1)S(1)}, u32[]{:S(2)}, u32[]{:S(2)}) %collective-permute-start.7) | collective-permute-done | bytes 196640 | tf_op jit(solution)/shard_map/ppermute | solution.py:155
  123.2 3.6 %collective-permute-done.10 = bf16[3,256,128]{2,1,0:T(8,128)(2,1)S(1)} collective-permute-done((bf16[3,256,128]{2,1,0:T(8,128)(2,1)S(1)}, bf16[3,256,128]{2,1,0:T(8,128)(2,1)S(1)}, u32[]{:S(2)}, u32[]{:S(2)}) %collective-permute-start.10) | collective-permute-done | bytes 196640 | tf_op jit(solution)/shard_map/ppermute | solution.py:155
  126.8 1.9 %partial_scores.1 = (f32[16,128,128]{2,1,0:T(8,128)S(1)}, f32[16,128,128]{2,1,0:T(8,128)S(1)}) custom-call(s32[3,32]{1,0:T(4,128)S(1)} %add_add_fusion.rows, bf16[16,128,256]{2,1,0:T(8,128)(2,1)S(1)} %all-to-all-done.train, bf16[16,256,128]{2,1,0:T(8,128)(2,1)S(1)} %all-to-all-done.1.first, bf16[6,256,128]{2,1,0:T(8,128)(2,1)S(1)} %pad_maximum_fusion.1.extra), custom_call_target="tpu_custom_call" | custom-call | tf_op jit(solution)/shard_map/partial_scores/pallas_call | solution.py:134
  128.8 2.6 %collective-permute-done.11 = f32[16,128,128]{2,1,0:T(8,128)S(1)} collective-permute-done((f32[16,128,128]{2,1,0:T(8,128)S(1)}, f32[16,128,128]{2,1,0:T(8,128)S(1)}, u32[]{:S(2)}, u32[]{:S(2)}) %collective-permute-start.11) | collective-permute-done | bytes 1048608 | tf_op jit(solution)/shard_map/ppermute | solution.py:155
  131.5 0.1 add.161
  131.6 1.6 %collective-permute-start.12 = (bf16[2,2,2,128,128]{4,3,2,1,0:T(8,128)(2,1)S(1)}, bf16[2,2,2,128,128]{4,3,2,1,0:T(8,128)(2,1)S(1)}, u32[]{:S(2)}, u32[]{:S(2)}) collective-permute-start(bf16[2,2,2,128,128]{4,3,2,1,0:T(8,128)(2,1)S(1)} %fusion), channel_id=1, source_target_pairs={{0,2},{1,3},{2,0},{3,1},{4,6},{5,7},{6,4},{7,5},{8,10},{9,11},{10,... | collective-permute-start | bytes 786440 | tf_op jit(solution)/shard_map/ppermute | solution.py:155
  133.2 6.9 %collective-permute-done.12 = bf16[2,2,2,128,128]{4,3,2,1,0:T(8,128)(2,1)S(1)} collective-permute-done((bf16[2,2,2,128,128]{4,3,2,1,0:T(8,128)(2,1)S(1)}, bf16[2,2,2,128,128]{4,3,2,1,0:T(8,128)(2,1)S(1)}, u32[]{:S(2)}, u32[]{:S(2)}) %collective-permute-start.12) | collective-permute-done | bytes 262176 | tf_op jit(solution)/shard_map/ppermute | solution.py:155
  140.2 7.5 %collective-permute-done.13 = f32[2,2,128,128]{3,2,1,0:T(8,128)S(1)} collective-permute-done((f32[2,2,128,128]{3,2,1,0:T(8,128)S(1)}, f32[2,2,128,128]{3,2,1,0:T(8,128)S(1)}, u32[]{:S(2)}, u32[]{:S(2)}) %collective-permute-start.13) | collective-permute-done | bytes 262176 | tf_op jit(solution)/shard_map/ppermute | solution.py:155
  147.8 1.3 collective-permute-start.14
  149.1 6.3 %collective-permute-done.14 = f32[2,128,128]{2,1,0:T(8,128)S(1)} collective-permute-done((f32[2,128,128]{2,1,0:T(8,128)S(1)}, f32[2,128,128]{2,1,0:T(8,128)S(1)}, u32[]{:S(2)}, u32[]{:S(2)}) %collective-permute-start.14) | collective-permute-done | bytes 131104 | tf_op jit(solution)/shard_map/ppermute | solution.py:155
  155.4 0.7 bitcast_add_fusion.8
  (65 shorter events, 2.2 us)
Async XLA Ops:
  0.8 1.3 collective-permute-start
  2.1 4.4 %collective-permute-start.1 = (s32[4,2]{0,1:T(2,128)S(1)}, s32[4,2]{0,1:T(2,128)S(1)}, u32[]{:S(2)}, u32[]{:S(2)}) collective-permute-start(s32[4,2]{0,1:T(2,128)S(1)} %add_select_fusion.1), channel_id=1, source_target_pairs={{0,2},{1,3},{2,0},{3,1},{4,6},{5,7},{6,4},{7,5},{8,10},{9,11},{10,... | collective-permute-start | bytes 104 | tf_op jit(solution)/shard_map/ppermute | solution.py:155
  6.6 3.6 %collective-permute-start.2 = (s32[8,2]{0,1:T(2,128)S(1)}, s32[8,2]{0,1:T(2,128)S(1)}, u32[]{:S(2)}, u32[]{:S(2)}) collective-permute-start(s32[8,2]{0,1:T(2,128)S(1)} %add_select_fusion.2), channel_id=1, source_target_pairs={{0,4},{1,5},{2,6},{3,7},{4,0},{5,1},{6,2},{7,3},{8,12},{9,13},{10,... | collective-permute-start | bytes 200 | tf_op jit(solution)/shard_map/ppermute | solution.py:155
  10.3 4.6 %collective-permute-start.3 = (s32[16,2]{0,1:T(2,128)S(1)}, s32[16,2]{0,1:T(2,128)S(1)}, u32[]{:S(2)}, u32[]{:S(2)}) collective-permute-start(s32[16,2]{0,1:T(2,128)S(1)} %add_select_fusion.3), channel_id=1, source_target_pairs={{0,8},{1,9},{2,10},{3,11},{4,12},{5,13},{6,14},{7,15},{8,0},{9,1},... | collective-permute-start | bytes 392 | tf_op jit(solution)/shard_map/ppermute | solution.py:155
  23.7 2.2 %copy-start.3 = (bf16[3,2,2,2,2,256,128]{6,5,4,3,2,1,0:T(8,128)(2,1)}, bf16[3,2,2,2,2,256,128]{6,5,4,3,2,1,0:T(8,128)(2,1)S(1)}, u32[]{:S(2)}) copy-start(bf16[3,2,2,2,2,256,128]{6,5,4,3,2,1,0:T(8,128)(2,1)S(1)} %pad_maximum_fusion) | copy-start | bytes 9437188
  23.7 2.2 %copy-start.8 = (f32[64]{0:T(128)S(1)}, f32[64]{0:T(128)}, u32[]{:S(2)}) copy-start(f32[64]{0:T(128)} %param.14) | copy-start | bytes 772
  23.7 2.3 %copy-start.9 = (f32[64]{0:T(128)S(1)}, f32[64]{0:T(128)}, u32[]{:S(2)}) copy-start(f32[64]{0:T(128)} %param.13) | copy-start | bytes 772
  23.7 3.2 %copy-start = (bf16[4096,128]{1,0:T(8,128)(2,1)S(1)}, bf16[4096,128]{1,0:T(8,128)(2,1)}, u32[]{:S(2)}) copy-start(bf16[4096,128]{1,0:T(8,128)(2,1)} %train.1) | copy-start | bytes 3145732
  23.8 3.2 %copy-start.1 = (f32[64,64]{1,0:T(8,128)S(1)}, f32[64,64]{1,0:T(8,128)}, u32[]{:S(2)}) copy-start(f32[64,64]{1,0:T(8,128)} %basis_in.1) | copy-start | bytes 49156
  23.8 3.2 %copy-start.2 = (f32[64,64]{1,0:T(8,128)S(1)}, f32[64,64]{1,0:T(8,128)}, u32[]{:S(2)}) copy-start(f32[64,64]{1,0:T(8,128)} %basis_out.1) | copy-start | bytes 49156
  25.9 14.0 %collective-permute-start.4 = (bf16[3,2,2,2,256,128]{5,4,3,2,1,0:T(8,128)(2,1)}, bf16[3,2,2,2,256,128]{5,4,3,2,1,0:T(8,128)(2,1)S(1)}, u32[]{:S(2)}, u32[]{:S(2)}) collective-permute-start(bf16[3,2,2,2,256,128]{5,4,3,2,1,0:T(8,128)(2,1)} %dynamic-slice_bitcast_fusion), channel_id=1, source_target_pairs={{0,1},{1,0},{2,3},{3,2},{4,5},{5,4},{6,7},{7,6},{8,9},{9,8},{10,11... | collective-permute-start | bytes 4718600 | tf_op jit(solution)/shard_map/ppermute | solution.py:155
  32.6 40.4 %all-to-all-start = ((bf16[16,128,256]{2,1,0:T(8,128)(2,1)}), bf16[16,128,256]{2,1,0:T(8,128)(2,1)S(1)}, u32[]{:S(2)}, u32[]{:S(2)}) async-start(bf16[16,128,256]{2,1,0:T(8,128)(2,1)} %precondition.1), calls=%async_computation | async-start | bytes 2097152 | tf_op jit(solution)/shard_map/all_to_all | solution.py:164
  39.9 1.1 copy-start.7
  45.5 1.1 copy-start.6
  45.5 4.2 %copy-start.4 = (bf16[3,2,2,2,256,128]{5,4,3,2,1,0:T(8,128)(2,1)}, bf16[3,2,2,2,256,128]{5,4,3,2,1,0:T(8,128)(2,1)S(1)}, u32[]{:S(2)}) copy-start(bf16[3,2,2,2,256,128]{5,4,3,2,1,0:T(8,128)(2,1)S(1)} %get-tuple-element.18) | copy-start | bytes 4718596
  46.7 24.8 %collective-permute-start.5 = (bf16[3,2,2,256,128]{4,3,2,1,0:T(8,128)(2,1)S(1)}, bf16[3,2,2,256,128]{4,3,2,1,0:T(8,128)(2,1)}, u32[]{:S(2)}, u32[]{:S(2)}) collective-permute-start(bf16[3,2,2,256,128]{4,3,2,1,0:T(8,128)(2,1)S(1)} %dynamic-slice_bitcast_fusion.2), channel_id=1, source_target_pairs={{0,2},{1,3},{2,0},{3,1},{4,6},{5,7},{6,4},{7,5},{8,10},{9,11},{10,... | collective-permute-start | bytes 2359304 | tf_op jit(solution)/shard_map/ppermute | solution.py:155
  49.7 30.6 %collective-permute-start.8 = (bf16[3,2,2,256,128]{4,3,2,1,0:T(8,128)(2,1)}, bf16[3,2,2,256,128]{4,3,2,1,0:T(8,128)(2,1)}, u32[]{:S(2)}, u32[]{:S(2)}) collective-permute-start(bf16[3,2,2,256,128]{4,3,2,1,0:T(8,128)(2,1)} %dynamic-slice_bitcast_fusion.1), channel_id=1, source_target_pairs={{0,4},{1,5},{2,6},{3,7},{4,0},{5,1},{6,2},{7,3},{8,12},{9,13},{10,... | collective-permute-start | bytes 2359304 | tf_op jit(solution)/shard_map/ppermute | solution.py:155
  73.0 53.8 %all-to-all-start.1 = ((bf16[16,256,128]{2,1,0:T(8,128)(2,1)}), bf16[16,256,128]{2,1,0:T(8,128)(2,1)S(1)}, u32[]{:S(2)}, u32[]{:S(2)}) async-start(bf16[16,256,128]{2,1,0:T(8,128)(2,1)} %bitcast.6), calls=%async_computation.1 | async-start | bytes 2097152 | tf_op jit(solution)/shard_map/all_to_all | solution.py:207
  78.2 2.1 %copy-start.5 = (bf16[3,2,2,2,256,128]{5,4,3,2,1,0:T(8,128)(2,1)S(1)}, bf16[3,2,2,2,256,128]{5,4,3,2,1,0:T(8,128)(2,1)}, u32[]{:S(2)}) copy-start(bf16[3,2,2,2,256,128]{5,4,3,2,1,0:T(8,128)(2,1)} %copy-done.4) | copy-start | bytes 4718596
  78.3 28.3 %collective-permute-start.6 = (bf16[3,2,256,128]{3,2,0,1:T(8,128)(2,1)S(1)}, bf16[3,2,256,128]{3,2,0,1:T(8,128)(2,1)S(1)}, u32[]{:S(2)}, u32[]{:S(2)}) collective-permute-start(bf16[3,2,256,128]{3,2,0,1:T(8,128)(2,1)S(1)} %bitcast.72), channel_id=1, source_target_pairs={{0,4},{1,5},{2,6},{3,7},{4,0},{5,1},{6,2},{7,3},{8,12},{9,13},{10,... | collective-permute-start | bytes 1179656 | tf_op jit(solution)/shard_map/ppermute | solution.py:155
  81.6 27.6 %collective-permute-start.9 = (bf16[3,2,256,128]{3,2,0,1:T(8,128)(2,1)S(1)}, bf16[3,2,256,128]{3,2,0,1:T(8,128)(2,1)S(1)}, u32[]{:S(2)}, u32[]{:S(2)}) collective-permute-start(bf16[3,2,256,128]{3,2,0,1:T(8,128)(2,1)S(1)} %bitcast.73), channel_id=1, source_target_pairs={{0,2},{1,3},{2,0},{3,1},{4,6},{5,7},{6,4},{7,5},{8,10},{9,11},{10,... | collective-permute-start | bytes 1179656 | tf_op jit(solution)/shard_map/ppermute | solution.py:155
  106.7 16.4 %collective-permute-start.7 = (bf16[3,256,128]{2,1,0:T(8,128)(2,1)S(1)}, bf16[3,256,128]{2,1,0:T(8,128)(2,1)S(1)}, u32[]{:S(2)}, u32[]{:S(2)}) collective-permute-start(bf16[3,256,128]{2,1,0:T(8,128)(2,1)S(1)} %dynamic-slice_bitcast_fusion.5), channel_id=1, source_target_pairs={{0,8},{1,9},{2,10},{3,11},{4,12},{5,13},{6,14},{7,15},{8,0},{9,1},... | collective-permute-start | bytes 589832 | tf_op jit(solution)/shard_map/ppermute | solution.py:155
  109.4 17.4 %collective-permute-start.10 = (bf16[3,256,128]{2,1,0:T(8,128)(2,1)S(1)}, bf16[3,256,128]{2,1,0:T(8,128)(2,1)S(1)}, u32[]{:S(2)}, u32[]{:S(2)}) collective-permute-start(bf16[3,256,128]{2,1,0:T(8,128)(2,1)S(1)} %dynamic-slice_bitcast_fusion.4), channel_id=1, source_target_pairs={{0,8},{1,9},{2,10},{3,11},{4,12},{5,13},{6,14},{7,15},{8,0},{9,1},... | collective-permute-start | bytes 589832 | tf_op jit(solution)/shard_map/ppermute | solution.py:155
  128.7 2.7 %collective-permute-start.11 = (f32[16,128,128]{2,1,0:T(8,128)S(1)}, f32[16,128,128]{2,1,0:T(8,128)S(1)}, u32[]{:S(2)}, u32[]{:S(2)}) collective-permute-start(f32[16,128,128]{2,1,0:T(8,128)S(1)} %get-tuple-element.8), channel_id=1, source_target_pairs={{0,1},{1,0},{2,3},{3,2},{4,5},{5,4},{6,7},{7,6},{8,9},{9,8},{10,11... | collective-permute-start | bytes 3145736 | tf_op jit(solution)/shard_map/ppermute | solution.py:155
  131.6 8.4 %collective-permute-start.12 = (bf16[2,2,2,128,128]{4,3,2,1,0:T(8,128)(2,1)S(1)}, bf16[2,2,2,128,128]{4,3,2,1,0:T(8,128)(2,1)S(1)}, u32[]{:S(2)}, u32[]{:S(2)}) collective-permute-start(bf16[2,2,2,128,128]{4,3,2,1,0:T(8,128)(2,1)S(1)} %fusion), channel_id=1, source_target_pairs={{0,2},{1,3},{2,0},{3,1},{4,6},{5,7},{6,4},{7,5},{8,10},{9,11},{10,... | collective-permute-start | bytes 786440 | tf_op jit(solution)/shard_map/ppermute | solution.py:155
  140.2 7.6 %collective-permute-start.13 = (f32[2,2,128,128]{3,2,1,0:T(8,128)S(1)}, f32[2,2,128,128]{3,2,1,0:T(8,128)S(1)}, u32[]{:S(2)}, u32[]{:S(2)}) collective-permute-start(f32[2,2,128,128]{3,2,1,0:T(8,128)S(1)} %dynamic-slice_bitcast_fusion.3), channel_id=1, source_target_pairs={{0,4},{1,5},{2,6},{3,7},{4,0},{5,1},{6,2},{7,3},{8,12},{9,13},{10,... | collective-permute-start | bytes 786440 | tf_op jit(solution)/shard_map/ppermute | solution.py:155
  147.8 7.6 %collective-permute-start.14 = (f32[2,128,128]{2,1,0:T(8,128)S(1)}, f32[2,128,128]{2,1,0:T(8,128)S(1)}, u32[]{:S(2)}, u32[]{:S(2)}) collective-permute-start(f32[2,128,128]{2,1,0:T(8,128)S(1)} %dynamic-slice_bitcast_fusion.6), channel_id=1, source_target_pairs={{0,8},{1,9},{2,10},{3,11},{4,12},{5,13},{6,14},{7,15},{8,0},{9,1},... | collective-permute-start | bytes 393224 | tf_op jit(solution)/shard_map/ppermute | solution.py:155

commit v2 on v1

--- a/solution.py
+++ b/solution.py
@@ -15,6 +15,7 @@
 WIDE = GROUPED * SIDE
 TILES = SIDE // GROUPED
 VMEM_LIMIT = 40 * 1024 * 1024
+FULL_VMEM = 60 * 1024 * 1024
 f32, bf16 = jnp.float32, jnp.bfloat16
 
 
@@ -141,82 +142,176 @@
     )(rows, train, first, extra)
 
 
+def plan_kernel(
+    me_ref, pairs, query, rows, hots, first, keep, send, masks, ranks, own, first_sem, keep_sem, send_sem
+):
+    me = me_ref[0]
+    devices, total = masks.shape[0], pairs.shape[0]
+    local_blocks = query.shape[3] // COLS
+    level = local_blocks.bit_length() - 1
+
+    @pl.loop(0, devices, unroll=8)
+    def _(d):
+        masks[d] = 0
+
+    @pl.loop(0, total, unroll=8)
+    def _(p):
+        block = pairs[p, 1]
+        d = lax.shift_right_logical(block, level)
+        masks[d] = masks[d] | lax.shift_left(1, block & (local_blocks - 1))
+
+    count = jnp.int32(0)
+    mask = masks[me]
+    for k in range(local_blocks):
+        bit = lax.shift_right_logical(mask, k) & 1
+
+        @pl.when(bit == 1)
+        def _():
+            own[jnp.minimum(count, EXTRA)] = k
+
+        count = count + bit
+    is_hot = count > 1
+
+    def cut(k, source, target, sem):
+        start = pl.multiple_of(own[k] * COLS, COLS)
+        return pltpu.make_async_copy(source.at[..., pl.ds(start, COLS)], target, sem)
+
+    core = me & 1
+    first_copy = cut(0, query, first, first_sem)
+    first_copy.start()
+
+    def extra_copies(k):
+        return (
+            cut(k + 1, query.at[:, core], keep.at[k], keep_sem.at[k]),
+            cut(k + 1, query.at[:, 1 - core], send.at[k], send_sem.at[k]),
+        )
+
+    @pl.when(is_hot)
+    def _():
+        for k in range(EXTRA):
+            for copy in extra_copies(k):
+                copy.start()
+
+    def rank_step(d, rank):
+        mask = masks[d]
+        hot = (mask & (mask - 1)) != 0
+
+        ranks[d] = rank
+
+        @pl.when(hot)
+        def _():
+            hots[jnp.minimum(rank, hots.shape[0] - 1)] = d
+
+        return rank + jnp.where(hot, 1, 0)
+
+    lax.fori_loop(0, devices, rank_step, jnp.int32(0), unroll=4)
+
+    @pl.loop(0, total, unroll=4)
+    def _(p):
+        block = pairs[p, 1]
+        d = lax.shift_right_logical(block, level)
+        before = masks[d] & (lax.shift_left(1, block & (local_blocks - 1)) - 1)
+        order = before & 1
+        for k in range(1, local_blocks):
+            order = order + (lax.shift_right_logical(before, k) & 1)
+        rows[0, p] = pairs[p, 0]
+        rows[1, p] = jnp.where(order == 0, d, devices + EXTRA * ranks[d] + order - 1)
+
+    first_copy.wait()
+
+    @pl.when(is_hot)
+    def _():
+        for k in range(EXTRA):
+            for copy in extra_copies(k):
+                copy.wait()
+
+
+def plan(me, pairs, query, devices, share, hot_total):
+    smem, hbm = pl.BlockSpec(memory_space=pltpu.SMEM), pl.BlockSpec(memory_space=pl.ANY)
+    vmem = pl.BlockSpec(memory_space=pltpu.VMEM)
+    half = devices // 2
+    extra = jax.ShapeDtypeStruct((EXTRA, half, share, COLS), bf16)
+    return pl.pallas_call(
+        plan_kernel,
+        out_shape=(
+            jax.ShapeDtypeStruct((2, pairs.shape[0]), jnp.int32),
+            jax.ShapeDtypeStruct((hot_total,), jnp.int32),
+            jax.ShapeDtypeStruct((half, 2, share, COLS), bf16),
+            extra,
+            extra,
+        ),
+        in_specs=[smem, smem, hbm],
+        out_specs=(smem, smem, vmem, vmem, vmem),
+        scratch_shapes=[
+            pltpu.SMEM((devices,), jnp.int32),
+            pltpu.SMEM((devices,), jnp.int32),
+            pltpu.SMEM((NAMED_MOST,), jnp.int32),
+            pltpu.SemaphoreType.DMA,
+            pltpu.SemaphoreType.DMA((EXTRA,)),
+            pltpu.SemaphoreType.DMA((EXTRA,)),
+        ],
+        compiler_params=pltpu.CompilerParams(vmem_limit_bytes=FULL_VMEM),
+        name="plan",
+    )(me.reshape(1), pairs, query.reshape(half, 2, share, -1))
+
+
 def body(devices, train_features, query_gradients, block_pairs, basis_out, basis_in, eigen_out, eigen_in, damping):
     bits = devices.bit_length() - 1
-    me = lax.axis_index("dp")
+    me = lax.axis_index("dp").astype(jnp.int32)
     mine = [(me >> b) & 1 for b in range(bits)]
-    features, local_columns = query_gradients.shape
-    local_blocks = local_columns // COLS
     per_device = block_pairs.shape[0]
-    share = features // devices
+    share = query_gradients.shape[0] // devices
     hot_total = devices // 8
 
     def across(x, b):
         return lax.ppermute(x, "dp", [(d, d ^ (1 << b)) for d in range(devices)])
+
+    def to_all(x):
+        return lax.all_to_all(x, "dp", split_axis=0, concat_axis=0, tiled=True)
 
     pairs = block_pairs
     for b in range(bits):
         other = across(pairs, b)
         pairs = jnp.where(mine[b] == 0, jnp.concatenate([pairs, other]), jnp.concatenate([other, pairs]))
 
-    inverse = 1.0 / (eigen_out[None, :, None] * eigen_in.reshape(TILES, GROUPED).T[:, None, :] + damping[0])
-    conditioned = precondition(train_features, basis_in, basis_out, inverse.reshape(WIDE, TILES), devices)
-    train_share = lax.all_to_all(conditioned, "dp", split_axis=0, concat_axis=0, tiled=True)
-
-    blocks = jnp.arange(devices * local_blocks, dtype=jnp.int32)
-    named = jnp.any(pairs[:, 1:2] == blocks[None, :], axis=0).reshape(devices, local_blocks)
-    ahead = jnp.arange(local_blocks)[:, None] < jnp.arange(local_blocks)[None, :]
-    order = jnp.sum(jnp.where(named[:, :, None] & ahead[None], 1, 0), axis=1)
-    hot = jnp.sum(named.astype(jnp.int32), axis=1) > 1
-    earlier = jnp.arange(devices)[:, None] < jnp.arange(devices)[None, :]
-    hot_order = jnp.sum(jnp.where(hot[:, None] & earlier, 1, 0), axis=0)
-    slot = jnp.where(
-        order == 0, jnp.arange(devices)[:, None], devices + EXTRA * hot_order[:, None] + order - 1
-    ).reshape(-1)
-    pair_slot = jnp.sum(jnp.where(pairs[:, 1:2] == blocks[None, :], slot[None, :], 0), axis=1)
-    rows = jnp.stack([pairs[:, 0], pair_slot, jnp.broadcast_to(mine[0], pair_slot.shape)]).astype(jnp.int32)
-
-    own_named = lax.dynamic_index_in_dim(named, me, 0, False)
-    own_order = lax.dynamic_index_in_dim(order, me, 0, False)
-    local_ids = jnp.arange(local_blocks, dtype=jnp.int32)
-
-    def named_block(k):
-        which = jnp.sum(jnp.where(own_named & (own_order == k), local_ids, 0))
-        return lax.dynamic_slice_in_dim(query_gradients, which * COLS, COLS, 1)
-
-    own = jnp.stack([named_block(k) for k in range(1, NAMED_MOST)])
-    own = own.reshape((EXTRA,) + (2,) * bits + (share, COLS))
-
+    rows, hots, first, keep, send = plan(me, pairs, query_gradients, devices, share, hot_total)
+    first_share = to_all(first.reshape(devices, share, COLS))
     def halves(x, b, left):
-        axis = 1 + [k for k in sorted(left, reverse=True)].index(b)
+        axis = 1 + sorted(left, reverse=True).index(b)
+        left.remove(b)
         keep = lax.dynamic_index_in_dim(x, mine[b], axis, False)
         return keep, lax.dynamic_index_in_dim(x, 1 - mine[b], axis, False)
 
-    keep, send = halves(own, 0, list(range(bits)))
+    def arrived(hot, b, keep, other):
+        return jnp.where(((me ^ hot) >> b) & 1 == 1, other, keep)
+
+    inverse = 1.0 / (eigen_out[None, :, None] * eigen_in.reshape(TILES, GROUPED).T[:, None, :] + damping[0])
     other = across(send, 0)
+    keep, other = (x.reshape((EXTRA,) + (2,) * (bits - 1) + (share, COLS)) for x in (keep, other))
     chains = []
     for rank in range(hot_total):
-        is_rank = hot & (hot_order == rank)
-        from_me = is_rank[me]
-        from_other = is_rank[me ^ 1]
-        x = jnp.where(from_me, keep, jnp.where(from_other, other, jnp.zeros_like(other)))
         rest = list(range(1, bits))
         turn = rank % 2
-        chains.append([x, rest[turn : turn + 1] + rest[:turn] + rest[turn + 1 :], rest])
-
-    first_share = lax.all_to_all(
-        named_block(0).reshape(devices, share, COLS), "dp", split_axis=0, concat_axis=0, tiled=True
-    )
-
-    for _ in range(1, bits):
-        for chain in chains:
-            x, todo, left = chain
-            b = todo.pop(0)
-            keep, send = halves(x, b, left)
-            left.remove(b)
-            chain[0] = keep + across(send, b)
+        steps = rest[turn : turn + 1] + rest[:turn] + rest[turn + 1 :]
+        chains.append([arrived(hots[rank], 0, keep, other), steps, rest])
+
+    for k in range(bits - 1):
+        parts = [halves(x, steps[k], left) for x, steps, left in chains]
+        sends = [part[1] for part in parts]
+        if k == 0:
+            *sends, inverse = lax.optimization_barrier((*sends, inverse))
+            conditioned = precondition(train_features, basis_in, basis_out, inverse.reshape(WIDE, TILES), devices)
+            conditioned, first_share = lax.optimization_barrier((conditioned, first_share))
+            train_share = to_all(conditioned)
+        if k == bits - 2:
+            *sends, train_share = lax.optimization_barrier((*sends, train_share))
+        others = [across(send, chain[1][k]) for send, chain in zip(sends, chains)]
+        others = lax.optimization_barrier(others)
+        for rank, chain in enumerate(chains):
+            chain[0] = arrived(hots[rank], chain[1][k], parts[rank][0], others[rank])
     extra_share = jnp.concatenate([chain[0] for chain in chains], axis=0)
 
+    rows = jnp.concatenate([rows, jnp.broadcast_to(mine[0], (1, rows.shape[1]))])
     keep, send = partial_scores(rows, per_device, train_share, first_share, extra_share)
     tiles = keep + across(send, 0)
     tiles = tiles.reshape((2,) * (bits - 1) + (per_device, COLS, COLS))

time: 156 us -> 142 us (0.910)
  waiting for transfers between devices: 89 us -> 82.2 us
  local copies, waits for them, and re-layouts: 11.7 us -> 6.2 us
  Pallas kernels: 7.55 us -> 12 us
  other arithmetic: 11.3 us -> 7.27 us
    ppermute x15, waiting for transfers between devices: 89 us -> 74.2 us  [across(): return lax.ppermute(x, 'dp', [(d, d ^ 1 << b) for d in range(devices)])]
    all_to_all x2, waiting for transfers between devices: 0.01 us -> 8 us  [to_all(): return lax.all_to_all(x, 'dp', split_axis=0, concat_axis=0, tiled=True)]
    dynamic_slice x6 -> x0, local copies, waits for them, and re-layouts: 4.69 us -> none  [the longest x1 3.85 us: named_block(): return lax.dynamic_slice_in_dim(query_gradients, which * COLS, COLS, 1)]
    pallas_call x0 -> x1, Pallas kernels: none -> 4.42 us  [plan(): pl.pallas_call(plan_kernel, out_shape=(jax.ShapeDtypeStruct((2, pairs.sha...]
    ppermute x15, starting transfers between devices: 21.4 us -> 18.3 us  [across(): return lax.ppermute(x, 'dp', [(d, d ^ 1 << b) for d in range(devices)])]
    add x7 -> x0, other arithmetic: 2.82 us -> none  [the longest x6 2.81 us: body(): chain[0] = keep + across(send, b)]
    reduce_sum x6 -> x0, other arithmetic: 1.89 us -> none  [the longest x2 1.41 us: named_block(): which = jnp.sum(jnp.where(own_named & (own_order == k), local_ids, 0))]
    all_to_all x2, starting transfers between devices: 11.5 us -> 13.2 us  [to_all(): return lax.all_to_all(x, 'dp', split_axis=0, concat_axis=0, tiled=True)]
  transfers between devices with their start and end apart: 17 -> 17, of which waited for: 12 -> 15; matrix products, arithmetic and copies ran while one was open for 7% -> 5% of each run, Pallas kernels for 4% -> 4%
where the time goes in v2:
time: 142 us; the launch traced here: 141 us
  waiting for transfers between devices  82.2 us (58%)
  starting transfers between devices  31.5 us (22%)
  Pallas kernels  12 us (8%)
  other arithmetic  7.27 us (5%)
  local copies, waits for them, and re-layouts  6.2 us (4%)
  between operations  2.22 us (2%)
    ppermute x15, waiting for transfers between devices, across(): return lax.ppermute(x, 'dp', [(d, d ^ 1 << b) for d in range(devices)])  74.2 us
    ppermute x15, starting transfers between devices, across(): return lax.ppermute(x, 'dp', [(d, d ^ 1 << b) for d in range(devices)])  18.3 us
    all_to_all x2, starting transfers between devices, to_all(): return lax.all_to_all(x, 'dp', split_axis=0, concat_axis=0, tiled=True)  13.2 us
    all_to_all x2, waiting for transfers between devices, to_all(): return lax.all_to_all(x, 'dp', split_axis=0, concat_axis=0, tiled=True)  8 us
    pallas_call x1, Pallas kernels, precondition(): pl.pallas_call(precondition_kernel, out_shape=jax.ShapeDtypeStruct((chunk...  5.63 us
    select_n x6, other arithmetic, arrived(): return jnp.where((me ^ hot) >> b & 1 == 1, other, keep)  5.33 us
    pallas_call x1, Pallas kernels, plan(): pl.pallas_call(plan_kernel, out_shape=(jax.ShapeDtypeStruct((2, pairs.sha...  4.42 us
    unnamed x27, local copies, waits for them, and re-layouts  3.32 us
  transfers between devices with their start and end apart: 17, of which 15 were waited for; matrix products, arithmetic and copies ran while one was open for 5% of the time, Pallas kernels for 4%

profile of v2, /device:TPU:0, one launch (start us, length us, event | category | flops | bytes accessed | tf_op | source)
XLA Modules:
  0.0 141.3 jit_solution(8410051755625060376)
XLA Ops:
  0.0 0.8 copy.21
  0.8 0.5 collective-permute-start
  1.2 0.8 collective-permute-done
  2.1 2.8 %collective-permute-start.1 = (s32[4,2]{0,1:T(2,128)S(1)}, s32[4,2]{0,1:T(2,128)S(1)}, u32[]{:S(2)}, u32[]{:S(2)}) collective-permute-start(s32[4,2]{0,1:T(2,128)S(1)} %add_select_fusion), channel_id=1, source_target_pairs={{0,2},{1,3},{2,0},{3,1},{4,6},{5,7},{6,4},{7,5},{8,10},{9,11},{10,... | collective-permute-start | bytes 104 | tf_op jit(solution)/shard_map/ppermute | solution.py:267
  5.0 1.5 %collective-permute-done.1 = s32[4,2]{0,1:T(2,128)S(1)} collective-permute-done((s32[4,2]{0,1:T(2,128)S(1)}, s32[4,2]{0,1:T(2,128)S(1)}, u32[]{:S(2)}, u32[]{:S(2)}) %collective-permute-start.1) | collective-permute-done | bytes 64 | tf_op jit(solution)/shard_map/ppermute | solution.py:267
  6.6 2.1 %collective-permute-start.2 = (s32[8,2]{0,1:T(2,128)S(1)}, s32[8,2]{0,1:T(2,128)S(1)}, u32[]{:S(2)}, u32[]{:S(2)}) collective-permute-start(s32[8,2]{0,1:T(2,128)S(1)} %add_select_fusion.1), channel_id=1, source_target_pairs={{0,4},{1,5},{2,6},{3,7},{4,0},{5,1},{6,2},{7,3},{8,12},{9,13},{10,... | collective-permute-start | bytes 200 | tf_op jit(solution)/shard_map/ppermute | solution.py:267
  8.7 1.5 %collective-permute-done.2 = s32[8,2]{0,1:T(2,128)S(1)} collective-permute-done((s32[8,2]{0,1:T(2,128)S(1)}, s32[8,2]{0,1:T(2,128)S(1)}, u32[]{:S(2)}, u32[]{:S(2)}) %collective-permute-start.2) | collective-permute-done | bytes 96 | tf_op jit(solution)/shard_map/ppermute | solution.py:267
  10.3 3.0 %collective-permute-start.3 = (s32[16,2]{0,1:T(2,128)S(1)}, s32[16,2]{0,1:T(2,128)S(1)}, u32[]{:S(2)}, u32[]{:S(2)}) collective-permute-start(s32[16,2]{0,1:T(2,128)S(1)} %add_select_fusion.2), channel_id=1, source_target_pairs={{0,8},{1,9},{2,10},{3,11},{4,12},{5,13},{6,14},{7,15},{8,0},{9,1},... | collective-permute-start | bytes 392 | tf_op jit(solution)/shard_map/ppermute | solution.py:267
  13.3 1.5 %collective-permute-done.3 = s32[16,2]{0,1:T(2,128)S(1)} collective-permute-done((s32[16,2]{0,1:T(2,128)S(1)}, s32[16,2]{0,1:T(2,128)S(1)}, u32[]{:S(2)}, u32[]{:S(2)}) %collective-permute-start.3) | collective-permute-done | bytes 160 | tf_op jit(solution)/shard_map/ppermute | solution.py:267
  14.9 0.1 copy.23
  15.1 0.6 broadcast_select_fusion.2.pairs
  15.7 4.4 %plan.1 = (s32[2,32]{1,0:T(2,128)}, s32[2]{0:T(128)}, bf16[8,2,256,128]{3,2,1,0:T(8,128)(2,1)}, bf16[3,8,256,128]{3,2,1,0:T(8,128)(2,1)}, bf16[3,8,256,128]{3,2,1,0:T(8,128)(2,1)}) custom-call(s32[1]{0:T(128)} %bitcast.me_ref, s32[32,2]{1,0:T(8,128)} %broadcast_select_fusion.2.pairs, bf16[8,2,256,1024]{3,2,1,0:T(8,128)(2,1)} %bitcast.57), custom_call_target="tpu_custom_call" | custom-call | tf_op jit(solution)/shard_map/plan/pallas_call | solution.py:234
  20.3 6.5 %all-to-all-start = ((bf16[16,256,128]{2,1,0:T(8,128)(2,1)}), bf16[16,256,128]{2,1,0:T(8,128)(2,1)S(1)}, u32[]{:S(2)}, u32[]{:S(2)}) async-start(bf16[16,256,128]{2,1,0:T(8,128)(2,1)} %bitcast.64), calls=%async_computation | async-start | bytes 2097152 | tf_op jit(solution)/shard_map/all_to_all | solution.py:270
  27.7 0.1 add_divide_fusion
  27.8 0.6 fusion.1
  29.6 1.6 %broadcast_select_fusion = (bf16[3,8,256,128]{3,2,1,0:T(8,128)(2,1)S(1)}, bf16[3,8,256,128]{3,2,1,0:T(8,128)(2,1)S(1)}) fusion(bf16[3,8,256,128]{3,2,1,0:T(8,128)(2,1)} %collective-permute-done.4, bf16[3,8,256,128]{3,2,1,0:T(8,128)(2,1)S(1)} %copy-done.8, pred[]{:T(512)S(6)} %eq.43, pred[]{:T(512)S(6)} %eq.42), kind=kLoop, calls=%fused_computation | loop fusion | flops 1572864 | bytes 6291458 | tf_op jit(solution)/shard_map/jit(_where)/select_n | solution.py:286
  31.3 0.9 dynamic-slice_bitcast_fusion.1
  32.3 0.3 copy-done.3
  32.6 0.6 copy-done.5
  33.2 1.9 %collective-permute-start.5 = (bf16[3,2,2,256,128]{4,3,2,1,0:T(8,128)(2,1)}, bf16[3,2,2,256,128]{4,3,2,1,0:T(8,128)(2,1)}, u32[]{:S(2)}, u32[]{:S(2)}) collective-permute-start(bf16[3,2,2,256,128]{4,3,2,1,0:T(8,128)(2,1)} %dynamic-slice_bitcast_fusion.1), channel_id=1, source_target_pairs={{0,2},{1,3},{2,0},{3,1},{4,6},{5,7},{6,4},{7,5},{8,10},{9,11},{10,... | collective-permute-start | bytes 2359304 | tf_op jit(solution)/shard_map/ppermute | solution.py:267
  35.1 1.5 %collective-permute-start.6 = (bf16[3,2,2,256,128]{4,3,2,1,0:T(8,128)(2,1)S(1)}, bf16[3,2,2,256,128]{4,3,2,1,0:T(8,128)(2,1)}, u32[]{:S(2)}, u32[]{:S(2)}) collective-permute-start(bf16[3,2,2,256,128]{4,3,2,1,0:T(8,128)(2,1)S(1)} %dynamic-slice_bitcast_fusion), channel_id=1, source_target_pairs={{0,4},{1,5},{2,6},{3,7},{4,0},{5,1},{6,2},{7,3},{8,12},{9,13},{10,... | collective-permute-start | bytes 2359304 | tf_op jit(solution)/shard_map/ppermute | solution.py:267
  36.6 5.6 %precondition.1 = bf16[16,128,256]{2,1,0:T(8,128)(2,1)} custom-call(bf16[4096,128]{1,0:T(8,128)(2,1)S(1)} %copy-done, f32[64,64]{1,0:T(8,128)S(1)} %copy-done.1, f32[64,64]{1,0:T(8,128)S(1)} %copy-done.2, f32[256,16]{1,0:T(8,128)S(1)} %bitcast.56), custom_call_target="tpu_custom_call" | custom-call | flops 3000000000 | bytes 2097152 | tf_op jit(solution)/shard_map/precondition/pallas_call | solution.py:99
  42.2 8.0 %all-to-all-done.first = bf16[16,256,128]{2,1,0:T(8,128)(2,1)S(1)} async-done(((bf16[16,256,128]{2,1,0:T(8,128)(2,1)}), bf16[16,256,128]{2,1,0:T(8,128)(2,1)S(1)}, u32[]{:S(2)}, u32[]{:S(2)}) %all-to-all-start) | async-done | bytes 1048608 | tf_op jit(solution)/shard_map/all_to_all | solution.py:270
  50.2 6.7 %all-to-all-start.1 = ((bf16[16,128,256]{2,1,0:T(8,128)(2,1)}), bf16[16,128,256]{2,1,0:T(8,128)(2,1)S(1)}, u32[]{:S(2)}, u32[]{:S(2)}) async-start(bf16[16,128,256]{2,1,0:T(8,128)(2,1)} %precondition.1), calls=%async_computation.1 | async-start | bytes 2097152 | tf_op jit(solution)/shard_map/all_to_all | solution.py:270
  56.9 2.1 %collective-permute-done.5 = bf16[3,2,2,256,128]{4,3,2,1,0:T(8,128)(2,1)} collective-permute-done((bf16[3,2,2,256,128]{4,3,2,1,0:T(8,128)(2,1)}, bf16[3,2,2,256,128]{4,3,2,1,0:T(8,128)(2,1)}, u32[]{:S(2)}, u32[]{:S(2)}) %collective-permute-start.5) | collective-permute-done | bytes 786464 | tf_op jit(solution)/shard_map/ppermute | solution.py:267
  59.0 10.8 %collective-permute-done.6 = bf16[3,2,2,256,128]{4,3,2,1,0:T(8,128)(2,1)} collective-permute-done((bf16[3,2,2,256,128]{4,3,2,1,0:T(8,128)(2,1)S(1)}, bf16[3,2,2,256,128]{4,3,2,1,0:T(8,128)(2,1)}, u32[]{:S(2)}, u32[]{:S(2)}) %collective-permute-start.6) | collective-permute-done | bytes 786464 | tf_op jit(solution)/shard_map/ppermute | solution.py:267
  69.8 1.5 %bitcast_select_fusion = bf16[3,2,2,256,128]{4,3,2,1,0:T(8,128)(2,1)S(1)} fusion(bf16[3,2,2,256,128]{4,3,2,1,0:T(8,128)(2,1)} %collective-permute-done.6, bf16[3,2,2,2,256,128]{5,4,3,2,1,0:T(8,128)(2,1)} %bitcast.61, s32[]{:T(128)S(6)} %select_n.152, pred[]{:T(512)S(6)} %eq.44), kind=kLoop, calls=%fused_computation.2 | loop fusion | flops 393216 | bytes 2359301 | tf_op jit(solution)/shard_map/jit(_where)/select_n | solution.py:286
  71.3 0.1 collective-permute-start.8
  71.6 0.9 copy-done.6
  72.5 0.8 dynamic-slice_bitcast_fusion.3
  73.3 12.5 %collective-permute-done.8 = bf16[3,2,256,128]{3,2,1,0:T(8,128)(2,1)} collective-permute-done((bf16[3,2,256,128]{3,2,1,0:T(8,128)(2,1)S(1)}, bf16[3,2,256,128]{3,2,1,0:T(8,128)(2,1)}, u32[]{:S(2)}, u32[]{:S(2)}) %collective-permute-start.8) | collective-permute-done | bytes 393248 | tf_op jit(solution)/shard_map/ppermute | solution.py:267
  85.7 3.3 %collective-permute-done.7 = bf16[3,2,256,128]{3,2,1,0:T(8,128)(2,1)} collective-permute-done((bf16[3,2,256,128]{3,2,1,0:T(8,128)(2,1)}, bf16[3,2,256,128]{3,2,1,0:T(8,128)(2,1)}, u32[]{:S(2)}, u32[]{:S(2)}) %collective-permute-start.7) | collective-permute-done | bytes 393248 | tf_op jit(solution)/shard_map/ppermute | solution.py:267
  89.0 1.2 bitcast_select_fusion.2
  90.3 0.7 copy-done.7
  91.0 2.6 %collective-permute-start.10 = (bf16[3,256,128]{2,1,0:T(8,128)(2,1)S(1)}, bf16[3,256,128]{2,1,0:T(8,128)(2,1)S(1)}, u32[]{:S(2)}, u32[]{:S(2)}) collective-permute-start(bf16[3,256,128]{2,1,0:T(8,128)(2,1)S(1)} %dynamic-slice_bitcast_fusion.5), channel_id=1, source_target_pairs={{0,8},{1,9},{2,10},{3,11},{4,12},{5,13},{6,14},{7,15},{8,0},{9,1},... | collective-permute-start | bytes 589832 | tf_op jit(solution)/shard_map/ppermute | solution.py:267
  93.6 0.4 collective-permute-start.9
  94.0 13.5 %collective-permute-done.10 = bf16[3,256,128]{2,1,0:T(8,128)(2,1)S(1)} collective-permute-done((bf16[3,256,128]{2,1,0:T(8,128)(2,1)S(1)}, bf16[3,256,128]{2,1,0:T(8,128)(2,1)S(1)}, u32[]{:S(2)}, u32[]{:S(2)}) %collective-permute-start.10) | collective-permute-done | bytes 196640 | tf_op jit(solution)/shard_map/ppermute | solution.py:267
  107.5 3.6 %collective-permute-done.9 = bf16[3,256,128]{2,1,0:T(8,128)(2,1)S(1)} collective-permute-done((bf16[3,256,128]{2,1,0:T(8,128)(2,1)S(1)}, bf16[3,256,128]{2,1,0:T(8,128)(2,1)S(1)}, u32[]{:S(2)}, u32[]{:S(2)}) %collective-permute-start.9) | collective-permute-done | bytes 196640 | tf_op jit(solution)/shard_map/ppermute | solution.py:267
  111.1 0.9 bitcast_select_fusion.5
  112.1 1.9 %partial_scores.1 = (f32[16,128,128]{2,1,0:T(8,128)S(1)}, f32[16,128,128]{2,1,0:T(8,128)S(1)}) custom-call(s32[3,32]{1,0:T(4,128)S(1)} %concatenate.38.rows, bf16[16,128,256]{2,1,0:T(8,128)(2,1)S(1)} %all-to-all-done.1.train, bf16[16,256,128]{2,1,0:T(8,128)(2,1)S(1)} %all-to-all-done.first, bf16[6,256,128]{2,1,0:T(8,128)(2,1)S(1)} %pad_maximum_fusion.extra), custom_call_target="tpu_custom_call" | custom-call | tf_op jit(solution)/shard_map/partial_scores/pallas_call | solution.py:135
  114.1 2.6 %collective-permute-done.11 = f32[16,128,128]{2,1,0:T(8,128)S(1)} collective-permute-done((f32[16,128,128]{2,1,0:T(8,128)S(1)}, f32[16,128,128]{2,1,0:T(8,128)S(1)}, u32[]{:S(2)}, u32[]{:S(2)}) %collective-permute-start.11) | collective-permute-done | bytes 1048608 | tf_op jit(solution)/shard_map/ppermute | solution.py:267
  116.7 0.1 add.68
  116.9 1.7 %collective-permute-start.12 = (bf16[2,2,2,128,128]{4,3,2,1,0:T(8,128)(2,1)S(1)}, bf16[2,2,2,128,128]{4,3,2,1,0:T(8,128)(2,1)S(1)}, u32[]{:S(2)}, u32[]{:S(2)}) collective-permute-start(bf16[2,2,2,128,128]{4,3,2,1,0:T(8,128)(2,1)S(1)} %fusion), channel_id=1, source_target_pairs={{0,2},{1,3},{2,0},{3,1},{4,6},{5,7},{6,4},{7,5},{8,10},{9,11},{10,... | collective-permute-start | bytes 786440 | tf_op jit(solution)/shard_map/ppermute | solution.py:267
  118.6 6.7 %collective-permute-done.12 = bf16[2,2,2,128,128]{4,3,2,1,0:T(8,128)(2,1)S(1)} collective-permute-done((bf16[2,2,2,128,128]{4,3,2,1,0:T(8,128)(2,1)S(1)}, bf16[2,2,2,128,128]{4,3,2,1,0:T(8,128)(2,1)S(1)}, u32[]{:S(2)}, u32[]{:S(2)}) %collective-permute-start.12) | collective-permute-done | bytes 262176 | tf_op jit(solution)/shard_map/ppermute | solution.py:267
  125.5 7.5 %collective-permute-done.13 = f32[2,2,128,128]{3,2,1,0:T(8,128)S(1)} collective-permute-done((f32[2,2,128,128]{3,2,1,0:T(8,128)S(1)}, f32[2,2,128,128]{3,2,1,0:T(8,128)S(1)}, u32[]{:S(2)}, u32[]{:S(2)}) %collective-permute-start.13) | collective-permute-done | bytes 262176 | tf_op jit(solution)/shard_map/ppermute | solution.py:267
  133.1 1.5 %collective-permute-start.14 = (f32[2,128,128]{2,1,0:T(8,128)S(1)}, f32[2,128,128]{2,1,0:T(8,128)S(1)}, u32[]{:S(2)}, u32[]{:S(2)}) collective-permute-start(f32[2,128,128]{2,1,0:T(8,128)S(1)} %dynamic-slice_bitcast_fusion.7), channel_id=1, source_target_pairs={{0,8},{1,9},{2,10},{3,11},{4,12},{5,13},{6,14},{7,15},{8,0},{9,1},... | collective-permute-start | bytes 393224 | tf_op jit(solution)/shard_map/ppermute | solution.py:267
  134.6 6.1 %collective-permute-done.14 = f32[2,128,128]{2,1,0:T(8,128)S(1)} collective-permute-done((f32[2,128,128]{2,1,0:T(8,128)S(1)}, f32[2,128,128]{2,1,0:T(8,128)S(1)}, u32[]{:S(2)}, u32[]{:S(2)}) %collective-permute-start.14) | collective-permute-done | bytes 131104 | tf_op jit(solution)/shard_map/ppermute | solution.py:267
  140.7 0.7 bitcast_add_fusion.2
  (48 shorter events, 1.3 us)
Async XLA Ops:
  0.8 1.3 collective-permute-start
  2.1 4.4 %collective-permute-start.1 = (s32[4,2]{0,1:T(2,128)S(1)}, s32[4,2]{0,1:T(2,128)S(1)}, u32[]{:S(2)}, u32[]{:S(2)}) collective-permute-start(s32[4,2]{0,1:T(2,128)S(1)} %add_select_fusion), channel_id=1, source_target_pairs={{0,2},{1,3},{2,0},{3,1},{4,6},{5,7},{6,4},{7,5},{8,10},{9,11},{10,... | collective-permute-start | bytes 104 | tf_op jit(solution)/shard_map/ppermute | solution.py:267
  6.6 3.6 %collective-permute-start.2 = (s32[8,2]{0,1:T(2,128)S(1)}, s32[8,2]{0,1:T(2,128)S(1)}, u32[]{:S(2)}, u32[]{:S(2)}) collective-permute-start(s32[8,2]{0,1:T(2,128)S(1)} %add_select_fusion.1), channel_id=1, source_target_pairs={{0,4},{1,5},{2,6},{3,7},{4,0},{5,1},{6,2},{7,3},{8,12},{9,13},{10,... | collective-permute-start | bytes 200 | tf_op jit(solution)/shard_map/ppermute | solution.py:267
  10.3 4.6 %collective-permute-start.3 = (s32[16,2]{0,1:T(2,128)S(1)}, s32[16,2]{0,1:T(2,128)S(1)}, u32[]{:S(2)}, u32[]{:S(2)}) collective-permute-start(s32[16,2]{0,1:T(2,128)S(1)} %add_select_fusion.2), channel_id=1, source_target_pairs={{0,8},{1,9},{2,10},{3,11},{4,12},{5,13},{6,14},{7,15},{8,0},{9,1},... | collective-permute-start | bytes 392 | tf_op jit(solution)/shard_map/ppermute | solution.py:267
  20.2 6.7 %copy-start.12 = (f32[64]{0:T(128)S(1)}, f32[64]{0:T(128)}, u32[]{:S(2)}) copy-start(f32[64]{0:T(128)} %param.14) | copy-start | bytes 772
  20.2 7.5 %copy-start.11 = (f32[64]{0:T(128)S(1)}, f32[64]{0:T(128)}, u32[]{:S(2)}) copy-start(f32[64]{0:T(128)} %param.13) | copy-start | bytes 772
  20.2 7.6 %copy-start.9 = (s32[2]{0:T(128)S(1)}, s32[2]{0:T(128)}, u32[]{:S(2)}) copy-start(s32[2]{0:T(128)} %get-tuple-element.27) | copy-start | bytes 28
  20.2 9.4 %copy-start.8 = (bf16[3,8,256,128]{3,2,1,0:T(8,128)(2,1)S(1)}, bf16[3,8,256,128]{3,2,1,0:T(8,128)(2,1)}, u32[]{:S(2)}) copy-start(bf16[3,8,256,128]{3,2,1,0:T(8,128)(2,1)} %get-tuple-element.29) | copy-start | bytes 4718596
  20.2 9.4 %collective-permute-start.4 = (bf16[3,8,256,128]{3,2,1,0:T(8,128)(2,1)}, bf16[3,8,256,128]{3,2,1,0:T(8,128)(2,1)}, u32[]{:S(2)}, u32[]{:S(2)}) collective-permute-start(bf16[3,8,256,128]{3,2,1,0:T(8,128)(2,1)} %get-tuple-element.28), channel_id=1, source_target_pairs={{0,1},{1,0},{2,3},{3,2},{4,5},{5,4},{6,7},{7,6},{8,9},{9,8},{10,11... | collective-permute-start | bytes 4718600 | tf_op jit(solution)/shard_map/ppermute | solution.py:267
  20.3 29.9 %all-to-all-start = ((bf16[16,256,128]{2,1,0:T(8,128)(2,1)}), bf16[16,256,128]{2,1,0:T(8,128)(2,1)S(1)}, u32[]{:S(2)}, u32[]{:S(2)}) async-start(bf16[16,256,128]{2,1,0:T(8,128)(2,1)} %bitcast.64), calls=%async_computation | async-start | bytes 2097152 | tf_op jit(solution)/shard_map/all_to_all | solution.py:270
  31.2 1.4 copy-start.3
  31.2 2.0 %copy-start.5 = (bf16[3,8,256,128]{3,2,1,0:T(8,128)(2,1)}, bf16[3,8,256,128]{3,2,1,0:T(8,128)(2,1)S(1)}, u32[]{:S(2)}) copy-start(bf16[3,8,256,128]{3,2,1,0:T(8,128)(2,1)S(1)} %get-tuple-element.47) | copy-start | bytes 4718596
  31.2 5.3 %copy-start = (bf16[4096,128]{1,0:T(8,128)(2,1)S(1)}, bf16[4096,128]{1,0:T(8,128)(2,1)}, u32[]{:S(2)}) copy-start(bf16[4096,128]{1,0:T(8,128)(2,1)} %train.1) | copy-start | bytes 3145732
  31.2 5.3 %copy-start.1 = (f32[64,64]{1,0:T(8,128)S(1)}, f32[64,64]{1,0:T(8,128)}, u32[]{:S(2)}) copy-start(f32[64,64]{1,0:T(8,128)} %basis_in.1) | copy-start | bytes 49156
  31.2 5.3 %copy-start.2 = (f32[64,64]{1,0:T(8,128)S(1)}, f32[64,64]{1,0:T(8,128)}, u32[]{:S(2)}) copy-start(f32[64,64]{1,0:T(8,128)} %basis_out.1) | copy-start | bytes 49156
  33.2 25.8 %collective-permute-start.5 = (bf16[3,2,2,256,128]{4,3,2,1,0:T(8,128)(2,1)}, bf16[3,2,2,256,128]{4,3,2,1,0:T(8,128)(2,1)}, u32[]{:S(2)}, u32[]{:S(2)}) collective-permute-start(bf16[3,2,2,256,128]{4,3,2,1,0:T(8,128)(2,1)} %dynamic-slice_bitcast_fusion.1), channel_id=1, source_target_pairs={{0,2},{1,3},{2,0},{3,1},{4,6},{5,7},{6,4},{7,5},{8,10},{9,11},{10,... | collective-permute-start | bytes 2359304 | tf_op jit(solution)/shard_map/ppermute | solution.py:267
  35.1 34.8 %collective-permute-start.6 = (bf16[3,2,2,256,128]{4,3,2,1,0:T(8,128)(2,1)S(1)}, bf16[3,2,2,256,128]{4,3,2,1,0:T(8,128)(2,1)}, u32[]{:S(2)}, u32[]{:S(2)}) collective-permute-start(bf16[3,2,2,256,128]{4,3,2,1,0:T(8,128)(2,1)S(1)} %dynamic-slice_bitcast_fusion), channel_id=1, source_target_pairs={{0,4},{1,5},{2,6},{3,7},{4,0},{5,1},{6,2},{7,3},{8,12},{9,13},{10,... | collective-permute-start | bytes 2359304 | tf_op jit(solution)/shard_map/ppermute | solution.py:267
  50.2 40.8 %all-to-all-start.1 = ((bf16[16,128,256]{2,1,0:T(8,128)(2,1)}), bf16[16,128,256]{2,1,0:T(8,128)(2,1)S(1)}, u32[]{:S(2)}, u32[]{:S(2)}) async-start(bf16[16,128,256]{2,1,0:T(8,128)(2,1)} %precondition.1), calls=%async_computation.1 | async-start | bytes 2097152 | tf_op jit(solution)/shard_map/all_to_all | solution.py:270
  56.9 14.6 %copy-start.4 = (bf16[3,8,256,128]{3,2,1,0:T(8,128)(2,1)S(1)}, bf16[3,8,256,128]{3,2,1,0:T(8,128)(2,1)}, u32[]{:S(2)}) copy-start(bf16[3,8,256,128]{3,2,1,0:T(8,128)(2,1)} %copy-done.3) | copy-start | bytes 4718596
  71.3 14.4 %collective-permute-start.8 = (bf16[3,2,256,128]{3,2,1,0:T(8,128)(2,1)S(1)}, bf16[3,2,256,128]{3,2,1,0:T(8,128)(2,1)}, u32[]{:S(2)}, u32[]{:S(2)}) collective-permute-start(bf16[3,2,256,128]{3,2,1,0:T(8,128)(2,1)S(1)} %dynamic-slice_bitcast_fusion.2), channel_id=1, source_target_pairs={{0,2},{1,3},{2,0},{3,1},{4,6},{5,7},{6,4},{7,5},{8,10},{9,11},{10,... | collective-permute-start | bytes 1179656 | tf_op jit(solution)/shard_map/ppermute | solution.py:267
  71.6 0.9 copy-start.6
  73.2 15.8 %collective-permute-start.7 = (bf16[3,2,256,128]{3,2,1,0:T(8,128)(2,1)}, bf16[3,2,256,128]{3,2,1,0:T(8,128)(2,1)}, u32[]{:S(2)}, u32[]{:S(2)}) collective-permute-start(bf16[3,2,256,128]{3,2,1,0:T(8,128)(2,1)} %dynamic-slice_bitcast_fusion.3), channel_id=1, source_target_pairs={{0,4},{1,5},{2,6},{3,7},{4,0},{5,1},{6,2},{7,3},{8,12},{9,13},{10,... | collective-permute-start | bytes 1179656 | tf_op jit(solution)/shard_map/ppermute | solution.py:267
  73.3 20.8 %copy-start.10 = (s32[2,32]{1,0:T(2,128)S(1)}, s32[2,32]{1,0:T(2,128)}, u32[]{:S(2)}) copy-start(s32[2,32]{1,0:T(2,128)} %get-tuple-element.26) | copy-start | bytes 772
  90.2 0.8 copy-start.7
  91.0 16.5 %collective-permute-start.10 = (bf16[3,256,128]{2,1,0:T(8,128)(2,1)S(1)}, bf16[3,256,128]{2,1,0:T(8,128)(2,1)S(1)}, u32[]{:S(2)}, u32[]{:S(2)}) collective-permute-start(bf16[3,256,128]{2,1,0:T(8,128)(2,1)S(1)} %dynamic-slice_bitcast_fusion.5), channel_id=1, source_target_pairs={{0,8},{1,9},{2,10},{3,11},{4,12},{5,13},{6,14},{7,15},{8,0},{9,1},... | collective-permute-start | bytes 589832 | tf_op jit(solution)/shard_map/ppermute | solution.py:267
  93.6 17.4 %collective-permute-start.9 = (bf16[3,256,128]{2,1,0:T(8,128)(2,1)S(1)}, bf16[3,256,128]{2,1,0:T(8,128)(2,1)S(1)}, u32[]{:S(2)}, u32[]{:S(2)}) collective-permute-start(bf16[3,256,128]{2,1,0:T(8,128)(2,1)S(1)} %dynamic-slice_bitcast_fusion.6), channel_id=1, source_target_pairs={{0,8},{1,9},{2,10},{3,11},{4,12},{5,13},{6,14},{7,15},{8,0},{9,1},... | collective-permute-start | bytes 589832 | tf_op jit(solution)/shard_map/ppermute | solution.py:267
  114.0 2.7 %collective-permute-start.11 = (f32[16,128,128]{2,1,0:T(8,128)S(1)}, f32[16,128,128]{2,1,0:T(8,128)S(1)}, u32[]{:S(2)}, u32[]{:S(2)}) collective-permute-start(f32[16,128,128]{2,1,0:T(8,128)S(1)} %get-tuple-element.46), channel_id=1, source_target_pairs={{0,1},{1,0},{2,3},{3,2},{4,5},{5,4},{6,7},{7,6},{8,9},{9,8},{10,11... | collective-permute-start | bytes 3145736 | tf_op jit(solution)/shard_map/ppermute | solution.py:267
  116.9 8.4 %collective-permute-start.12 = (bf16[2,2,2,128,128]{4,3,2,1,0:T(8,128)(2,1)S(1)}, bf16[2,2,2,128,128]{4,3,2,1,0:T(8,128)(2,1)S(1)}, u32[]{:S(2)}, u32[]{:S(2)}) collective-permute-start(bf16[2,2,2,128,128]{4,3,2,1,0:T(8,128)(2,1)S(1)} %fusion), channel_id=1, source_target_pairs={{0,2},{1,3},{2,0},{3,1},{4,6},{5,7},{6,4},{7,5},{8,10},{9,11},{10,... | collective-permute-start | bytes 786440 | tf_op jit(solution)/shard_map/ppermute | solution.py:267
  125.4 7.6 %collective-permute-start.13 = (f32[2,2,128,128]{3,2,1,0:T(8,128)S(1)}, f32[2,2,128,128]{3,2,1,0:T(8,128)S(1)}, u32[]{:S(2)}, u32[]{:S(2)}) collective-permute-start(f32[2,2,128,128]{3,2,1,0:T(8,128)S(1)} %dynamic-slice_bitcast_fusion.4), channel_id=1, source_target_pairs={{0,4},{1,5},{2,6},{3,7},{4,0},{5,1},{6,2},{7,3},{8,12},{9,13},{10,... | collective-permute-start | bytes 786440 | tf_op jit(solution)/shard_map/ppermute | solution.py:267
  133.1 7.6 %collective-permute-start.14 = (f32[2,128,128]{2,1,0:T(8,128)S(1)}, f32[2,128,128]{2,1,0:T(8,128)S(1)}, u32[]{:S(2)}, u32[]{:S(2)}) collective-permute-start(f32[2,128,128]{2,1,0:T(8,128)S(1)} %dynamic-slice_bitcast_fusion.7), channel_id=1, source_target_pairs={{0,8},{1,9},{2,10},{3,11},{4,12},{5,13},{6,14},{7,15},{8,0},{9,1},... | collective-permute-start | bytes 393224 | tf_op jit(solution)/shard_map/ppermute | solution.py:267

commit v3 on v2

--- a/solution.py
+++ b/solution.py
@@ -315,14 +315,24 @@
     keep, send = partial_scores(rows, per_device, train_share, first_share, extra_share)
     tiles = keep + across(send, 0)
     tiles = tiles.reshape((2,) * (bits - 1) + (per_device, COLS, COLS))
-    for b in range(1, bits):
-        axis = bits - 1 - b
-        keep = lax.dynamic_index_in_dim(tiles, mine[b], axis, False)
-        send = lax.dynamic_index_in_dim(tiles, 1 - mine[b], axis, False)
-        if b == 1:
-            tiles = keep + across(send.astype(bf16), b).astype(f32)
-        else:
-            tiles = keep + across(send, b)
+    sums, middle = [], list(range(1, bits - 1))
+    for pair in range(per_device):
+        x, left = tiles[..., pair, :, :], list(range(1, bits))
+        turn = pair % 2
+        for k, b in enumerate(middle[turn:] + middle[:turn]):
+            axis = sorted(left, reverse=True).index(b)
+            left.remove(b)
+            keep = lax.dynamic_index_in_dim(x, mine[b], axis, False)
+            send = lax.dynamic_index_in_dim(x, 1 - mine[b], axis, False)
+            if k == 0:
+                x = keep + across(send.astype(bf16), b).astype(f32)
+            else:
+                x = keep + across(send, b)
+        sums.append(x)
+    tiles = jnp.stack(sums, axis=1)
+    keep = lax.dynamic_index_in_dim(tiles, mine[-1], 0, False)
+    send = lax.dynamic_index_in_dim(tiles, 1 - mine[-1], 0, False)
+    tiles = keep + across(send, bits - 1)
     return tiles
 
 

time: 142 us -> 138 us (0.972)
  waiting for transfers between devices: 82.2 us -> 75.4 us
    ppermute x15 -> x17, waiting for transfers between devices: 74.2 us -> 67.4 us  [across(): return lax.ppermute(x, 'dp', [(d, d ^ 1 << b) for d in range(devices)])]
    ppermute x15 -> x17, starting transfers between devices: 18.3 us -> 19.8 us  [across(): return lax.ppermute(x, 'dp', [(d, d ^ 1 << b) for d in range(devices)])]
  transfers between devices with their start and end apart: 17 -> 19, of which waited for: 15 -> 16; matrix products, arithmetic and copies ran while one was open for 5% -> 6% of each run, Pallas kernels for 4% -> 4%
where the time goes in v3:
time: 138 us; the launch traced here: 137 us
  waiting for transfers between devices  75.4 us (55%)
  starting transfers between devices  32.9 us (24%)
  Pallas kernels  12 us (9%)
  other arithmetic  8.42 us (6%)
  local copies, waits for them, and re-layouts  6.24 us (5%)
  between operations  2.32 us (2%)
    ppermute x17, waiting for transfers between devices, across(): return lax.ppermute(x, 'dp', [(d, d ^ 1 << b) for d in range(devices)])  67.4 us
    ppermute x17, starting transfers between devices, across(): return lax.ppermute(x, 'dp', [(d, d ^ 1 << b) for d in range(devices)])  19.8 us
    all_to_all x2, starting transfers between devices, to_all(): return lax.all_to_all(x, 'dp', split_axis=0, concat_axis=0, tiled=True)  13.1 us
    all_to_all x2, waiting for transfers between devices, to_all(): return lax.all_to_all(x, 'dp', split_axis=0, concat_axis=0, tiled=True)  7.94 us
    select_n x6, other arithmetic, arrived(): return jnp.where((me ^ hot) >> b & 1 == 1, other, keep)  6.46 us
    pallas_call x1, Pallas kernels, precondition(): pl.pallas_call(precondition_kernel, out_shape=jax.ShapeDtypeStruct((chunk...  5.62 us
    pallas_call x1, Pallas kernels, plan(): pl.pallas_call(plan_kernel, out_shape=(jax.ShapeDtypeStruct((2, pairs.sha...  4.42 us
    unnamed x27, local copies, waits for them, and re-layouts  3.32 us
  transfers between devices with their start and end apart: 19, of which 16 were waited for; matrix products, arithmetic and copies ran while one was open for 6% of the time, Pallas kernels for 4%

profile of v3, /device:TPU:0, one launch (start us, length us, event | category | flops | bytes accessed | tf_op | source)
XLA Modules:
  0.0 137.1 jit_solution(16257425815035564409)
XLA Ops:
  0.0 0.8 copy.21
  0.8 0.5 collective-permute-start
  1.2 0.8 collective-permute-done
  2.1 2.8 %collective-permute-start.1 = (s32[4,2]{0,1:T(2,128)S(1)}, s32[4,2]{0,1:T(2,128)S(1)}, u32[]{:S(2)}, u32[]{:S(2)}) collective-permute-start(s32[4,2]{0,1:T(2,128)S(1)} %add_select_fusion), channel_id=1, source_target_pairs={{0,2},{1,3},{2,0},{3,1},{4,6},{5,7},{6,4},{7,5},{8,10},{9,11},{10,... | collective-permute-start | bytes 104 | tf_op jit(solution)/shard_map/ppermute | solution.py:267
  5.0 1.5 %collective-permute-done.1 = s32[4,2]{0,1:T(2,128)S(1)} collective-permute-done((s32[4,2]{0,1:T(2,128)S(1)}, s32[4,2]{0,1:T(2,128)S(1)}, u32[]{:S(2)}, u32[]{:S(2)}) %collective-permute-start.1) | collective-permute-done | bytes 64 | tf_op jit(solution)/shard_map/ppermute | solution.py:267
  6.6 2.1 %collective-permute-start.2 = (s32[8,2]{0,1:T(2,128)S(1)}, s32[8,2]{0,1:T(2,128)S(1)}, u32[]{:S(2)}, u32[]{:S(2)}) collective-permute-start(s32[8,2]{0,1:T(2,128)S(1)} %add_select_fusion.1), channel_id=1, source_target_pairs={{0,4},{1,5},{2,6},{3,7},{4,0},{5,1},{6,2},{7,3},{8,12},{9,13},{10,... | collective-permute-start | bytes 200 | tf_op jit(solution)/shard_map/ppermute | solution.py:267
  8.7 1.5 %collective-permute-done.2 = s32[8,2]{0,1:T(2,128)S(1)} collective-permute-done((s32[8,2]{0,1:T(2,128)S(1)}, s32[8,2]{0,1:T(2,128)S(1)}, u32[]{:S(2)}, u32[]{:S(2)}) %collective-permute-start.2) | collective-permute-done | bytes 96 | tf_op jit(solution)/shard_map/ppermute | solution.py:267
  10.3 3.0 %collective-permute-start.3 = (s32[16,2]{0,1:T(2,128)S(1)}, s32[16,2]{0,1:T(2,128)S(1)}, u32[]{:S(2)}, u32[]{:S(2)}) collective-permute-start(s32[16,2]{0,1:T(2,128)S(1)} %add_select_fusion.2), channel_id=1, source_target_pairs={{0,8},{1,9},{2,10},{3,11},{4,12},{5,13},{6,14},{7,15},{8,0},{9,1},... | collective-permute-start | bytes 392 | tf_op jit(solution)/shard_map/ppermute | solution.py:267
  13.3 1.5 %collective-permute-done.3 = s32[16,2]{0,1:T(2,128)S(1)} collective-permute-done((s32[16,2]{0,1:T(2,128)S(1)}, s32[16,2]{0,1:T(2,128)S(1)}, u32[]{:S(2)}, u32[]{:S(2)}) %collective-permute-start.3) | collective-permute-done | bytes 160 | tf_op jit(solution)/shard_map/ppermute | solution.py:267
  15.1 0.6 broadcast_select_fusion.2.pairs
  15.7 4.4 %plan.1 = (s32[2,32]{1,0:T(2,128)}, s32[2]{0:T(128)}, bf16[8,2,256,128]{3,2,1,0:T(8,128)(2,1)}, bf16[3,8,256,128]{3,2,1,0:T(8,128)(2,1)}, bf16[3,8,256,128]{3,2,1,0:T(8,128)(2,1)}) custom-call(s32[1]{0:T(128)} %bitcast.me_ref, s32[32,2]{1,0:T(8,128)} %broadcast_select_fusion.2.pairs, bf16[8,2,256,1024]{3,2,1,0:T(8,128)(2,1)} %bitcast.75), custom_call_target="tpu_custom_call" | custom-call | tf_op jit(solution)/shard_map/plan/pallas_call | solution.py:234
  20.3 6.4 %all-to-all-start = ((bf16[16,256,128]{2,1,0:T(8,128)(2,1)}), bf16[16,256,128]{2,1,0:T(8,128)(2,1)S(1)}, u32[]{:S(2)}, u32[]{:S(2)}) async-start(bf16[16,256,128]{2,1,0:T(8,128)(2,1)} %bitcast.81), calls=%async_computation | async-start | bytes 2097152 | tf_op jit(solution)/shard_map/all_to_all | solution.py:270
  27.7 0.6 fusion.10
  29.5 1.6 %broadcast_select_fusion = (bf16[3,8,256,128]{3,2,1,0:T(8,128)(2,1)S(1)}, bf16[3,8,256,128]{3,2,1,0:T(8,128)(2,1)S(1)}) fusion(bf16[3,8,256,128]{3,2,1,0:T(8,128)(2,1)} %collective-permute-done.4, bf16[3,8,256,128]{3,2,1,0:T(8,128)(2,1)S(1)} %copy-done.8, pred[]{:T(512)S(6)} %eq.43, pred[]{:T(512)S(6)} %eq.42), kind=kLoop, calls=%fused_computation | loop fusion | flops 1572864 | bytes 6291458 | tf_op jit(solution)/shard_map/jit(_where)/select_n | solution.py:286
  31.3 0.9 dynamic-slice_bitcast_fusion.1
  32.2 0.3 copy-done.3
  32.6 0.6 copy-done.5
  33.1 1.9 %collective-permute-start.5 = (bf16[3,2,2,256,128]{4,3,2,1,0:T(8,128)(2,1)}, bf16[3,2,2,256,128]{4,3,2,1,0:T(8,128)(2,1)}, u32[]{:S(2)}, u32[]{:S(2)}) collective-permute-start(bf16[3,2,2,256,128]{4,3,2,1,0:T(8,128)(2,1)} %dynamic-slice_bitcast_fusion.1), channel_id=1, source_target_pairs={{0,2},{1,3},{2,0},{3,1},{4,6},{5,7},{6,4},{7,5},{8,10},{9,11},{10,... | collective-permute-start | bytes 2359304 | tf_op jit(solution)/shard_map/ppermute | solution.py:267
  35.0 1.5 %collective-permute-start.6 = (bf16[3,2,2,256,128]{4,3,2,1,0:T(8,128)(2,1)S(1)}, bf16[3,2,2,256,128]{4,3,2,1,0:T(8,128)(2,1)}, u32[]{:S(2)}, u32[]{:S(2)}) collective-permute-start(bf16[3,2,2,256,128]{4,3,2,1,0:T(8,128)(2,1)S(1)} %dynamic-slice_bitcast_fusion), channel_id=1, source_target_pairs={{0,4},{1,5},{2,6},{3,7},{4,0},{5,1},{6,2},{7,3},{8,12},{9,13},{10,... | collective-permute-start | bytes 2359304 | tf_op jit(solution)/shard_map/ppermute | solution.py:267
  36.5 5.6 %precondition.1 = bf16[16,128,256]{2,1,0:T(8,128)(2,1)} custom-call(bf16[4096,128]{1,0:T(8,128)(2,1)S(1)} %copy-done, f32[64,64]{1,0:T(8,128)S(1)} %copy-done.1, f32[64,64]{1,0:T(8,128)S(1)} %copy-done.2, f32[256,16]{1,0:T(8,128)S(1)} %bitcast.74), custom_call_target="tpu_custom_call" | custom-call | flops 3000000000 | bytes 2097152 | tf_op jit(solution)/shard_map/precondition/pallas_call | solution.py:99
  42.1 7.9 %all-to-all-done.first = bf16[16,256,128]{2,1,0:T(8,128)(2,1)S(1)} async-done(((bf16[16,256,128]{2,1,0:T(8,128)(2,1)}), bf16[16,256,128]{2,1,0:T(8,128)(2,1)S(1)}, u32[]{:S(2)}, u32[]{:S(2)}) %all-to-all-start) | async-done | bytes 1048608 | tf_op jit(solution)/shard_map/all_to_all | solution.py:270
  50.1 6.7 %all-to-all-start.1 = ((bf16[16,128,256]{2,1,0:T(8,128)(2,1)}), bf16[16,128,256]{2,1,0:T(8,128)(2,1)S(1)}, u32[]{:S(2)}, u32[]{:S(2)}) async-start(bf16[16,128,256]{2,1,0:T(8,128)(2,1)} %precondition.1), calls=%async_computation.1 | async-start | bytes 2097152 | tf_op jit(solution)/shard_map/all_to_all | solution.py:270
  56.8 2.2 %collective-permute-done.5 = bf16[3,2,2,256,128]{4,3,2,1,0:T(8,128)(2,1)} collective-permute-done((bf16[3,2,2,256,128]{4,3,2,1,0:T(8,128)(2,1)}, bf16[3,2,2,256,128]{4,3,2,1,0:T(8,128)(2,1)}, u32[]{:S(2)}, u32[]{:S(2)}) %collective-permute-start.5) | collective-permute-done | bytes 786464 | tf_op jit(solution)/shard_map/ppermute | solution.py:267
  58.9 10.8 %collective-permute-done.6 = bf16[3,2,2,256,128]{4,3,2,1,0:T(8,128)(2,1)} collective-permute-done((bf16[3,2,2,256,128]{4,3,2,1,0:T(8,128)(2,1)S(1)}, bf16[3,2,2,256,128]{4,3,2,1,0:T(8,128)(2,1)}, u32[]{:S(2)}, u32[]{:S(2)}) %collective-permute-start.6) | collective-permute-done | bytes 786464 | tf_op jit(solution)/shard_map/ppermute | solution.py:267
  69.7 1.5 %bitcast_select_fusion = bf16[3,2,2,256,128]{4,3,2,1,0:T(8,128)(2,1)S(1)} fusion(bf16[3,2,2,256,128]{4,3,2,1,0:T(8,128)(2,1)} %collective-permute-done.6, bf16[3,2,2,2,256,128]{5,4,3,2,1,0:T(8,128)(2,1)} %bitcast.79, s32[]{:T(128)S(6)} %select_n.157, pred[]{:T(512)S(6)} %eq.44), kind=kLoop, calls=%fused_computation.2 | loop fusion | flops 393216 | bytes 2359301 | tf_op jit(solution)/shard_map/jit(_where)/select_n | solution.py:286
  71.4 1.2 bitcast_select_fusion.1
  72.6 0.9 copy-done.6
  73.5 0.8 dynamic-slice_bitcast_fusion.3
  74.3 11.4 %collective-permute-done.8 = bf16[3,2,256,128]{3,2,1,0:T(8,128)(2,1)} collective-permute-done((bf16[3,2,256,128]{3,2,1,0:T(8,128)(2,1)S(1)}, bf16[3,2,256,128]{3,2,1,0:T(8,128)(2,1)}, u32[]{:S(2)}, u32[]{:S(2)}) %collective-permute-start.8) | collective-permute-done | bytes 393248 | tf_op jit(solution)/shard_map/ppermute | solution.py:267
  85.6 3.3 %collective-permute-done.7 = bf16[3,2,256,128]{3,2,1,0:T(8,128)(2,1)} collective-permute-done((bf16[3,2,256,128]{3,2,1,0:T(8,128)(2,1)}, bf16[3,2,256,128]{3,2,1,0:T(8,128)(2,1)}, u32[]{:S(2)}, u32[]{:S(2)}) %collective-permute-start.7) | collective-permute-done | bytes 393248 | tf_op jit(solution)/shard_map/ppermute | solution.py:267
  88.9 1.2 bitcast_select_fusion.2
  90.2 0.7 copy-done.7
  90.9 2.6 %collective-permute-start.10 = (bf16[3,256,128]{2,1,0:T(8,128)(2,1)S(1)}, bf16[3,256,128]{2,1,0:T(8,128)(2,1)S(1)}, u32[]{:S(2)}, u32[]{:S(2)}) collective-permute-start(bf16[3,256,128]{2,1,0:T(8,128)(2,1)S(1)} %dynamic-slice_bitcast_fusion.4), channel_id=1, source_target_pairs={{0,8},{1,9},{2,10},{3,11},{4,12},{5,13},{6,14},{7,15},{8,0},{9,1},... | collective-permute-start | bytes 589832 | tf_op jit(solution)/shard_map/ppermute | solution.py:267
  93.5 0.4 collective-permute-start.9
  93.9 13.7 %collective-permute-done.10 = bf16[3,256,128]{2,1,0:T(8,128)(2,1)S(1)} collective-permute-done((bf16[3,256,128]{2,1,0:T(8,128)(2,1)S(1)}, bf16[3,256,128]{2,1,0:T(8,128)(2,1)S(1)}, u32[]{:S(2)}, u32[]{:S(2)}) %collective-permute-start.10) | collective-permute-done | bytes 196640 | tf_op jit(solution)/shard_map/ppermute | solution.py:267
  107.6 3.3 %collective-permute-done.9 = bf16[3,256,128]{2,1,0:T(8,128)(2,1)S(1)} collective-permute-done((bf16[3,256,128]{2,1,0:T(8,128)(2,1)S(1)}, bf16[3,256,128]{2,1,0:T(8,128)(2,1)S(1)}, u32[]{:S(2)}, u32[]{:S(2)}) %collective-permute-start.9) | collective-permute-done | bytes 196640 | tf_op jit(solution)/shard_map/ppermute | solution.py:267
  110.9 0.9 bitcast_select_fusion.5
  112.0 1.9 %partial_scores.1 = (f32[16,128,128]{2,1,0:T(8,128)S(1)}, f32[16,128,128]{2,1,0:T(8,128)S(1)}) custom-call(s32[3,32]{1,0:T(4,128)S(1)} %concatenate.38.rows, bf16[16,128,256]{2,1,0:T(8,128)(2,1)S(1)} %all-to-all-done.1.train, bf16[16,256,128]{2,1,0:T(8,128)(2,1)S(1)} %all-to-all-done.first, bf16[6,256,128]{2,1,0:T(8,128)(2,1)S(1)} %pad_maximum_fusion.extra), custom_call_target="tpu_custom_call" | custom-call | tf_op jit(solution)/shard_map/partial_scores/pallas_call | solution.py:135
  114.0 2.6 %collective-permute-done.11 = f32[16,128,128]{2,1,0:T(8,128)S(1)} collective-permute-done((f32[16,128,128]{2,1,0:T(8,128)S(1)}, f32[16,128,128]{2,1,0:T(8,128)S(1)}, u32[]{:S(2)}, u32[]{:S(2)}) %collective-permute-start.11) | collective-permute-done | bytes 1048608 | tf_op jit(solution)/shard_map/ppermute | solution.py:267
  117.0 1.4 %collective-permute-start.12 = (bf16[2,2,128,128]{3,2,1,0:T(8,128)(2,1)S(1)}, bf16[2,2,128,128]{3,2,1,0:T(8,128)(2,1)S(1)}, u32[]{:S(2)}, u32[]{:S(2)}) collective-permute-start(bf16[2,2,128,128]{3,2,1,0:T(8,128)(2,1)S(1)} %fusion), channel_id=1, source_target_pairs={{0,2},{1,3},{2,0},{3,1},{4,6},{5,7},{6,4},{7,5},{8,10},{9,11},{10,... | collective-permute-start | bytes 393224 | tf_op jit(solution)/shard_map/ppermute | solution.py:267
  118.4 4.1 %collective-permute-done.14 = bf16[2,2,128,128]{3,2,1,0:T(8,128)(2,1)S(1)} collective-permute-done((bf16[2,2,128,128]{3,2,1,0:T(8,128)(2,1)S(1)}, bf16[2,2,128,128]{3,2,1,0:T(8,128)(2,1)S(1)}, u32[]{:S(2)}, u32[]{:S(2)}) %collective-permute-start.14) | collective-permute-done | bytes 131104 | tf_op jit(solution)/shard_map/ppermute | solution.py:267
  122.5 1.4 %collective-permute-start.15 = (f32[2,128,128]{2,1,0:T(8,128)S(1)}, f32[2,128,128]{2,1,0:T(8,128)S(1)}, u32[]{:S(2)}, u32[]{:S(2)}) collective-permute-start(f32[2,128,128]{2,1,0:T(8,128)S(1)} %dynamic-slice_bitcast_fusion.6), channel_id=1, source_target_pairs={{0,2},{1,3},{2,0},{3,1},{4,6},{5,7},{6,4},{7,5},{8,10},{9,11},{10,... | collective-permute-start | bytes 393224 | tf_op jit(solution)/shard_map/ppermute | solution.py:267
  124.0 0.4 collective-permute-start.13
  124.4 3.1 %collective-permute-done.15 = f32[2,128,128]{2,1,0:T(8,128)S(1)} collective-permute-done((f32[2,128,128]{2,1,0:T(8,128)S(1)}, f32[2,128,128]{2,1,0:T(8,128)S(1)}, u32[]{:S(2)}, u32[]{:S(2)}) %collective-permute-start.15) | collective-permute-done | bytes 131104 | tf_op jit(solution)/shard_map/ppermute | solution.py:267
  127.6 1.5 %collective-permute-done.13 = f32[2,128,128]{2,1,0:T(8,128)S(1)} collective-permute-done((f32[2,128,128]{2,1,0:T(8,128)S(1)}, f32[2,128,128]{2,1,0:T(8,128)S(1)}, u32[]{:S(2)}, u32[]{:S(2)}) %collective-permute-start.13) | collective-permute-done | bytes 131104 | tf_op jit(solution)/shard_map/ppermute | solution.py:267
  129.1 1.4 collective-permute-start.16
  130.5 6.0 %collective-permute-done.16 = f32[2,128,128]{2,1,0:T(8,128)S(1)} collective-permute-done((f32[2,128,128]{2,1,0:T(8,128)S(1)}, f32[2,128,128]{2,1,0:T(8,128)S(1)}, u32[]{:S(2)}, u32[]{:S(2)}) %collective-permute-start.16) | collective-permute-done | bytes 131104 | tf_op jit(solution)/shard_map/ppermute | solution.py:267
  136.5 0.7 fusion.6
  (57 shorter events, 1.8 us)
Async XLA Ops:
  0.8 1.3 collective-permute-start
  2.1 4.4 %collective-permute-start.1 = (s32[4,2]{0,1:T(2,128)S(1)}, s32[4,2]{0,1:T(2,128)S(1)}, u32[]{:S(2)}, u32[]{:S(2)}) collective-permute-start(s32[4,2]{0,1:T(2,128)S(1)} %add_select_fusion), channel_id=1, source_target_pairs={{0,2},{1,3},{2,0},{3,1},{4,6},{5,7},{6,4},{7,5},{8,10},{9,11},{10,... | collective-permute-start | bytes 104 | tf_op jit(solution)/shard_map/ppermute | solution.py:267
  6.6 3.6 %collective-permute-start.2 = (s32[8,2]{0,1:T(2,128)S(1)}, s32[8,2]{0,1:T(2,128)S(1)}, u32[]{:S(2)}, u32[]{:S(2)}) collective-permute-start(s32[8,2]{0,1:T(2,128)S(1)} %add_select_fusion.1), channel_id=1, source_target_pairs={{0,4},{1,5},{2,6},{3,7},{4,0},{5,1},{6,2},{7,3},{8,12},{9,13},{10,... | collective-permute-start | bytes 200 | tf_op jit(solution)/shard_map/ppermute | solution.py:267
  10.3 4.6 %collective-permute-start.3 = (s32[16,2]{0,1:T(2,128)S(1)}, s32[16,2]{0,1:T(2,128)S(1)}, u32[]{:S(2)}, u32[]{:S(2)}) collective-permute-start(s32[16,2]{0,1:T(2,128)S(1)} %add_select_fusion.2), channel_id=1, source_target_pairs={{0,8},{1,9},{2,10},{3,11},{4,12},{5,13},{6,14},{7,15},{8,0},{9,1},... | collective-permute-start | bytes 392 | tf_op jit(solution)/shard_map/ppermute | solution.py:267
  20.2 6.6 %copy-start.12 = (f32[64]{0:T(128)S(1)}, f32[64]{0:T(128)}, u32[]{:S(2)}) copy-start(f32[64]{0:T(128)} %param.14) | copy-start | bytes 772
  20.2 7.4 %copy-start.11 = (f32[64]{0:T(128)S(1)}, f32[64]{0:T(128)}, u32[]{:S(2)}) copy-start(f32[64]{0:T(128)} %param.13) | copy-start | bytes 772
  20.2 7.5 %copy-start.9 = (s32[2]{0:T(128)S(1)}, s32[2]{0:T(128)}, u32[]{:S(2)}) copy-start(s32[2]{0:T(128)} %get-tuple-element.27) | copy-start | bytes 28
  20.2 9.4 %copy-start.8 = (bf16[3,8,256,128]{3,2,1,0:T(8,128)(2,1)S(1)}, bf16[3,8,256,128]{3,2,1,0:T(8,128)(2,1)}, u32[]{:S(2)}) copy-start(bf16[3,8,256,128]{3,2,1,0:T(8,128)(2,1)} %get-tuple-element.29) | copy-start | bytes 4718596
  20.2 9.3 %collective-permute-start.4 = (bf16[3,8,256,128]{3,2,1,0:T(8,128)(2,1)}, bf16[3,8,256,128]{3,2,1,0:T(8,128)(2,1)}, u32[]{:S(2)}, u32[]{:S(2)}) collective-permute-start(bf16[3,8,256,128]{3,2,1,0:T(8,128)(2,1)} %get-tuple-element.28), channel_id=1, source_target_pairs={{0,1},{1,0},{2,3},{3,2},{4,5},{5,4},{6,7},{7,6},{8,9},{9,8},{10,11... | collective-permute-start | bytes 4718600 | tf_op jit(solution)/shard_map/ppermute | solution.py:267
  20.3 29.8 %all-to-all-start = ((bf16[16,256,128]{2,1,0:T(8,128)(2,1)}), bf16[16,256,128]{2,1,0:T(8,128)(2,1)S(1)}, u32[]{:S(2)}, u32[]{:S(2)}) async-start(bf16[16,256,128]{2,1,0:T(8,128)(2,1)} %bitcast.81), calls=%async_computation | async-start | bytes 2097152 | tf_op jit(solution)/shard_map/all_to_all | solution.py:270
  31.2 1.4 %copy-start.3 = (bf16[3,8,256,128]{3,2,1,0:T(8,128)(2,1)}, bf16[3,8,256,128]{3,2,1,0:T(8,128)(2,1)S(1)}, u32[]{:S(2)}) copy-start(bf16[3,8,256,128]{3,2,1,0:T(8,128)(2,1)S(1)} %get-tuple-element.48) | copy-start | bytes 4718596
  31.2 2.0 %copy-start.5 = (bf16[3,8,256,128]{3,2,1,0:T(8,128)(2,1)}, bf16[3,8,256,128]{3,2,1,0:T(8,128)(2,1)S(1)}, u32[]{:S(2)}) copy-start(bf16[3,8,256,128]{3,2,1,0:T(8,128)(2,1)S(1)} %get-tuple-element.47) | copy-start | bytes 4718596
  31.2 5.3 %copy-start = (bf16[4096,128]{1,0:T(8,128)(2,1)S(1)}, bf16[4096,128]{1,0:T(8,128)(2,1)}, u32[]{:S(2)}) copy-start(bf16[4096,128]{1,0:T(8,128)(2,1)} %train.1) | copy-start | bytes 3145732
  31.2 5.3 %copy-start.1 = (f32[64,64]{1,0:T(8,128)S(1)}, f32[64,64]{1,0:T(8,128)}, u32[]{:S(2)}) copy-start(f32[64,64]{1,0:T(8,128)} %basis_in.1) | copy-start | bytes 49156
  31.2 5.3 %copy-start.2 = (f32[64,64]{1,0:T(8,128)S(1)}, f32[64,64]{1,0:T(8,128)}, u32[]{:S(2)}) copy-start(f32[64,64]{1,0:T(8,128)} %basis_out.1) | copy-start | bytes 49156
  33.1 25.8 %collective-permute-start.5 = (bf16[3,2,2,256,128]{4,3,2,1,0:T(8,128)(2,1)}, bf16[3,2,2,256,128]{4,3,2,1,0:T(8,128)(2,1)}, u32[]{:S(2)}, u32[]{:S(2)}) collective-permute-start(bf16[3,2,2,256,128]{4,3,2,1,0:T(8,128)(2,1)} %dynamic-slice_bitcast_fusion.1), channel_id=1, source_target_pairs={{0,2},{1,3},{2,0},{3,1},{4,6},{5,7},{6,4},{7,5},{8,10},{9,11},{10,... | collective-permute-start | bytes 2359304 | tf_op jit(solution)/shard_map/ppermute | solution.py:267
  35.0 34.7 %collective-permute-start.6 = (bf16[3,2,2,256,128]{4,3,2,1,0:T(8,128)(2,1)S(1)}, bf16[3,2,2,256,128]{4,3,2,1,0:T(8,128)(2,1)}, u32[]{:S(2)}, u32[]{:S(2)}) collective-permute-start(bf16[3,2,2,256,128]{4,3,2,1,0:T(8,128)(2,1)S(1)} %dynamic-slice_bitcast_fusion), channel_id=1, source_target_pairs={{0,4},{1,5},{2,6},{3,7},{4,0},{5,1},{6,2},{7,3},{8,12},{9,13},{10,... | collective-permute-start | bytes 2359304 | tf_op jit(solution)/shard_map/ppermute | solution.py:267
  50.1 40.8 %all-to-all-start.1 = ((bf16[16,128,256]{2,1,0:T(8,128)(2,1)}), bf16[16,128,256]{2,1,0:T(8,128)(2,1)S(1)}, u32[]{:S(2)}, u32[]{:S(2)}) async-start(bf16[16,128,256]{2,1,0:T(8,128)(2,1)} %precondition.1), calls=%async_computation.1 | async-start | bytes 2097152 | tf_op jit(solution)/shard_map/all_to_all | solution.py:270
  56.8 14.6 %copy-start.4 = (bf16[3,8,256,128]{3,2,1,0:T(8,128)(2,1)S(1)}, bf16[3,8,256,128]{3,2,1,0:T(8,128)(2,1)}, u32[]{:S(2)}) copy-start(bf16[3,8,256,128]{3,2,1,0:T(8,128)(2,1)} %copy-done.3) | copy-start | bytes 4718596
  71.2 14.4 %collective-permute-start.8 = (bf16[3,2,256,128]{3,2,1,0:T(8,128)(2,1)S(1)}, bf16[3,2,256,128]{3,2,1,0:T(8,128)(2,1)}, u32[]{:S(2)}, u32[]{:S(2)}) collective-permute-start(bf16[3,2,256,128]{3,2,1,0:T(8,128)(2,1)S(1)} %dynamic-slice_bitcast_fusion.2), channel_id=1, source_target_pairs={{0,2},{1,3},{2,0},{3,1},{4,6},{5,7},{6,4},{7,5},{8,10},{9,11},{10,... | collective-permute-start | bytes 1179656 | tf_op jit(solution)/shard_map/ppermute | solution.py:267
  72.6 0.9 copy-start.6
  74.3 14.7 %collective-permute-start.7 = (bf16[3,2,256,128]{3,2,1,0:T(8,128)(2,1)}, bf16[3,2,256,128]{3,2,1,0:T(8,128)(2,1)}, u32[]{:S(2)}, u32[]{:S(2)}) collective-permute-start(bf16[3,2,256,128]{3,2,1,0:T(8,128)(2,1)} %dynamic-slice_bitcast_fusion.3), channel_id=1, source_target_pairs={{0,4},{1,5},{2,6},{3,7},{4,0},{5,1},{6,2},{7,3},{8,12},{9,13},{10,... | collective-permute-start | bytes 1179656 | tf_op jit(solution)/shard_map/ppermute | solution.py:267
  74.3 19.6 %copy-start.10 = (s32[2,32]{1,0:T(2,128)S(1)}, s32[2,32]{1,0:T(2,128)}, u32[]{:S(2)}) copy-start(s32[2,32]{1,0:T(2,128)} %get-tuple-element.26) | copy-start | bytes 772
  90.1 0.7 copy-start.7
  90.9 16.7 %collective-permute-start.10 = (bf16[3,256,128]{2,1,0:T(8,128)(2,1)S(1)}, bf16[3,256,128]{2,1,0:T(8,128)(2,1)S(1)}, u32[]{:S(2)}, u32[]{:S(2)}) collective-permute-start(bf16[3,256,128]{2,1,0:T(8,128)(2,1)S(1)} %dynamic-slice_bitcast_fusion.4), channel_id=1, source_target_pairs={{0,8},{1,9},{2,10},{3,11},{4,12},{5,13},{6,14},{7,15},{8,0},{9,1},... | collective-permute-start | bytes 589832 | tf_op jit(solution)/shard_map/ppermute | solution.py:267
  93.5 17.4 %collective-permute-start.9 = (bf16[3,256,128]{2,1,0:T(8,128)(2,1)S(1)}, bf16[3,256,128]{2,1,0:T(8,128)(2,1)S(1)}, u32[]{:S(2)}, u32[]{:S(2)}) collective-permute-start(bf16[3,256,128]{2,1,0:T(8,128)(2,1)S(1)} %dynamic-slice_bitcast_fusion.5), channel_id=1, source_target_pairs={{0,8},{1,9},{2,10},{3,11},{4,12},{5,13},{6,14},{7,15},{8,0},{9,1},... | collective-permute-start | bytes 589832 | tf_op jit(solution)/shard_map/ppermute | solution.py:267
  113.9 2.7 %collective-permute-start.11 = (f32[16,128,128]{2,1,0:T(8,128)S(1)}, f32[16,128,128]{2,1,0:T(8,128)S(1)}, u32[]{:S(2)}, u32[]{:S(2)}) collective-permute-start(f32[16,128,128]{2,1,0:T(8,128)S(1)} %get-tuple-element.46), channel_id=1, source_target_pairs={{0,1},{1,0},{2,3},{3,2},{4,5},{5,4},{6,7},{7,6},{8,9},{9,8},{10,11... | collective-permute-start | bytes 3145736 | tf_op jit(solution)/shard_map/ppermute | solution.py:267
  116.9 5.6 %collective-permute-start.14 = (bf16[2,2,128,128]{3,2,1,0:T(8,128)(2,1)S(1)}, bf16[2,2,128,128]{3,2,1,0:T(8,128)(2,1)S(1)}, u32[]{:S(2)}, u32[]{:S(2)}) collective-permute-start(bf16[2,2,128,128]{3,2,1,0:T(8,128)(2,1)S(1)} %fusion.1), channel_id=1, source_target_pairs={{0,4},{1,5},{2,6},{3,7},{4,0},{5,1},{6,2},{7,3},{8,12},{9,13},{10,... | collective-permute-start | bytes 393224 | tf_op jit(solution)/shard_map/ppermute | solution.py:267
  117.0 7.0 %collective-permute-start.12 = (bf16[2,2,128,128]{3,2,1,0:T(8,128)(2,1)S(1)}, bf16[2,2,128,128]{3,2,1,0:T(8,128)(2,1)S(1)}, u32[]{:S(2)}, u32[]{:S(2)}) collective-permute-start(bf16[2,2,128,128]{3,2,1,0:T(8,128)(2,1)S(1)} %fusion), channel_id=1, source_target_pairs={{0,2},{1,3},{2,0},{3,1},{4,6},{5,7},{6,4},{7,5},{8,10},{9,11},{10,... | collective-permute-start | bytes 393224 | tf_op jit(solution)/shard_map/ppermute | solution.py:267
  122.5 5.0 %collective-permute-start.15 = (f32[2,128,128]{2,1,0:T(8,128)S(1)}, f32[2,128,128]{2,1,0:T(8,128)S(1)}, u32[]{:S(2)}, u32[]{:S(2)}) collective-permute-start(f32[2,128,128]{2,1,0:T(8,128)S(1)} %dynamic-slice_bitcast_fusion.6), channel_id=1, source_target_pairs={{0,2},{1,3},{2,0},{3,1},{4,6},{5,7},{6,4},{7,5},{8,10},{9,11},{10,... | collective-permute-start | bytes 393224 | tf_op jit(solution)/shard_map/ppermute | solution.py:267
  124.0 5.0 %collective-permute-start.13 = (f32[2,128,128]{2,1,0:T(8,128)S(1)}, f32[2,128,128]{2,1,0:T(8,128)S(1)}, u32[]{:S(2)}, u32[]{:S(2)}) collective-permute-start(f32[2,128,128]{2,1,0:T(8,128)S(1)} %dynamic-slice_bitcast_fusion.7), channel_id=1, source_target_pairs={{0,4},{1,5},{2,6},{3,7},{4,0},{5,1},{6,2},{7,3},{8,12},{9,13},{10,... | collective-permute-start | bytes 393224 | tf_op jit(solution)/shard_map/ppermute | solution.py:267
  129.1 7.3 %collective-permute-start.16 = (f32[2,128,128]{2,1,0:T(8,128)S(1)}, f32[2,128,128]{2,1,0:T(8,128)S(1)}, u32[]{:S(2)}, u32[]{:S(2)}) collective-permute-start(f32[2,128,128]{2,1,0:T(8,128)S(1)} %fusion.3), channel_id=1, source_target_pairs={{0,8},{1,9},{2,10},{3,11},{4,12},{5,13},{6,14},{7,15},{8,0},{9,1},... | collective-permute-start | bytes 393224 | tf_op jit(solution)/shard_map/ppermute | solution.py:267

commit v4 on v3

--- a/solution.py
+++ b/solution.py
@@ -108,16 +108,56 @@
     )(train, basis_in, basis_out, inverse)
 
 
-def score_kernel(per_device, rows, train, first, extra, keep, send):
-    core = rows[2, 0]
+def came_across(me, where, hot, bit):
+    return lax.shift_right_logical(me[0] ^ where[hot], bit) & 1
+
+
+def pick_kernel(plan_of, me, where, *refs):
+    count = len(plan_of)
+    sources, outs = refs[: 2 * count], refs[2 * count :]
+    for hot, (bit, next_bit) in enumerate(plan_of):
+        mine = lax.shift_right_logical(me[0], next_bit) & 1
+        across = came_across(me, where, hot, bit)
+        for way in range(2):
+            source = sources[2 * hot + way]
+
+            @pl.when(across == way)
+            def _():
+                for k in range(source.shape[0]):
+                    outs[2 * hot][k] = source[k, mine]
+                    outs[2 * hot + 1][k] = source[k, 1 - mine]
+
+
+def pick(me, where, sources, plan_of):
+    whole = pl.BlockSpec(memory_space=pltpu.VMEM)
+    shapes = [jax.ShapeDtypeStruct(x.shape[:1] + x.shape[2:], x.dtype) for x in sources]
+    return pl.pallas_call(
+        functools.partial(pick_kernel, plan_of),
+        out_shape=shapes,
+        in_specs=[pl.BlockSpec(memory_space=pltpu.SMEM)] * 2 + [whole] * len(sources),
+        out_specs=[whole] * len(shapes),
+        compiler_params=pltpu.CompilerParams(vmem_limit_bytes=VMEM_LIMIT),
+        name="pick",
+    )(me.reshape(1), where, *sources)
+
+
+def score_kernel(per_device, local_blocks, me_ref, pairs, masks, ranks, train, first, extra, keep, send):
+    core = me_ref[0] & 1
+    level = local_blocks.bit_length() - 1
     devices = first.shape[0]
 
     def tile(pair):
-        slot = rows[1, pair]
+        block = pairs[pair, 1]
+        d = lax.shift_right_logical(block, level)
+        before = masks[d] & (lax.shift_left(1, block & (local_blocks - 1)) - 1)
+        order = before & 1
+        for k in range(1, local_blocks):
+            order = order + (lax.shift_right_logical(before, k) & 1)
+        slot = jnp.where(order == 0, d, devices + EXTRA * ranks[d] + order - 1)
         a = first[jnp.minimum(slot, devices - 1)]
         b = extra[jnp.maximum(slot - devices, 0)]
         q = jnp.where(slot < devices, a.astype(f32), b.astype(f32)).astype(bf16)
-        return mm(train[rows[0, pair]], q)
+        return mm(train[pairs[pair, 0]], q)
 
     def step(h, carry):
         base = h // per_device * (2 * per_device) + h % per_device
@@ -128,22 +168,22 @@
     lax.fori_loop(0, keep.shape[0], step, 0, unroll=4)
 
 
-def partial_scores(rows, per_device, train, first, extra):
-    half = rows.shape[1] // 2
+def partial_scores(per_device, local_blocks, me, pairs, masks, ranks, train, first, extra):
+    half = pairs.shape[0] // 2
     tiles = jax.ShapeDtypeStruct((half, COLS, COLS), f32)
     whole = pl.BlockSpec(memory_space=pltpu.VMEM)
     return pl.pallas_call(
-        functools.partial(score_kernel, per_device),
+        functools.partial(score_kernel, per_device, local_blocks),
         out_shape=(tiles, tiles),
-        in_specs=[pl.BlockSpec(memory_space=pltpu.SMEM), whole, whole, whole],
+        in_specs=[pl.BlockSpec(memory_space=pltpu.SMEM)] * 4 + [whole] * 3,
         out_specs=(whole, whole),
         compiler_params=pltpu.CompilerParams(vmem_limit_bytes=VMEM_LIMIT),
         name="partial_scores",
-    )(rows, train, first, extra)
+    )(me.reshape(1), pairs, masks, ranks, train, first, extra)
 
 
 def plan_kernel(
-    me_ref, pairs, query, rows, hots, first, keep, send, masks, ranks, own, first_sem, keep_sem, send_sem
+    me_ref, pairs, query, masks, ranks, hots, first, keep, send, own, first_sem, keep_sem, send_sem
 ):
     me = me_ref[0]
     devices, total = masks.shape[0], pairs.shape[0]
@@ -177,8 +217,15 @@
         return pltpu.make_async_copy(source.at[..., pl.ds(start, COLS)], target, sem)
 
     core = me & 1
-    first_copy = cut(0, query, first, first_sem)
-    first_copy.start()
+    parts = first_sem.shape[0]
+    length = query.shape[0] // parts
+
+    def first_copies(part):
+        at = pl.ds(part * length, length)
+        return cut(0, query.at[at], first.at[at], first_sem.at[part])
+
+    for part in range(parts):
+        first_copies(part).start()
 
     def extra_copies(k):
         return (
@@ -206,18 +253,8 @@
 
     lax.fori_loop(0, devices, rank_step, jnp.int32(0), unroll=4)
 
-    @pl.loop(0, total, unroll=4)
-    def _(p):
-        block = pairs[p, 1]
-        d = lax.shift_right_logical(block, level)
-        before = masks[d] & (lax.shift_left(1, block & (local_blocks - 1)) - 1)
-        order = before & 1
-        for k in range(1, local_blocks):
-            order = order + (lax.shift_right_logical(before, k) & 1)
-        rows[0, p] = pairs[p, 0]
-        rows[1, p] = jnp.where(order == 0, d, devices + EXTRA * ranks[d] + order - 1)
-
-    first_copy.wait()
+    for part in range(parts):
+        first_copies(part).wait()
 
     @pl.when(is_hot)
     def _():
@@ -234,19 +271,18 @@
     return pl.pallas_call(
         plan_kernel,
         out_shape=(
-            jax.ShapeDtypeStruct((2, pairs.shape[0]), jnp.int32),
+            jax.ShapeDtypeStruct((devices,), jnp.int32),
+            jax.ShapeDtypeStruct((devices,), jnp.int32),
             jax.ShapeDtypeStruct((hot_total,), jnp.int32),
             jax.ShapeDtypeStruct((half, 2, share, COLS), bf16),
             extra,
             extra,
         ),
         in_specs=[smem, smem, hbm],
-        out_specs=(smem, smem, vmem, vmem, vmem),
+        out_specs=(smem, smem, smem, vmem, vmem, vmem),
         scratch_shapes=[
-            pltpu.SMEM((devices,), jnp.int32),
-            pltpu.SMEM((devices,), jnp.int32),
             pltpu.SMEM((NAMED_MOST,), jnp.int32),
-            pltpu.SemaphoreType.DMA,
+            pltpu.SemaphoreType.DMA((8,)),
             pltpu.SemaphoreType.DMA((EXTRA,)),
             pltpu.SemaphoreType.DMA((EXTRA,)),
         ],
@@ -274,7 +310,7 @@
         other = across(pairs, b)
         pairs = jnp.where(mine[b] == 0, jnp.concatenate([pairs, other]), jnp.concatenate([other, pairs]))
 
-    rows, hots, first, keep, send = plan(me, pairs, query_gradients, devices, share, hot_total)
+    masks, ranks, hots, first, keep, send = plan(me, pairs, query_gradients, devices, share, hot_total)
     first_share = to_all(first.reshape(devices, share, COLS))
     def halves(x, b, left):
         axis = 1 + sorted(left, reverse=True).index(b)
@@ -293,10 +329,25 @@
         rest = list(range(1, bits))
         turn = rank % 2
         steps = rest[turn : turn + 1] + rest[:turn] + rest[turn + 1 :]
-        chains.append([arrived(hots[rank], 0, keep, other), steps, rest])
+        chains.append([keep, other, 0, steps, rest])
 
     for k in range(bits - 1):
-        parts = [halves(x, steps[k], left) for x, steps, left in chains]
+        if k in (0,):
+            sources, plan_of = [], []
+            for keep, other, bit, steps, left in chains:
+                before = EXTRA * 2 ** sorted(left, reverse=True).index(steps[k])
+                sources += [x.reshape(before, 2, -1, COLS) for x in (keep, other)]
+                plan_of.append((bit, steps[k]))
+                left.remove(steps[k])
+            halved = pick(me, hots, sources, tuple(plan_of))
+            parts = [
+                [x.reshape((EXTRA,) + (2,) * len(chain[4]) + (share, COLS)) for x in halved[2 * r : 2 * r + 2]]
+                for r, chain in enumerate(chains)
+            ]
+        else:
+            parts = []
+            for rank, (keep, other, bit, steps, left) in enumerate(chains):
+                parts.append(halves(arrived(hots[rank], bit, keep, other), steps[k], left))
         sends = [part[1] for part in parts]
         if k == 0:
             *sends, inverse = lax.optimization_barrier((*sends, inverse))
@@ -305,14 +356,16 @@
             train_share = to_all(conditioned)
         if k == bits - 2:
             *sends, train_share = lax.optimization_barrier((*sends, train_share))
-        others = [across(send, chain[1][k]) for send, chain in zip(sends, chains)]
+        others = [across(send, chain[3][k]) for send, chain in zip(sends, chains)]
         others = lax.optimization_barrier(others)
         for rank, chain in enumerate(chains):
-            chain[0] = arrived(hots[rank], chain[1][k], parts[rank][0], others[rank])
-    extra_share = jnp.concatenate([chain[0] for chain in chains], axis=0)
-
-    rows = jnp.concatenate([rows, jnp.broadcast_to(mine[0], (1, rows.shape[1]))])
-    keep, send = partial_scores(rows, per_device, train_share, first_share, extra_share)
+            chain[:3] = parts[rank][0], others[rank], chain[3][k]
+    extra_share = jnp.concatenate([arrived(hots[r], chain[2], chain[0], chain[1]) for r, chain in enumerate(chains)])
+
+    local_blocks = query_gradients.shape[1] // COLS
+    keep, send = partial_scores(
+        per_device, local_blocks, me, pairs, masks, ranks, train_share, first_share, extra_share
+    )
     tiles = keep + across(send, 0)
     tiles = tiles.reshape((2,) * (bits - 1) + (per_device, COLS, COLS))
     sums, middle = [], list(range(1, bits - 1))

time: 138 us -> 136 us (0.986)
  other arithmetic: 8.42 us -> 2.23 us
  Pallas kernels: 12 us -> 14.8 us
  local copies, waits for them, and re-layouts: 6.24 us -> 3.93 us
  waiting for transfers between devices: 75.4 us -> 77.7 us
  starting transfers between devices: 32.9 us -> 34.5 us
    select_n x6 -> x5, other arithmetic: 6.46 us -> 0.3 us  [arrived(): return jnp.where((me ^ hot) >> b & 1 == 1, other, keep)]
    pallas_call x2 -> x3, Pallas kernels: 6.34 us -> 9.14 us  [the longest x1 4.53 us: plan(): pl.pallas_call(plan_kernel, out_shape=(jax.ShapeDtypeStruct((devices,), j...]
    squeeze x6 -> x2, local copies, waits for them, and re-layouts: 1.83 us -> 0.05 us  [halves(): return (keep, lax.dynamic_index_in_dim(x, 1 - mine[b], axis, False))]
    all_to_all x2, waiting for transfers between devices: 7.94 us -> 9.7 us  [to_all(): return lax.all_to_all(x, 'dp', split_axis=0, concat_axis=0, tiled=True)]
    ppermute x17, starting transfers between devices: 19.8 us -> 21.3 us  [across(): return lax.ppermute(x, 'dp', [(d, d ^ 1 << b) for d in range(devices)])]
    unnamed x27 -> x29, local copies, waits for them, and re-layouts: 3.32 us -> 2.63 us
  transfers between devices with their start and end apart: 19 -> 19, of which waited for: 16 -> 15; matrix products, arithmetic and copies ran while one was open for 6% -> 1% of each run, Pallas kernels for 4% -> 6%
where the time goes in v4:
time: 136 us; the launch traced here: 135 us
  waiting for transfers between devices  77.7 us (57%)
  starting transfers between devices  34.5 us (25%)
  Pallas kernels  14.8 us (11%)
  local copies, waits for them, and re-layouts  3.93 us (3%)
  between operations  2.25 us (2%)
  other arithmetic  2.23 us (2%)
    ppermute x17, waiting for transfers between devices, across(): return lax.ppermute(x, 'dp', [(d, d ^ 1 << b) for d in range(devices)])  68 us
    ppermute x17, starting transfers between devices, across(): return lax.ppermute(x, 'dp', [(d, d ^ 1 << b) for d in range(devices)])  21.3 us
    all_to_all x2, starting transfers between devices, to_all(): return lax.all_to_all(x, 'dp', split_axis=0, concat_axis=0, tiled=True)  13.1 us
    all_to_all x2, waiting for transfers between devices, to_all(): return lax.all_to_all(x, 'dp', split_axis=0, concat_axis=0, tiled=True)  9.7 us
    pallas_call x1, Pallas kernels, precondition(): pl.pallas_call(precondition_kernel, out_shape=jax.ShapeDtypeStruct((chunk...  5.62 us
    pallas_call x1, Pallas kernels, plan(): pl.pallas_call(plan_kernel, out_shape=(jax.ShapeDtypeStruct((devices,), j...  4.53 us
  transfers between devices with their start and end apart: 19, of which 15 were waited for; matrix products, arithmetic and copies ran while one was open for 1% of the time, Pallas kernels for 6%

profile of v4, /device:TPU:0, one launch (start us, length us, event | category | flops | bytes accessed | tf_op | source)
XLA Modules:
  0.0 135.3 jit_solution(16125347426829629501)
XLA Ops:
  0.0 0.8 copy.20
  0.8 0.5 collective-permute-start
  1.2 0.8 collective-permute-done
  2.0 0.1 add_select_fusion
  2.1 2.8 %collective-permute-start.1 = (s32[4,2]{0,1:T(2,128)S(1)}, s32[4,2]{0,1:T(2,128)S(1)}, u32[]{:S(2)}, u32[]{:S(2)}) collective-permute-start(s32[4,2]{0,1:T(2,128)S(1)} %add_select_fusion), channel_id=1, source_target_pairs={{0,2},{1,3},{2,0},{3,1},{4,6},{5,7},{6,4},{7,5},{8,10},{9,11},{10,... | collective-permute-start | bytes 104 | tf_op jit(solution)/shard_map/ppermute | solution.py:303
  5.0 1.5 %collective-permute-done.1 = s32[4,2]{0,1:T(2,128)S(1)} collective-permute-done((s32[4,2]{0,1:T(2,128)S(1)}, s32[4,2]{0,1:T(2,128)S(1)}, u32[]{:S(2)}, u32[]{:S(2)}) %collective-permute-start.1) | collective-permute-done | bytes 64 | tf_op jit(solution)/shard_map/ppermute | solution.py:303
  6.6 2.1 %collective-permute-start.2 = (s32[8,2]{0,1:T(2,128)S(1)}, s32[8,2]{0,1:T(2,128)S(1)}, u32[]{:S(2)}, u32[]{:S(2)}) collective-permute-start(s32[8,2]{0,1:T(2,128)S(1)} %add_select_fusion.1), channel_id=1, source_target_pairs={{0,4},{1,5},{2,6},{3,7},{4,0},{5,1},{6,2},{7,3},{8,12},{9,13},{10,... | collective-permute-start | bytes 200 | tf_op jit(solution)/shard_map/ppermute | solution.py:303
  8.7 1.5 %collective-permute-done.2 = s32[8,2]{0,1:T(2,128)S(1)} collective-permute-done((s32[8,2]{0,1:T(2,128)S(1)}, s32[8,2]{0,1:T(2,128)S(1)}, u32[]{:S(2)}, u32[]{:S(2)}) %collective-permute-start.2) | collective-permute-done | bytes 96 | tf_op jit(solution)/shard_map/ppermute | solution.py:303
  10.3 3.0 %collective-permute-start.3 = (s32[16,2]{0,1:T(2,128)S(1)}, s32[16,2]{0,1:T(2,128)S(1)}, u32[]{:S(2)}, u32[]{:S(2)}) collective-permute-start(s32[16,2]{0,1:T(2,128)S(1)} %add_select_fusion.2), channel_id=1, source_target_pairs={{0,8},{1,9},{2,10},{3,11},{4,12},{5,13},{6,14},{7,15},{8,0},{9,1},... | collective-permute-start | bytes 392 | tf_op jit(solution)/shard_map/ppermute | solution.py:303
  13.3 1.5 %collective-permute-done.3 = s32[16,2]{0,1:T(2,128)S(1)} collective-permute-done((s32[16,2]{0,1:T(2,128)S(1)}, s32[16,2]{0,1:T(2,128)S(1)}, u32[]{:S(2)}, u32[]{:S(2)}) %collective-permute-start.3) | collective-permute-done | bytes 160 | tf_op jit(solution)/shard_map/ppermute | solution.py:303
  14.9 0.1 copy.22
  15.0 0.1 copy.23
  15.1 0.6 broadcast_select_fusion.2.pairs
  15.7 4.5 %plan.1 = (s32[16]{0:T(128)}, s32[16]{0:T(128)}, s32[2]{0:T(128)}, bf16[8,2,256,128]{3,2,1,0:T(8,128)(2,1)}, bf16[3,8,256,128]{3,2,1,0:T(8,128)(2,1)}, /*index=5*/bf16[3,8,256,128]{3,2,1,0:T(8,128)(2,1)}) custom-call(s32[1]{0:T(128)} %bitcast.me_ref.me, s32[32,2]{1,0:T(8,128)} %broadcast_select_fusion.2.pairs, bf16[8,2,256,1024]{3,2,1,0:T(8,128)(2,1)} %bitcast.73), custom_call_target="tpu_custom_call" | custom-call | tf_op jit(solution)/shard_map/plan/pallas_call | solution.py:271
  20.4 6.5 %all-to-all-start = ((bf16[16,256,128]{2,1,0:T(8,128)(2,1)}), bf16[16,256,128]{2,1,0:T(8,128)(2,1)}, u32[]{:S(2)}, u32[]{:S(2)}) async-start(bf16[16,256,128]{2,1,0:T(8,128)(2,1)} %bitcast.75), calls=%async_computation | async-start | bytes 2097152 | tf_op jit(solution)/shard_map/all_to_all | solution.py:306
  26.9 0.1 reshape.48
  27.0 0.1 copy.24
  27.7 0.1 add_divide_fusion
  27.9 1.9 %pick.1 = (bf16[12,256,128]{2,1,0:T(8,128)(2,1)S(1)}, bf16[12,256,128]{2,1,0:T(8,128)(2,1)}, bf16[6,512,128]{2,1,0:T(8,128)(2,1)S(1)}, bf16[6,512,128]{2,1,0:T(8,128)(2,1)}) custom-call(s32[1]{0:T(128)} %bitcast.me_ref.me, s32[2]{0:T(128)S(1)} %copy-done.6, bf16[12,2,256,128]{3,2,1,0:T(8,128)(2,1)S(1)} %bitcast.66, bf16[12,2,256,128]{3,2,1,0:T(8,128)(2,1)S(1)} %bitcast.68, ...), custom_call_target="tpu_custom_call" | custom-call | tf_op jit(solution)/shard_map/pick/pallas_call | solution.py:134
  29.8 0.9 copy-done.1
  30.7 0.9 copy-done.3
  31.6 1.9 %collective-permute-start.5 = (bf16[3,2,2,256,128]{4,3,2,1,0:T(8,128)(2,1)}, bf16[3,2,2,256,128]{4,3,2,1,0:T(8,128)(2,1)}, u32[]{:S(2)}, u32[]{:S(2)}) collective-permute-start(bf16[3,2,2,256,128]{4,3,2,1,0:T(8,128)(2,1)} %bitcast.7), channel_id=1, source_target_pairs={{0,2},{1,3},{2,0},{3,1},{4,6},{5,7},{6,4},{7,5},{8,10},{9,11},{10,... | collective-permute-start | bytes 2359304 | tf_op jit(solution)/shard_map/ppermute | solution.py:303
  33.5 1.5 %collective-permute-start.6 = (bf16[3,2,2,256,128]{4,3,2,1,0:T(8,128)(2,1)}, bf16[3,2,2,256,128]{4,3,2,1,0:T(8,128)(2,1)}, u32[]{:S(2)}, u32[]{:S(2)}) collective-permute-start(bf16[3,2,2,256,128]{4,3,2,1,0:T(8,128)(2,1)} %bitcast.8), channel_id=1, source_target_pairs={{0,4},{1,5},{2,6},{3,7},{4,0},{5,1},{6,2},{7,3},{8,12},{9,13},{10,... | collective-permute-start | bytes 2359304 | tf_op jit(solution)/shard_map/ppermute | solution.py:303
  35.0 5.6 %precondition.1 = bf16[16,128,256]{2,1,0:T(8,128)(2,1)} custom-call(bf16[4096,128]{1,0:T(8,128)(2,1)S(1)} %copy-done.9, f32[64,64]{1,0:T(8,128)S(1)} %copy-done.10, f32[64,64]{1,0:T(8,128)S(1)} %copy-done.11, f32[256,16]{1,0:T(8,128)S(1)} %bitcast.72), custom_call_target="tpu_custom_call" | custom-call | flops 3000000000 | bytes 2097152 | tf_op jit(solution)/shard_map/precondition/pallas_call | solution.py:99
  40.6 9.7 %all-to-all-done.first = bf16[16,256,128]{2,1,0:T(8,128)(2,1)} async-done(((bf16[16,256,128]{2,1,0:T(8,128)(2,1)}), bf16[16,256,128]{2,1,0:T(8,128)(2,1)}, u32[]{:S(2)}, u32[]{:S(2)}) %all-to-all-start) | async-done | bytes 1048608 | tf_op jit(solution)/shard_map/all_to_all | solution.py:306
  50.3 6.7 %all-to-all-start.1 = ((bf16[16,128,256]{2,1,0:T(8,128)(2,1)}), bf16[16,128,256]{2,1,0:T(8,128)(2,1)S(1)}, u32[]{:S(2)}, u32[]{:S(2)}) async-start(bf16[16,128,256]{2,1,0:T(8,128)(2,1)} %precondition.1), calls=%async_computation.1 | async-start | bytes 2097152 | tf_op jit(solution)/shard_map/all_to_all | solution.py:306
  57.0 0.6 fusion.10
  58.7 11.1 %collective-permute-done.6 = bf16[3,2,2,256,128]{4,3,2,1,0:T(8,128)(2,1)} collective-permute-done((bf16[3,2,2,256,128]{4,3,2,1,0:T(8,128)(2,1)}, bf16[3,2,2,256,128]{4,3,2,1,0:T(8,128)(2,1)}, u32[]{:S(2)}, u32[]{:S(2)}) %collective-permute-start.6) | collective-permute-done | bytes 786464 | tf_op jit(solution)/shard_map/ppermute | solution.py:303
  69.8 0.2 broadcast_select_fusion
  70.1 1.3 collective-permute-start.8
  71.6 13.8 %collective-permute-done.8 = bf16[3,2,256,128]{3,2,0,1:T(8,128)(2,1)S(1)} collective-permute-done((bf16[3,2,256,128]{3,2,0,1:T(8,128)(2,1)S(1)}, bf16[3,2,256,128]{3,2,0,1:T(8,128)(2,1)S(1)}, u32[]{:S(2)}, u32[]{:S(2)}) %collective-permute-start.8) | collective-permute-done | bytes 393248 | tf_op jit(solution)/shard_map/ppermute | solution.py:303
  85.4 3.6 %collective-permute-done.7 = bf16[3,2,256,128]{3,2,0,1:T(8,128)(2,1)S(1)} collective-permute-done((bf16[3,2,256,128]{3,2,0,1:T(8,128)(2,1)S(1)}, bf16[3,2,256,128]{3,2,0,1:T(8,128)(2,1)S(1)}, u32[]{:S(2)}, u32[]{:S(2)}) %collective-permute-start.7) | collective-permute-done | bytes 393248 | tf_op jit(solution)/shard_map/ppermute | solution.py:303
  89.1 2.6 %collective-permute-start.10 = (bf16[3,256,128]{2,1,0:T(8,128)(2,1)S(1)}, bf16[3,256,128]{2,1,0:T(8,128)(2,1)S(1)}, u32[]{:S(2)}, u32[]{:S(2)}) collective-permute-start(bf16[3,256,128]{2,1,0:T(8,128)(2,1)S(1)} %dynamic-slice_bitcast_fusion), channel_id=1, source_target_pairs={{0,8},{1,9},{2,10},{3,11},{4,12},{5,13},{6,14},{7,15},{8,0},{9,1},... | collective-permute-start | bytes 589832 | tf_op jit(solution)/shard_map/ppermute | solution.py:303
  91.7 0.4 collective-permute-start.9
  92.1 13.6 %collective-permute-done.10 = bf16[3,256,128]{2,1,0:T(8,128)(2,1)S(1)} collective-permute-done((bf16[3,256,128]{2,1,0:T(8,128)(2,1)S(1)}, bf16[3,256,128]{2,1,0:T(8,128)(2,1)S(1)}, u32[]{:S(2)}, u32[]{:S(2)}) %collective-permute-start.10) | collective-permute-done | bytes 196640 | tf_op jit(solution)/shard_map/ppermute | solution.py:303
  105.7 3.4 %collective-permute-done.9 = bf16[3,256,128]{2,1,0:T(8,128)(2,1)S(1)} collective-permute-done((bf16[3,256,128]{2,1,0:T(8,128)(2,1)S(1)}, bf16[3,256,128]{2,1,0:T(8,128)(2,1)S(1)}, u32[]{:S(2)}, u32[]{:S(2)}) %collective-permute-start.9) | collective-permute-done | bytes 196640 | tf_op jit(solution)/shard_map/ppermute | solution.py:303
  109.3 2.7 %partial_scores.1 = (f32[16,128,128]{2,1,0:T(8,128)S(1)}, f32[16,128,128]{2,1,0:T(8,128)S(1)}) custom-call(s32[1]{0:T(128)} %bitcast.me_ref.me, s32[32,2]{1,0:T(8,128)S(1)} %copy-done.5, s32[16]{0:T(128)S(1)} %copy-done.7, s32[16]{0:T(128)S(1)} %copy-done.8, bf16[16,128,256]{2,1,0:T(8,128)(2,1)S(1)} %all-to-all-done.1.train, ...), custom_call_target="tpu_custom_call" | custom-call | tf_op jit(solution)/shard_map/partial_scores/pallas_call | solution.py:175
  112.1 2.6 %collective-permute-done.11 = f32[16,128,128]{2,1,0:T(8,128)S(1)} collective-permute-done((f32[16,128,128]{2,1,0:T(8,128)S(1)}, f32[16,128,128]{2,1,0:T(8,128)S(1)}, u32[]{:S(2)}, u32[]{:S(2)}) %collective-permute-start.11) | collective-permute-done | bytes 1048608 | tf_op jit(solution)/shard_map/ppermute | solution.py:303
  114.7 0.1 add.71
  115.1 1.6 %collective-permute-start.12 = (bf16[2,2,128,128]{3,2,1,0:T(8,128)(2,1)S(1)}, bf16[2,2,128,128]{3,2,1,0:T(8,128)(2,1)S(1)}, u32[]{:S(2)}, u32[]{:S(2)}) collective-permute-start(bf16[2,2,128,128]{3,2,1,0:T(8,128)(2,1)S(1)} %fusion), channel_id=1, source_target_pairs={{0,2},{1,3},{2,0},{3,1},{4,6},{5,7},{6,4},{7,5},{8,10},{9,11},{10,... | collective-permute-start | bytes 393224 | tf_op jit(solution)/shard_map/ppermute | solution.py:303
  116.6 3.9 %collective-permute-done.14 = bf16[2,2,128,128]{3,2,1,0:T(8,128)(2,1)S(1)} collective-permute-done((bf16[2,2,128,128]{3,2,1,0:T(8,128)(2,1)S(1)}, bf16[2,2,128,128]{3,2,1,0:T(8,128)(2,1)S(1)}, u32[]{:S(2)}, u32[]{:S(2)}) %collective-permute-start.14) | collective-permute-done | bytes 131104 | tf_op jit(solution)/shard_map/ppermute | solution.py:303
  120.6 1.6 %collective-permute-start.15 = (f32[2,128,128]{2,1,0:T(8,128)S(1)}, f32[2,128,128]{2,1,0:T(8,128)S(1)}, u32[]{:S(2)}, u32[]{:S(2)}) collective-permute-start(f32[2,128,128]{2,1,0:T(8,128)S(1)} %dynamic-slice_bitcast_fusion.2), channel_id=1, source_target_pairs={{0,2},{1,3},{2,0},{3,1},{4,6},{5,7},{6,4},{7,5},{8,10},{9,11},{10,... | collective-permute-start | bytes 393224 | tf_op jit(solution)/shard_map/ppermute | solution.py:303
  122.2 0.4 collective-permute-start.13
  122.6 3.1 %collective-permute-done.15 = f32[2,128,128]{2,1,0:T(8,128)S(1)} collective-permute-done((f32[2,128,128]{2,1,0:T(8,128)S(1)}, f32[2,128,128]{2,1,0:T(8,128)S(1)}, u32[]{:S(2)}, u32[]{:S(2)}) %collective-permute-start.15) | collective-permute-done | bytes 131104 | tf_op jit(solution)/shard_map/ppermute | solution.py:303
  125.7 1.6 %collective-permute-done.13 = f32[2,128,128]{2,1,0:T(8,128)S(1)} collective-permute-done((f32[2,128,128]{2,1,0:T(8,128)S(1)}, f32[2,128,128]{2,1,0:T(8,128)S(1)}, u32[]{:S(2)}, u32[]{:S(2)}) %collective-permute-start.13) | collective-permute-done | bytes 131104 | tf_op jit(solution)/shard_map/ppermute | solution.py:303
  127.3 1.6 %collective-permute-start.16 = (f32[2,128,128]{2,1,0:T(8,128)S(1)}, f32[2,128,128]{2,1,0:T(8,128)S(1)}, u32[]{:S(2)}, u32[]{:S(2)}) collective-permute-start(f32[2,128,128]{2,1,0:T(8,128)S(1)} %fusion.3), channel_id=1, source_target_pairs={{0,8},{1,9},{2,10},{3,11},{4,12},{5,13},{6,14},{7,15},{8,0},{9,1},... | collective-permute-start | bytes 393224 | tf_op jit(solution)/shard_map/ppermute | solution.py:303
  128.9 5.7 %collective-permute-done.16 = f32[2,128,128]{2,1,0:T(8,128)S(1)} collective-permute-done((f32[2,128,128]{2,1,0:T(8,128)S(1)}, f32[2,128,128]{2,1,0:T(8,128)S(1)}, u32[]{:S(2)}, u32[]{:S(2)}) %collective-permute-start.16) | collective-permute-done | bytes 131104 | tf_op jit(solution)/shard_map/ppermute | solution.py:303
  134.7 0.7 fusion.6
  (58 shorter events, 1.2 us)
Async XLA Ops:
  0.8 1.3 collective-permute-start
  2.1 4.4 %collective-permute-start.1 = (s32[4,2]{0,1:T(2,128)S(1)}, s32[4,2]{0,1:T(2,128)S(1)}, u32[]{:S(2)}, u32[]{:S(2)}) collective-permute-start(s32[4,2]{0,1:T(2,128)S(1)} %add_select_fusion), channel_id=1, source_target_pairs={{0,2},{1,3},{2,0},{3,1},{4,6},{5,7},{6,4},{7,5},{8,10},{9,11},{10,... | collective-permute-start | bytes 104 | tf_op jit(solution)/shard_map/ppermute | solution.py:303
  6.6 3.6 %collective-permute-start.2 = (s32[8,2]{0,1:T(2,128)S(1)}, s32[8,2]{0,1:T(2,128)S(1)}, u32[]{:S(2)}, u32[]{:S(2)}) collective-permute-start(s32[8,2]{0,1:T(2,128)S(1)} %add_select_fusion.1), channel_id=1, source_target_pairs={{0,4},{1,5},{2,6},{3,7},{4,0},{5,1},{6,2},{7,3},{8,12},{9,13},{10,... | collective-permute-start | bytes 200 | tf_op jit(solution)/shard_map/ppermute | solution.py:303
  10.3 4.6 %collective-permute-start.3 = (s32[16,2]{0,1:T(2,128)S(1)}, s32[16,2]{0,1:T(2,128)S(1)}, u32[]{:S(2)}, u32[]{:S(2)}) collective-permute-start(s32[16,2]{0,1:T(2,128)S(1)} %add_select_fusion.2), channel_id=1, source_target_pairs={{0,8},{1,9},{2,10},{3,11},{4,12},{5,13},{6,14},{7,15},{8,0},{9,1},... | collective-permute-start | bytes 392 | tf_op jit(solution)/shard_map/ppermute | solution.py:303
  20.3 6.6 %copy-start.13 = (f32[64]{0:T(128)S(1)}, f32[64]{0:T(128)}, u32[]{:S(2)}) copy-start(f32[64]{0:T(128)} %param.14) | copy-start | bytes 772
  20.3 7.4 %copy-start.12 = (f32[64]{0:T(128)S(1)}, f32[64]{0:T(128)}, u32[]{:S(2)}) copy-start(f32[64]{0:T(128)} %param.13) | copy-start | bytes 772
  20.3 7.5 %copy-start = (bf16[3,8,256,128]{3,2,1,0:T(8,128)(2,1)S(1)}, bf16[3,8,256,128]{3,2,1,0:T(8,128)(2,1)}, u32[]{:S(2)}) copy-start(bf16[3,8,256,128]{3,2,1,0:T(8,128)(2,1)} %get-tuple-element.34) | copy-start | bytes 4718596
  20.3 7.5 %copy-start.6 = (s32[2]{0:T(128)S(1)}, s32[2]{0:T(128)}, u32[]{:S(2)}) copy-start(s32[2]{0:T(128)} %get-tuple-element.33.where) | copy-start | bytes 28
  20.3 7.5 %collective-permute-start.4 = (bf16[3,8,256,128]{3,2,1,0:T(8,128)(2,1)}, bf16[3,8,256,128]{3,2,1,0:T(8,128)(2,1)S(1)}, u32[]{:S(2)}, u32[]{:S(2)}) collective-permute-start(bf16[3,8,256,128]{3,2,1,0:T(8,128)(2,1)} %get-tuple-element.35), channel_id=1, source_target_pairs={{0,1},{1,0},{2,3},{3,2},{4,5},{5,4},{6,7},{7,6},{8,9},{9,8},{10,11... | collective-permute-start | bytes 4718600 | tf_op jit(solution)/shard_map/ppermute | solution.py:303
  20.4 29.9 %all-to-all-start = ((bf16[16,256,128]{2,1,0:T(8,128)(2,1)}), bf16[16,256,128]{2,1,0:T(8,128)(2,1)}, u32[]{:S(2)}, u32[]{:S(2)}) async-start(bf16[16,256,128]{2,1,0:T(8,128)(2,1)} %bitcast.75), calls=%async_computation | async-start | bytes 2097152 | tf_op jit(solution)/shard_map/all_to_all | solution.py:306
  27.8 7.1 %copy-start.9 = (bf16[4096,128]{1,0:T(8,128)(2,1)S(1)}, bf16[4096,128]{1,0:T(8,128)(2,1)}, u32[]{:S(2)}) copy-start(bf16[4096,128]{1,0:T(8,128)(2,1)} %train.1) | copy-start | bytes 3145732
  27.9 7.1 %copy-start.10 = (f32[64,64]{1,0:T(8,128)S(1)}, f32[64,64]{1,0:T(8,128)}, u32[]{:S(2)}) copy-start(f32[64,64]{1,0:T(8,128)} %basis_in.1) | copy-start | bytes 49156
  27.9 7.1 %copy-start.11 = (f32[64,64]{1,0:T(8,128)S(1)}, f32[64,64]{1,0:T(8,128)}, u32[]{:S(2)}) copy-start(f32[64,64]{1,0:T(8,128)} %basis_out.1) | copy-start | bytes 49156
  29.8 0.9 copy-start.1
  30.7 0.9 copy-start.3
  31.6 27.1 %collective-permute-start.5 = (bf16[3,2,2,256,128]{4,3,2,1,0:T(8,128)(2,1)}, bf16[3,2,2,256,128]{4,3,2,1,0:T(8,128)(2,1)}, u32[]{:S(2)}, u32[]{:S(2)}) collective-permute-start(bf16[3,2,2,256,128]{4,3,2,1,0:T(8,128)(2,1)} %bitcast.7), channel_id=1, source_target_pairs={{0,2},{1,3},{2,0},{3,1},{4,6},{5,7},{6,4},{7,5},{8,10},{9,11},{10,... | collective-permute-start | bytes 2359304 | tf_op jit(solution)/shard_map/ppermute | solution.py:303
  33.5 36.4 %collective-permute-start.6 = (bf16[3,2,2,256,128]{4,3,2,1,0:T(8,128)(2,1)}, bf16[3,2,2,256,128]{4,3,2,1,0:T(8,128)(2,1)}, u32[]{:S(2)}, u32[]{:S(2)}) collective-permute-start(bf16[3,2,2,256,128]{4,3,2,1,0:T(8,128)(2,1)} %bitcast.8), channel_id=1, source_target_pairs={{0,4},{1,5},{2,6},{3,7},{4,0},{5,1},{6,2},{7,3},{8,12},{9,13},{10,... | collective-permute-start | bytes 2359304 | tf_op jit(solution)/shard_map/ppermute | solution.py:303
  40.6 29.3 %copy-start.2 = (bf16[12,256,128]{2,1,0:T(8,128)(2,1)S(1)}, bf16[12,256,128]{2,1,0:T(8,128)(2,1)}, u32[]{:S(2)}) copy-start(bf16[12,256,128]{2,1,0:T(8,128)(2,1)} %copy-done.1) | copy-start | bytes 2359300
  40.6 29.3 %copy-start.4 = (bf16[6,512,128]{2,1,0:T(8,128)(2,1)S(1)}, bf16[6,512,128]{2,1,0:T(8,128)(2,1)}, u32[]{:S(2)}) copy-start(bf16[6,512,128]{2,1,0:T(8,128)(2,1)} %copy-done.3) | copy-start | bytes 2359300
  50.3 38.8 %all-to-all-start.1 = ((bf16[16,128,256]{2,1,0:T(8,128)(2,1)}), bf16[16,128,256]{2,1,0:T(8,128)(2,1)S(1)}, u32[]{:S(2)}, u32[]{:S(2)}) async-start(bf16[16,128,256]{2,1,0:T(8,128)(2,1)} %precondition.1), calls=%async_computation.1 | async-start | bytes 2097152 | tf_op jit(solution)/shard_map/all_to_all | solution.py:306
  70.1 15.2 %collective-permute-start.8 = (bf16[3,2,256,128]{3,2,0,1:T(8,128)(2,1)S(1)}, bf16[3,2,256,128]{3,2,0,1:T(8,128)(2,1)S(1)}, u32[]{:S(2)}, u32[]{:S(2)}) collective-permute-start(bf16[3,2,256,128]{3,2,0,1:T(8,128)(2,1)S(1)} %bitcast.76), channel_id=1, source_target_pairs={{0,2},{1,3},{2,0},{3,1},{4,6},{5,7},{6,4},{7,5},{8,10},{9,11},{10,... | collective-permute-start | bytes 1179656 | tf_op jit(solution)/shard_map/ppermute | solution.py:303
  71.5 17.4 %collective-permute-start.7 = (bf16[3,2,256,128]{3,2,0,1:T(8,128)(2,1)S(1)}, bf16[3,2,256,128]{3,2,0,1:T(8,128)(2,1)S(1)}, u32[]{:S(2)}, u32[]{:S(2)}) collective-permute-start(bf16[3,2,256,128]{3,2,0,1:T(8,128)(2,1)S(1)} %bitcast.77), channel_id=1, source_target_pairs={{0,4},{1,5},{2,6},{3,7},{4,0},{5,1},{6,2},{7,3},{8,12},{9,13},{10,... | collective-permute-start | bytes 1179656 | tf_op jit(solution)/shard_map/ppermute | solution.py:303
  89.0 20.3 %copy-start.5 = (s32[32,2]{1,0:T(8,128)S(1)}, s32[32,2]{1,0:T(8,128)}, u32[]{:S(2)}) copy-start(s32[32,2]{1,0:T(8,128)} %broadcast_select_fusion.2.pairs) | copy-start | bytes 772
  89.0 20.3 %copy-start.7 = (s32[16]{0:T(128)S(1)}, s32[16]{0:T(128)}, u32[]{:S(2)}) copy-start(s32[16]{0:T(128)} %get-tuple-element.31.masks) | copy-start | bytes 196
  89.0 20.3 %copy-start.8 = (s32[16]{0:T(128)S(1)}, s32[16]{0:T(128)}, u32[]{:S(2)}) copy-start(s32[16]{0:T(128)} %get-tuple-element.32.ranks) | copy-start | bytes 196
  89.1 16.6 %collective-permute-start.10 = (bf16[3,256,128]{2,1,0:T(8,128)(2,1)S(1)}, bf16[3,256,128]{2,1,0:T(8,128)(2,1)S(1)}, u32[]{:S(2)}, u32[]{:S(2)}) collective-permute-start(bf16[3,256,128]{2,1,0:T(8,128)(2,1)S(1)} %dynamic-slice_bitcast_fusion), channel_id=1, source_target_pairs={{0,8},{1,9},{2,10},{3,11},{4,12},{5,13},{6,14},{7,15},{8,0},{9,1},... | collective-permute-start | bytes 589832 | tf_op jit(solution)/shard_map/ppermute | solution.py:303
  91.7 17.4 %collective-permute-start.9 = (bf16[3,256,128]{2,1,0:T(8,128)(2,1)S(1)}, bf16[3,256,128]{2,1,0:T(8,128)(2,1)S(1)}, u32[]{:S(2)}, u32[]{:S(2)}) collective-permute-start(bf16[3,256,128]{2,1,0:T(8,128)(2,1)S(1)} %dynamic-slice_bitcast_fusion.1), channel_id=1, source_target_pairs={{0,8},{1,9},{2,10},{3,11},{4,12},{5,13},{6,14},{7,15},{8,0},{9,1},... | collective-permute-start | bytes 589832 | tf_op jit(solution)/shard_map/ppermute | solution.py:303
  112.0 2.7 %collective-permute-start.11 = (f32[16,128,128]{2,1,0:T(8,128)S(1)}, f32[16,128,128]{2,1,0:T(8,128)S(1)}, u32[]{:S(2)}, u32[]{:S(2)}) collective-permute-start(f32[16,128,128]{2,1,0:T(8,128)S(1)} %get-tuple-element.56), channel_id=1, source_target_pairs={{0,1},{1,0},{2,3},{3,2},{4,5},{5,4},{6,7},{7,6},{8,9},{9,8},{10,11... | collective-permute-start | bytes 3145736 | tf_op jit(solution)/shard_map/ppermute | solution.py:303
  115.0 5.6 %collective-permute-start.14 = (bf16[2,2,128,128]{3,2,1,0:T(8,128)(2,1)S(1)}, bf16[2,2,128,128]{3,2,1,0:T(8,128)(2,1)S(1)}, u32[]{:S(2)}, u32[]{:S(2)}) collective-permute-start(bf16[2,2,128,128]{3,2,1,0:T(8,128)(2,1)S(1)} %fusion.1), channel_id=1, source_target_pairs={{0,4},{1,5},{2,6},{3,7},{4,0},{5,1},{6,2},{7,3},{8,12},{9,13},{10,... | collective-permute-start | bytes 393224 | tf_op jit(solution)/shard_map/ppermute | solution.py:303
  115.1 7.1 %collective-permute-start.12 = (bf16[2,2,128,128]{3,2,1,0:T(8,128)(2,1)S(1)}, bf16[2,2,128,128]{3,2,1,0:T(8,128)(2,1)S(1)}, u32[]{:S(2)}, u32[]{:S(2)}) collective-permute-start(bf16[2,2,128,128]{3,2,1,0:T(8,128)(2,1)S(1)} %fusion), channel_id=1, source_target_pairs={{0,2},{1,3},{2,0},{3,1},{4,6},{5,7},{6,4},{7,5},{8,10},{9,11},{10,... | collective-permute-start | bytes 393224 | tf_op jit(solution)/shard_map/ppermute | solution.py:303
  120.6 5.0 %collective-permute-start.15 = (f32[2,128,128]{2,1,0:T(8,128)S(1)}, f32[2,128,128]{2,1,0:T(8,128)S(1)}, u32[]{:S(2)}, u32[]{:S(2)}) collective-permute-start(f32[2,128,128]{2,1,0:T(8,128)S(1)} %dynamic-slice_bitcast_fusion.2), channel_id=1, source_target_pairs={{0,2},{1,3},{2,0},{3,1},{4,6},{5,7},{6,4},{7,5},{8,10},{9,11},{10,... | collective-permute-start | bytes 393224 | tf_op jit(solution)/shard_map/ppermute | solution.py:303
  122.2 5.0 %collective-permute-start.13 = (f32[2,128,128]{2,1,0:T(8,128)S(1)}, f32[2,128,128]{2,1,0:T(8,128)S(1)}, u32[]{:S(2)}, u32[]{:S(2)}) collective-permute-start(f32[2,128,128]{2,1,0:T(8,128)S(1)} %dynamic-slice_bitcast_fusion.3), channel_id=1, source_target_pairs={{0,4},{1,5},{2,6},{3,7},{4,0},{5,1},{6,2},{7,3},{8,12},{9,13},{10,... | collective-permute-start | bytes 393224 | tf_op jit(solution)/shard_map/ppermute | solution.py:303
  127.3 7.3 %collective-permute-start.16 = (f32[2,128,128]{2,1,0:T(8,128)S(1)}, f32[2,128,128]{2,1,0:T(8,128)S(1)}, u32[]{:S(2)}, u32[]{:S(2)}) collective-permute-start(f32[2,128,128]{2,1,0:T(8,128)S(1)} %fusion.3), channel_id=1, source_target_pairs={{0,8},{1,9},{2,10},{3,11},{4,12},{5,13},{6,14},{7,15},{8,0},{9,1},... | collective-permute-start | bytes 393224 | tf_op jit(solution)/shard_map/ppermute | solution.py:303

commit v5 on v4

--- a/solution.py
+++ b/solution.py
@@ -141,117 +141,121 @@
     )(me.reshape(1), where, *sources)
 
 
-def score_kernel(per_device, local_blocks, me_ref, pairs, masks, ranks, train, first, extra, keep, send):
+def score_kernel(which, per_device, me_ref, rows, train, first, extra, keep, send):
     core = me_ref[0] & 1
+    devices = first.shape[0]
+
+    def tile(device):
+        pair = device * per_device + which
+        slot = rows[1, pair]
+        a = first[jnp.minimum(slot, devices - 1)]
+        b = extra[jnp.maximum(slot - devices, 0)]
+        q = jnp.where(slot < devices, a.astype(f32), b.astype(f32)).astype(bf16)
+        return mm(train[rows[0, pair]], q)
+
+    def step(h, carry):
+        keep[h] = tile(2 * h + core)
+        send[h] = tile(2 * h + 1 - core)
+        return carry
+
+    lax.fori_loop(0, keep.shape[0], step, 0, unroll=4)
+
+
+def partial_scores(which, per_device, me, rows, train, first, extra):
+    half = rows.shape[1] // (2 * per_device)
+    tiles = jax.ShapeDtypeStruct((half, COLS, COLS), f32)
+    whole = pl.BlockSpec(memory_space=pltpu.VMEM)
+    return pl.pallas_call(
+        functools.partial(score_kernel, which, per_device),
+        out_shape=(tiles, tiles),
+        in_specs=[pl.BlockSpec(memory_space=pltpu.SMEM)] * 2 + [whole] * 3,
+        out_specs=(whole, whole),
+        compiler_params=pltpu.CompilerParams(vmem_limit_bytes=VMEM_LIMIT),
+        name="partial_scores",
+    )(me.reshape(1), rows, train, first, extra)
+
+
+def plan_kernel(
+    me_ref, pairs, query, rows, hots, first, keep, send, masks, ranks, own, first_sem, keep_sem, send_sem
+):
+    me = me_ref[0]
+    devices, total = masks.shape[0], pairs.shape[0]
+    local_blocks = query.shape[3] // COLS
     level = local_blocks.bit_length() - 1
-    devices = first.shape[0]
-
-    def tile(pair):
-        block = pairs[pair, 1]
+
+    @pl.loop(0, devices, unroll=8)
+    def _(d):
+        masks[d] = 0
+
+    @pl.loop(0, total, unroll=8)
+    def _(p):
+        block = pairs[p, 1]
+        d = lax.shift_right_logical(block, level)
+        masks[d] = masks[d] | lax.shift_left(1, block & (local_blocks - 1))
+
+    count = jnp.int32(0)
+    mask = masks[me]
+    for k in range(local_blocks):
+        bit = lax.shift_right_logical(mask, k) & 1
+
+        @pl.when(bit == 1)
+        def _():
+            own[jnp.minimum(count, EXTRA)] = k
+
+        count = count + bit
+    is_hot = count > 1
+
+    def cut(k, source, target, sem):
+        start = pl.multiple_of(own[k] * COLS, COLS)
+        return pltpu.make_async_copy(source.at[..., pl.ds(start, COLS)], target, sem)
+
+    core = me & 1
+    parts = first_sem.shape[0]
+    length = query.shape[0] // parts
+
+    def first_copies(part):
+        at = pl.ds(part * length, length)
+        return cut(0, query.at[at], first.at[at], first_sem.at[part])
+
+    for part in range(parts):
+        first_copies(part).start()
+
+    def extra_copies(k):
+        return (
+            cut(k + 1, query.at[:, core], keep.at[k], keep_sem.at[k]),
+            cut(k + 1, query.at[:, 1 - core], send.at[k], send_sem.at[k]),
+        )
+
+    @pl.when(is_hot)
+    def _():
+        for k in range(EXTRA):
+            for copy in extra_copies(k):
+                copy.start()
+
+    def rank_step(d, rank):
+        mask = masks[d]
+        hot = (mask & (mask - 1)) != 0
+
+        ranks[d] = rank
+
+        @pl.when(hot)
+        def _():
+            hots[jnp.minimum(rank, hots.shape[0] - 1)] = d
+
+        return rank + jnp.where(hot, 1, 0)
+
+    lax.fori_loop(0, devices, rank_step, jnp.int32(0), unroll=4)
+
+    @pl.loop(0, total, unroll=4)
+    def _(p):
+        block = pairs[p, 1]
         d = lax.shift_right_logical(block, level)
         before = masks[d] & (lax.shift_left(1, block & (local_blocks - 1)) - 1)
         order = before & 1
         for k in range(1, local_blocks):
             order = order + (lax.shift_right_logical(before, k) & 1)
-        slot = jnp.where(order == 0, d, devices + EXTRA * ranks[d] + order - 1)
-        a = first[jnp.minimum(slot, devices - 1)]
-        b = extra[jnp.maximum(slot - devices, 0)]
-        q = jnp.where(slot < devices, a.astype(f32), b.astype(f32)).astype(bf16)
-        return mm(train[pairs[pair, 0]], q)
-
-    def step(h, carry):
-        base = h // per_device * (2 * per_device) + h % per_device
-        keep[h] = tile(base + core * per_device)
-        send[h] = tile(base + (1 - core) * per_device)
-        return carry
-
-    lax.fori_loop(0, keep.shape[0], step, 0, unroll=4)
-
-
-def partial_scores(per_device, local_blocks, me, pairs, masks, ranks, train, first, extra):
-    half = pairs.shape[0] // 2
-    tiles = jax.ShapeDtypeStruct((half, COLS, COLS), f32)
-    whole = pl.BlockSpec(memory_space=pltpu.VMEM)
-    return pl.pallas_call(
-        functools.partial(score_kernel, per_device, local_blocks),
-        out_shape=(tiles, tiles),
-        in_specs=[pl.BlockSpec(memory_space=pltpu.SMEM)] * 4 + [whole] * 3,
-        out_specs=(whole, whole),
-        compiler_params=pltpu.CompilerParams(vmem_limit_bytes=VMEM_LIMIT),
-        name="partial_scores",
-    )(me.reshape(1), pairs, masks, ranks, train, first, extra)
-
-
-def plan_kernel(
-    me_ref, pairs, query, masks, ranks, hots, first, keep, send, own, first_sem, keep_sem, send_sem
-):
-    me = me_ref[0]
-    devices, total = masks.shape[0], pairs.shape[0]
-    local_blocks = query.shape[3] // COLS
-    level = local_blocks.bit_length() - 1
-
-    @pl.loop(0, devices, unroll=8)
-    def _(d):
-        masks[d] = 0
-
-    @pl.loop(0, total, unroll=8)
-    def _(p):
-        block = pairs[p, 1]
-        d = lax.shift_right_logical(block, level)
-        masks[d] = masks[d] | lax.shift_left(1, block & (local_blocks - 1))
-
-    count = jnp.int32(0)
-    mask = masks[me]
-    for k in range(local_blocks):
-        bit = lax.shift_right_logical(mask, k) & 1
-
-        @pl.when(bit == 1)
-        def _():
-            own[jnp.minimum(count, EXTRA)] = k
-
-        count = count + bit
-    is_hot = count > 1
-
-    def cut(k, source, target, sem):
-        start = pl.multiple_of(own[k] * COLS, COLS)
-        return pltpu.make_async_copy(source.at[..., pl.ds(start, COLS)], target, sem)
-
-    core = me & 1
-    parts = first_sem.shape[0]
-    length = query.shape[0] // parts
-
-    def first_copies(part):
-        at = pl.ds(part * length, length)
-        return cut(0, query.at[at], first.at[at], first_sem.at[part])
-
-    for part in range(parts):
-        first_copies(part).start()
-
-    def extra_copies(k):
-        return (
-            cut(k + 1, query.at[:, core], keep.at[k], keep_sem.at[k]),
-            cut(k + 1, query.at[:, 1 - core], send.at[k], send_sem.at[k]),
-        )
-
-    @pl.when(is_hot)
-    def _():
-        for k in range(EXTRA):
-            for copy in extra_copies(k):
-                copy.start()
-
-    def rank_step(d, rank):
-        mask = masks[d]
-        hot = (mask & (mask - 1)) != 0
-
-        ranks[d] = rank
-
-        @pl.when(hot)
-        def _():
-            hots[jnp.minimum(rank, hots.shape[0] - 1)] = d
-
-        return rank + jnp.where(hot, 1, 0)
-
-    lax.fori_loop(0, devices, rank_step, jnp.int32(0), unroll=4)
+        rows[0, p] = pairs[p, 0]
+        rows[1, p] = jnp.where(order == 0, d, devices + EXTRA * ranks[d] + order - 1)
 
     for part in range(parts):
         first_copies(part).wait()
@@ -271,16 +275,17 @@
     return pl.pallas_call(
         plan_kernel,
         out_shape=(
-            jax.ShapeDtypeStruct((devices,), jnp.int32),
-            jax.ShapeDtypeStruct((devices,), jnp.int32),
+            jax.ShapeDtypeStruct((2, pairs.shape[0]), jnp.int32),
             jax.ShapeDtypeStruct((hot_total,), jnp.int32),
             jax.ShapeDtypeStruct((half, 2, share, COLS), bf16),
             extra,
             extra,
         ),
         in_specs=[smem, smem, hbm],
-        out_specs=(smem, smem, smem, vmem, vmem, vmem),
+        out_specs=(smem, smem, vmem, vmem, vmem),
         scratch_shapes=[
+            pltpu.SMEM((devices,), jnp.int32),
+            pltpu.SMEM((devices,), jnp.int32),
             pltpu.SMEM((NAMED_MOST,), jnp.int32),
             pltpu.SemaphoreType.DMA((8,)),
             pltpu.SemaphoreType.DMA((EXTRA,)),
@@ -310,7 +315,7 @@
         other = across(pairs, b)
         pairs = jnp.where(mine[b] == 0, jnp.concatenate([pairs, other]), jnp.concatenate([other, pairs]))
 
-    masks, ranks, hots, first, keep, send = plan(me, pairs, query_gradients, devices, share, hot_total)
+    rows, hots, first, keep, send = plan(me, pairs, query_gradients, devices, share, hot_total)
     first_share = to_all(first.reshape(devices, share, COLS))
     def halves(x, b, left):
         axis = 1 + sorted(left, reverse=True).index(b)
@@ -362,15 +367,10 @@
             chain[:3] = parts[rank][0], others[rank], chain[3][k]
     extra_share = jnp.concatenate([arrived(hots[r], chain[2], chain[0], chain[1]) for r, chain in enumerate(chains)])
 
-    local_blocks = query_gradients.shape[1] // COLS
-    keep, send = partial_scores(
-        per_device, local_blocks, me, pairs, masks, ranks, train_share, first_share, extra_share
-    )
-    tiles = keep + across(send, 0)
-    tiles = tiles.reshape((2,) * (bits - 1) + (per_device, COLS, COLS))
     sums, middle = [], list(range(1, bits - 1))
     for pair in range(per_device):
-        x, left = tiles[..., pair, :, :], list(range(1, bits))
+        keep, send = partial_scores(pair, per_device, me, rows, train_share, first_share, extra_share)
+        x, left = (keep + across(send, 0)).reshape((2,) * (bits - 1) + (COLS, COLS)), list(range(1, bits))
         turn = pair % 2
         for k, b in enumerate(middle[turn:] + middle[:turn]):
             axis = sorted(left, reverse=True).index(b)

time: 136 us -> 136 us (level)
  waiting for transfers between devices: 77.7 us -> 69.4 us
  local copies, waits for them, and re-layouts: 3.93 us -> 7.16 us
  other arithmetic: 2.23 us -> 4.33 us
  starting transfers between devices: 34.5 us -> 36 us
    ppermute x17 -> x18, waiting for transfers between devices: 68 us -> 62.9 us  [across(): return lax.ppermute(x, 'dp', [(d, d ^ 1 << b) for d in range(devices)])]
    all_to_all x2, waiting for transfers between devices: 9.7 us -> 6.46 us  [to_all(): return lax.all_to_all(x, 'dp', split_axis=0, concat_axis=0, tiled=True)]
    select_n x5 -> x6, other arithmetic: 0.3 us -> 2.38 us  [arrived(): return jnp.where((me ^ hot) >> b & 1 == 1, other, keep)]
    unnamed x29 -> x21, local copies, waits for them, and re-layouts: 2.63 us -> 4.42 us
    ppermute x17 -> x18, starting transfers between devices: 21.3 us -> 22.9 us  [across(): return lax.ppermute(x, 'dp', [(d, d ^ 1 << b) for d in range(devices)])]
    pallas_call x2 -> x3, Pallas kernels: 7.2 us -> 6.93 us  [the longest x1 4.55 us: plan(): pl.pallas_call(plan_kernel, out_shape=(jax.ShapeDtypeStruct((2, pairs.sha...]
  transfers between devices with their start and end apart: 19 -> 20, of which waited for: 15 -> 16; matrix products, arithmetic and copies ran while one was open for 1% -> 3% of each run, Pallas kernels for 6% -> 7%
where the time goes in v5:
time: 136 us; the launch traced here: 135 us
  waiting for transfers between devices  69.4 us (51%)
  starting transfers between devices  36 us (26%)
  Pallas kernels  15.8 us (12%)
  local copies, waits for them, and re-layouts  7.16 us (5%)
  other arithmetic  4.33 us (3%)
  between operations  2.36 us (2%)
    ppermute x18, waiting for transfers between devices, across(): return lax.ppermute(x, 'dp', [(d, d ^ 1 << b) for d in range(devices)])  62.9 us
    ppermute x18, starting transfers between devices, across(): return lax.ppermute(x, 'dp', [(d, d ^ 1 << b) for d in range(devices)])  22.9 us
    all_to_all x2, starting transfers between devices, to_all(): return lax.all_to_all(x, 'dp', split_axis=0, concat_axis=0, tiled=True)  13.1 us
    all_to_all x2, waiting for transfers between devices, to_all(): return lax.all_to_all(x, 'dp', split_axis=0, concat_axis=0, tiled=True)  6.46 us
    pallas_call x1, Pallas kernels, precondition(): pl.pallas_call(precondition_kernel, out_shape=jax.ShapeDtypeStruct((chunk...  5.64 us
    pallas_call x1, Pallas kernels, plan(): pl.pallas_call(plan_kernel, out_shape=(jax.ShapeDtypeStruct((2, pairs.sha...  4.55 us
    unnamed x21, local copies, waits for them, and re-layouts  4.42 us
    pallas_call x1, Pallas kernels, pick(): pl.pallas_call(functools.partial(pick_kernel, plan_of), out_shape=shapes,...  3.28 us
  transfers between devices with their start and end apart: 20, of which 16 were waited for; matrix products, arithmetic and copies ran while one was open for 3% of the time, Pallas kernels for 7%

profile of v5, /device:TPU:0, one launch (start us, length us, event | category | flops | bytes accessed | tf_op | source)
XLA Modules:
  0.0 135.1 jit_solution(902596686203411746)
XLA Ops:
  0.0 0.8 copy.20
  0.8 0.5 collective-permute-start
  1.2 0.8 collective-permute-done
  2.1 2.8 %collective-permute-start.1 = (s32[4,2]{0,1:T(2,128)S(1)}, s32[4,2]{0,1:T(2,128)S(1)}, u32[]{:S(2)}, u32[]{:S(2)}) collective-permute-start(s32[4,2]{0,1:T(2,128)S(1)} %add_select_fusion), channel_id=1, source_target_pairs={{0,2},{1,3},{2,0},{3,1},{4,6},{5,7},{6,4},{7,5},{8,10},{9,11},{10,... | collective-permute-start | bytes 104 | tf_op jit(solution)/shard_map/ppermute | solution.py:308
  5.0 1.5 %collective-permute-done.1 = s32[4,2]{0,1:T(2,128)S(1)} collective-permute-done((s32[4,2]{0,1:T(2,128)S(1)}, s32[4,2]{0,1:T(2,128)S(1)}, u32[]{:S(2)}, u32[]{:S(2)}) %collective-permute-start.1) | collective-permute-done | bytes 64 | tf_op jit(solution)/shard_map/ppermute | solution.py:308
  6.6 2.1 %collective-permute-start.2 = (s32[8,2]{0,1:T(2,128)S(1)}, s32[8,2]{0,1:T(2,128)S(1)}, u32[]{:S(2)}, u32[]{:S(2)}) collective-permute-start(s32[8,2]{0,1:T(2,128)S(1)} %add_select_fusion.1), channel_id=1, source_target_pairs={{0,4},{1,5},{2,6},{3,7},{4,0},{5,1},{6,2},{7,3},{8,12},{9,13},{10,... | collective-permute-start | bytes 200 | tf_op jit(solution)/shard_map/ppermute | solution.py:308
  8.7 1.5 %collective-permute-done.2 = s32[8,2]{0,1:T(2,128)S(1)} collective-permute-done((s32[8,2]{0,1:T(2,128)S(1)}, s32[8,2]{0,1:T(2,128)S(1)}, u32[]{:S(2)}, u32[]{:S(2)}) %collective-permute-start.2) | collective-permute-done | bytes 96 | tf_op jit(solution)/shard_map/ppermute | solution.py:308
  10.3 3.0 %collective-permute-start.3 = (s32[16,2]{0,1:T(2,128)S(1)}, s32[16,2]{0,1:T(2,128)S(1)}, u32[]{:S(2)}, u32[]{:S(2)}) collective-permute-start(s32[16,2]{0,1:T(2,128)S(1)} %add_select_fusion.2), channel_id=1, source_target_pairs={{0,8},{1,9},{2,10},{3,11},{4,12},{5,13},{6,14},{7,15},{8,0},{9,1},... | collective-permute-start | bytes 392 | tf_op jit(solution)/shard_map/ppermute | solution.py:308
  13.3 1.5 %collective-permute-done.3 = s32[16,2]{0,1:T(2,128)S(1)} collective-permute-done((s32[16,2]{0,1:T(2,128)S(1)}, s32[16,2]{0,1:T(2,128)S(1)}, u32[]{:S(2)}, u32[]{:S(2)}) %collective-permute-start.3) | collective-permute-done | bytes 160 | tf_op jit(solution)/shard_map/ppermute | solution.py:308
  15.1 0.6 broadcast_select_fusion.2.pairs
  15.7 4.5 %plan.1 = (s32[2,32]{1,0:T(2,128)}, s32[2]{0:T(128)}, bf16[8,2,256,128]{3,2,1,0:T(8,128)(2,1)}, bf16[3,8,256,128]{3,2,1,0:T(8,128)(2,1)}, bf16[3,8,256,128]{3,2,1,0:T(8,128)(2,1)}) custom-call(s32[1]{0:T(128)} %bitcast.me_ref.me, s32[32,2]{1,0:T(8,128)} %broadcast_select_fusion.2.pairs, bf16[8,2,256,1024]{3,2,1,0:T(8,128)(2,1)} %bitcast.72), custom_call_target="tpu_custom_call" | custom-call | tf_op jit(solution)/shard_map/plan/pallas_call | solution.py:275
  20.4 6.4 %all-to-all-start = ((bf16[16,256,128]{2,1,0:T(8,128)(2,1)}), bf16[16,256,128]{2,1,0:T(8,128)(2,1)S(1)}, u32[]{:S(2)}, u32[]{:S(2)}) async-start(bf16[16,256,128]{2,1,0:T(8,128)(2,1)} %bitcast.77), calls=%async_computation | async-start | bytes 2097152 | tf_op jit(solution)/shard_map/all_to_all | solution.py:311
  27.8 3.3 %pick.1 = (bf16[12,256,128]{2,1,0:T(8,128)(2,1)S(1)}, bf16[12,256,128]{2,1,0:T(8,128)(2,1)}, bf16[6,512,128]{2,1,0:T(8,128)(2,1)S(1)}, bf16[6,512,128]{2,1,0:T(8,128)(2,1)}) custom-call(s32[1]{0:T(128)} %bitcast.me_ref.me, s32[2]{0:T(128)S(1)} %copy-done.2, bf16[12,2,256,128]{3,2,1,0:T(8,128)(2,1)S(1)} %bitcast.67, ...), custom_call_target="tpu_custom_call" | custom-call | tf_op jit(solution)/shard_map/pick/pallas_call | solution.py:134
  31.1 0.9 copy-done.1
  32.0 1.9 %collective-permute-start.5 = (bf16[3,2,2,256,128]{4,3,2,1,0:T(8,128)(2,1)}, bf16[3,2,2,256,128]{4,3,2,1,0:T(8,128)(2,1)}, u32[]{:S(2)}, u32[]{:S(2)}) collective-permute-start(bf16[3,2,2,256,128]{4,3,2,1,0:T(8,128)(2,1)} %bitcast.7), channel_id=1, source_target_pairs={{0,2},{1,3},{2,0},{3,1},{4,6},{5,7},{6,4},{7,5},{8,10},{9,11},{10,... | collective-permute-start | bytes 2359304 | tf_op jit(solution)/shard_map/ppermute | solution.py:308
  33.9 1.5 %collective-permute-start.6 = (bf16[3,2,2,256,128]{4,3,2,1,0:T(8,128)(2,1)}, bf16[3,2,2,256,128]{4,3,2,1,0:T(8,128)(2,1)}, u32[]{:S(2)}, u32[]{:S(2)}) collective-permute-start(bf16[3,2,2,256,128]{4,3,2,1,0:T(8,128)(2,1)} %bitcast.8), channel_id=1, source_target_pairs={{0,4},{1,5},{2,6},{3,7},{4,0},{5,1},{6,2},{7,3},{8,12},{9,13},{10,... | collective-permute-start | bytes 2359304 | tf_op jit(solution)/shard_map/ppermute | solution.py:308
  35.4 1.2 copy-done.4
  36.6 0.8 copy-done.5
  37.3 0.8 copy-done.6
  38.1 5.6 %precondition.1 = bf16[16,128,256]{2,1,0:T(8,128)(2,1)} custom-call(bf16[4096,128]{1,0:T(8,128)(2,1)S(1)} %copy-done.4, f32[64,64]{1,0:T(8,128)S(1)} %copy-done.5, f32[64,64]{1,0:T(8,128)S(1)} %copy-done.6, f32[256,16]{1,0:T(8,128)S(1)} %bitcast.71), custom_call_target="tpu_custom_call" | custom-call | flops 3000000000 | bytes 2097152 | tf_op jit(solution)/shard_map/precondition/pallas_call | solution.py:99
  43.7 6.5 %all-to-all-done.first = bf16[16,256,128]{2,1,0:T(8,128)(2,1)S(1)} async-done(((bf16[16,256,128]{2,1,0:T(8,128)(2,1)}), bf16[16,256,128]{2,1,0:T(8,128)(2,1)S(1)}, u32[]{:S(2)}, u32[]{:S(2)}) %all-to-all-start) | async-done | bytes 1048608 | tf_op jit(solution)/shard_map/all_to_all | solution.py:311
  50.2 6.7 %all-to-all-start.1 = ((bf16[16,128,256]{2,1,0:T(8,128)(2,1)}), bf16[16,128,256]{2,1,0:T(8,128)(2,1)S(1)}, u32[]{:S(2)}, u32[]{:S(2)}) async-start(bf16[16,128,256]{2,1,0:T(8,128)(2,1)} %precondition.1), calls=%async_computation.1 | async-start | bytes 2097152 | tf_op jit(solution)/shard_map/all_to_all | solution.py:311
  56.9 0.6 fusion.9
  58.8 11.1 %collective-permute-done.6 = bf16[3,2,2,256,128]{4,3,2,1,0:T(8,128)(2,1)} collective-permute-done((bf16[3,2,2,256,128]{4,3,2,1,0:T(8,128)(2,1)}, bf16[3,2,2,256,128]{4,3,2,1,0:T(8,128)(2,1)}, u32[]{:S(2)}, u32[]{:S(2)}) %collective-permute-start.6) | collective-permute-done | bytes 786464 | tf_op jit(solution)/shard_map/ppermute | solution.py:308
  69.9 1.2 broadcast_select_fusion
  71.1 0.8 constant_dynamic-slice_fusion
  71.9 0.8 copy.33
  73.0 13.0 %collective-permute-done.8 = bf16[3,2,256,128]{3,2,0,1:T(8,128)(2,1)} collective-permute-done((bf16[3,2,256,128]{3,2,0,1:T(8,128)(2,1)}, bf16[3,2,256,128]{3,2,0,1:T(8,128)(2,1)}, u32[]{:S(2)}, u32[]{:S(2)}) %collective-permute-start.8) | collective-permute-done | bytes 393248 | tf_op jit(solution)/shard_map/ppermute | solution.py:308
  86.1 3.0 %collective-permute-done.7 = bf16[3,2,256,128]{3,2,0,1:T(8,128)(2,1)} collective-permute-done((bf16[3,2,256,128]{3,2,0,1:T(8,128)(2,1)S(1)}, bf16[3,2,256,128]{3,2,0,1:T(8,128)(2,1)}, u32[]{:S(2)}, u32[]{:S(2)}) %collective-permute-start.7) | collective-permute-done | bytes 393248 | tf_op jit(solution)/shard_map/ppermute | solution.py:308
  89.3 2.6 %collective-permute-start.10 = (bf16[3,256,128]{2,1,0:T(8,128)(2,1)S(1)}, bf16[3,256,128]{2,1,0:T(8,128)(2,1)S(1)}, u32[]{:S(2)}, u32[]{:S(2)}) collective-permute-start(bf16[3,256,128]{2,1,0:T(8,128)(2,1)S(1)} %get-tuple-element.52), channel_id=1, source_target_pairs={{0,8},{1,9},{2,10},{3,11},{4,12},{5,13},{6,14},{7,15},{8,0},{9,1},... | collective-permute-start | bytes 589832 | tf_op jit(solution)/shard_map/ppermute | solution.py:308
  91.9 0.4 collective-permute-start.9
  92.3 14.2 %collective-permute-done.10 = bf16[3,256,128]{2,1,0:T(8,128)(2,1)S(1)} collective-permute-done((bf16[3,256,128]{2,1,0:T(8,128)(2,1)S(1)}, bf16[3,256,128]{2,1,0:T(8,128)(2,1)S(1)}, u32[]{:S(2)}, u32[]{:S(2)}) %collective-permute-start.10) | collective-permute-done | bytes 196640 | tf_op jit(solution)/shard_map/ppermute | solution.py:308
  106.5 2.9 %collective-permute-done.9 = bf16[3,256,128]{2,1,0:T(8,128)(2,1)} collective-permute-done((bf16[3,256,128]{2,1,0:T(8,128)(2,1)S(1)}, bf16[3,256,128]{2,1,0:T(8,128)(2,1)}, u32[]{:S(2)}, u32[]{:S(2)}) %collective-permute-start.9) | collective-permute-done | bytes 196640 | tf_op jit(solution)/shard_map/ppermute | solution.py:308
  109.4 0.9 bitcast_select_fusion.3
  110.5 1.2 partial_scores.3
  111.8 1.2 partial_scores.2
  113.0 0.6 collective-permute-start.11
  113.7 0.5 collective-permute-start.15
  114.3 0.8 collective-permute-done.11
  115.2 2.5 %collective-permute-start.12 = (bf16[2,2,128,128]{3,2,1,0:T(8,128)(2,1)S(1)}, bf16[2,2,128,128]{3,2,1,0:T(8,128)(2,1)S(1)}, u32[]{:S(2)}, u32[]{:S(2)}) collective-permute-start(bf16[2,2,128,128]{3,2,1,0:T(8,128)(2,1)S(1)} %fusion), channel_id=1, source_target_pairs={{0,2},{1,3},{2,0},{3,1},{4,6},{5,7},{6,4},{7,5},{8,10},{9,11},{10,... | collective-permute-start | bytes 393224 | tf_op jit(solution)/shard_map/ppermute | solution.py:308
  117.7 1.7 %collective-permute-done.15 = bf16[2,2,128,128]{3,2,1,0:T(8,128)(2,1)S(1)} collective-permute-done((bf16[2,2,128,128]{3,2,1,0:T(8,128)(2,1)S(1)}, bf16[2,2,128,128]{3,2,1,0:T(8,128)(2,1)S(1)}, u32[]{:S(2)}, u32[]{:S(2)}) %collective-permute-start.15) | collective-permute-done | bytes 131104 | tf_op jit(solution)/shard_map/ppermute | solution.py:308
  119.4 2.5 %collective-permute-start.16 = (f32[2,128,128]{2,1,0:T(8,128)S(1)}, f32[2,128,128]{2,1,0:T(8,128)S(1)}, u32[]{:S(2)}, u32[]{:S(2)}) collective-permute-start(f32[2,128,128]{2,1,0:T(8,128)S(1)} %dynamic-slice_bitcast_fusion.2), channel_id=1, source_target_pairs={{0,2},{1,3},{2,0},{3,1},{4,6},{5,7},{6,4},{7,5},{8,10},{9,11},{10,... | collective-permute-start | bytes 393224 | tf_op jit(solution)/shard_map/ppermute | solution.py:308
  122.0 0.5 collective-permute-start.13
  122.4 2.4 %collective-permute-done.16 = f32[2,128,128]{2,1,0:T(8,128)S(1)} collective-permute-done((f32[2,128,128]{2,1,0:T(8,128)S(1)}, f32[2,128,128]{2,1,0:T(8,128)S(1)}, u32[]{:S(2)}, u32[]{:S(2)}) %collective-permute-start.16) | collective-permute-done | bytes 131104 | tf_op jit(solution)/shard_map/ppermute | solution.py:308
  124.9 2.1 %collective-permute-done.13 = f32[2,128,128]{2,1,0:T(8,128)S(1)} collective-permute-done((f32[2,128,128]{2,1,0:T(8,128)S(1)}, f32[2,128,128]{2,1,0:T(8,128)S(1)}, u32[]{:S(2)}, u32[]{:S(2)}) %collective-permute-start.13) | collective-permute-done | bytes 131104 | tf_op jit(solution)/shard_map/ppermute | solution.py:308
  127.1 1.3 collective-permute-start.17
  128.4 6.1 %collective-permute-done.17 = f32[2,128,128]{2,1,0:T(8,128)S(1)} collective-permute-done((f32[2,128,128]{2,1,0:T(8,128)S(1)}, f32[2,128,128]{2,1,0:T(8,128)S(1)}, u32[]{:S(2)}, u32[]{:S(2)}) %collective-permute-start.17) | collective-permute-done | bytes 131104 | tf_op jit(solution)/shard_map/ppermute | solution.py:308
  134.4 0.7 fusion.6
  (53 shorter events, 1.9 us)
Async XLA Ops:
  0.8 1.3 collective-permute-start
  2.1 4.4 %collective-permute-start.1 = (s32[4,2]{0,1:T(2,128)S(1)}, s32[4,2]{0,1:T(2,128)S(1)}, u32[]{:S(2)}, u32[]{:S(2)}) collective-permute-start(s32[4,2]{0,1:T(2,128)S(1)} %add_select_fusion), channel_id=1, source_target_pairs={{0,2},{1,3},{2,0},{3,1},{4,6},{5,7},{6,4},{7,5},{8,10},{9,11},{10,... | collective-permute-start | bytes 104 | tf_op jit(solution)/shard_map/ppermute | solution.py:308
  6.6 3.6 %collective-permute-start.2 = (s32[8,2]{0,1:T(2,128)S(1)}, s32[8,2]{0,1:T(2,128)S(1)}, u32[]{:S(2)}, u32[]{:S(2)}) collective-permute-start(s32[8,2]{0,1:T(2,128)S(1)} %add_select_fusion.1), channel_id=1, source_target_pairs={{0,4},{1,5},{2,6},{3,7},{4,0},{5,1},{6,2},{7,3},{8,12},{9,13},{10,... | collective-permute-start | bytes 200 | tf_op jit(solution)/shard_map/ppermute | solution.py:308
  10.3 4.6 %collective-permute-start.3 = (s32[16,2]{0,1:T(2,128)S(1)}, s32[16,2]{0,1:T(2,128)S(1)}, u32[]{:S(2)}, u32[]{:S(2)}) collective-permute-start(s32[16,2]{0,1:T(2,128)S(1)} %add_select_fusion.2), channel_id=1, source_target_pairs={{0,8},{1,9},{2,10},{3,11},{4,12},{5,13},{6,14},{7,15},{8,0},{9,1},... | collective-permute-start | bytes 392 | tf_op jit(solution)/shard_map/ppermute | solution.py:308
  20.3 6.5 %copy-start.9 = (f32[64]{0:T(128)S(1)}, f32[64]{0:T(128)}, u32[]{:S(2)}) copy-start(f32[64]{0:T(128)} %param.14) | copy-start | bytes 772
  20.3 7.4 %copy-start.8 = (f32[64]{0:T(128)S(1)}, f32[64]{0:T(128)}, u32[]{:S(2)}) copy-start(f32[64]{0:T(128)} %param.13) | copy-start | bytes 772
  20.3 7.5 %copy-start = (bf16[3,8,256,128]{3,2,1,0:T(8,128)(2,1)S(1)}, bf16[3,8,256,128]{3,2,1,0:T(8,128)(2,1)}, u32[]{:S(2)}) copy-start(bf16[3,8,256,128]{3,2,1,0:T(8,128)(2,1)} %get-tuple-element.34) | copy-start | bytes 4718596
  20.3 7.5 %copy-start.2 = (s32[2]{0:T(128)S(1)}, s32[2]{0:T(128)}, u32[]{:S(2)}) copy-start(s32[2]{0:T(128)} %get-tuple-element.33.where) | copy-start | bytes 28
  20.3 7.4 %collective-permute-start.4 = (bf16[3,8,256,128]{3,2,1,0:T(8,128)(2,1)}, bf16[3,8,256,128]{3,2,1,0:T(8,128)(2,1)}, u32[]{:S(2)}, u32[]{:S(2)}) collective-permute-start(bf16[3,8,256,128]{3,2,1,0:T(8,128)(2,1)} %get-tuple-element.35), channel_id=1, source_target_pairs={{0,1},{1,0},{2,3},{3,2},{4,5},{5,4},{6,7},{7,6},{8,9},{9,8},{10,11... | collective-permute-start | bytes 4718600 | tf_op jit(solution)/shard_map/ppermute | solution.py:308
  20.4 29.8 %all-to-all-start = ((bf16[16,256,128]{2,1,0:T(8,128)(2,1)}), bf16[16,256,128]{2,1,0:T(8,128)(2,1)S(1)}, u32[]{:S(2)}, u32[]{:S(2)}) async-start(bf16[16,256,128]{2,1,0:T(8,128)(2,1)} %bitcast.77), calls=%async_computation | async-start | bytes 2097152 | tf_op jit(solution)/shard_map/all_to_all | solution.py:311
  31.1 0.9 copy-start.1
  32.0 26.9 %collective-permute-start.5 = (bf16[3,2,2,256,128]{4,3,2,1,0:T(8,128)(2,1)}, bf16[3,2,2,256,128]{4,3,2,1,0:T(8,128)(2,1)}, u32[]{:S(2)}, u32[]{:S(2)}) collective-permute-start(bf16[3,2,2,256,128]{4,3,2,1,0:T(8,128)(2,1)} %bitcast.7), channel_id=1, source_target_pairs={{0,2},{1,3},{2,0},{3,1},{4,6},{5,7},{6,4},{7,5},{8,10},{9,11},{10,... | collective-permute-start | bytes 2359304 | tf_op jit(solution)/shard_map/ppermute | solution.py:308
  33.9 36.0 %collective-permute-start.6 = (bf16[3,2,2,256,128]{4,3,2,1,0:T(8,128)(2,1)}, bf16[3,2,2,256,128]{4,3,2,1,0:T(8,128)(2,1)}, u32[]{:S(2)}, u32[]{:S(2)}) collective-permute-start(bf16[3,2,2,256,128]{4,3,2,1,0:T(8,128)(2,1)} %bitcast.8), channel_id=1, source_target_pairs={{0,4},{1,5},{2,6},{3,7},{4,0},{5,1},{6,2},{7,3},{8,12},{9,13},{10,... | collective-permute-start | bytes 2359304 | tf_op jit(solution)/shard_map/ppermute | solution.py:308
  35.4 1.2 copy-start.4
  36.6 0.8 copy-start.5
  37.3 0.8 copy-start.6
  50.2 39.1 %all-to-all-start.1 = ((bf16[16,128,256]{2,1,0:T(8,128)(2,1)}), bf16[16,128,256]{2,1,0:T(8,128)(2,1)S(1)}, u32[]{:S(2)}, u32[]{:S(2)}) async-start(bf16[16,128,256]{2,1,0:T(8,128)(2,1)} %precondition.1), calls=%async_computation.1 | async-start | bytes 2097152 | tf_op jit(solution)/shard_map/all_to_all | solution.py:311
  72.7 13.4 %collective-permute-start.8 = (bf16[3,2,256,128]{3,2,0,1:T(8,128)(2,1)}, bf16[3,2,256,128]{3,2,0,1:T(8,128)(2,1)}, u32[]{:S(2)}, u32[]{:S(2)}) collective-permute-start(bf16[3,2,256,128]{3,2,0,1:T(8,128)(2,1)} %bitcast.64), channel_id=1, source_target_pairs={{0,2},{1,3},{2,0},{3,1},{4,6},{5,7},{6,4},{7,5},{8,10},{9,11},{10,... | collective-permute-start | bytes 1179656 | tf_op jit(solution)/shard_map/ppermute | solution.py:308
  72.8 16.3 %copy-start.7 = (bf16[3,2,1,256,128]{4,3,2,1,0:T(8,128)(2,1)S(1)}, bf16[3,2,1,256,128]{4,3,2,1,0:T(8,128)(2,1)}, u32[]{:S(2)}) copy-start(bf16[3,2,1,256,128]{4,3,2,1,0:T(8,128)(2,1)} %get-tuple-element.59) | copy-start | bytes 1179652
  73.0 16.1 %collective-permute-start.7 = (bf16[3,2,256,128]{3,2,0,1:T(8,128)(2,1)S(1)}, bf16[3,2,256,128]{3,2,0,1:T(8,128)(2,1)}, u32[]{:S(2)}, u32[]{:S(2)}) collective-permute-start(bf16[3,2,256,128]{3,2,0,1:T(8,128)(2,1)S(1)} %bitcast.78), channel_id=1, source_target_pairs={{0,4},{1,5},{2,6},{3,7},{4,0},{5,1},{6,2},{7,3},{8,12},{9,13},{10,... | collective-permute-start | bytes 1179656 | tf_op jit(solution)/shard_map/ppermute | solution.py:308
  89.2 21.3 %copy-start.3 = (s32[2,32]{1,0:T(2,128)S(1)}, s32[2,32]{1,0:T(2,128)}, u32[]{:S(2)}) copy-start(s32[2,32]{1,0:T(2,128)} %get-tuple-element.32.rows) | copy-start | bytes 772
  89.3 17.2 %collective-permute-start.10 = (bf16[3,256,128]{2,1,0:T(8,128)(2,1)S(1)}, bf16[3,256,128]{2,1,0:T(8,128)(2,1)S(1)}, u32[]{:S(2)}, u32[]{:S(2)}) collective-permute-start(bf16[3,256,128]{2,1,0:T(8,128)(2,1)S(1)} %get-tuple-element.52), channel_id=1, source_target_pairs={{0,8},{1,9},{2,10},{3,11},{4,12},{5,13},{6,14},{7,15},{8,0},{9,1},... | collective-permute-start | bytes 589832 | tf_op jit(solution)/shard_map/ppermute | solution.py:308
  91.9 17.6 %collective-permute-start.9 = (bf16[3,256,128]{2,1,0:T(8,128)(2,1)S(1)}, bf16[3,256,128]{2,1,0:T(8,128)(2,1)}, u32[]{:S(2)}, u32[]{:S(2)}) collective-permute-start(bf16[3,256,128]{2,1,0:T(8,128)(2,1)S(1)} %get-tuple-element.51), channel_id=1, source_target_pairs={{0,8},{1,9},{2,10},{3,11},{4,12},{5,13},{6,14},{7,15},{8,0},{9,1},... | collective-permute-start | bytes 589832 | tf_op jit(solution)/shard_map/ppermute | solution.py:308
  111.7 2.0 %collective-permute-start.14 = (f32[8,128,128]{2,1,0:T(8,128)S(1)}, f32[8,128,128]{2,1,0:T(8,128)S(1)}, u32[]{:S(2)}, u32[]{:S(2)}) collective-permute-start(f32[8,128,128]{2,1,0:T(8,128)S(1)} %get-tuple-element.58), channel_id=1, source_target_pairs={{0,1},{1,0},{2,3},{3,2},{4,5},{5,4},{6,7},{7,6},{8,9},{9,8},{10,11... | collective-permute-start | bytes 1572872 | tf_op jit(solution)/shard_map/ppermute | solution.py:308
  113.0 2.1 %collective-permute-start.11 = (f32[8,128,128]{2,1,0:T(8,128)S(1)}, f32[8,128,128]{2,1,0:T(8,128)S(1)}, u32[]{:S(2)}, u32[]{:S(2)}) collective-permute-start(f32[8,128,128]{2,1,0:T(8,128)S(1)} %get-tuple-element.56), channel_id=1, source_target_pairs={{0,1},{1,0},{2,3},{3,2},{4,5},{5,4},{6,7},{7,6},{8,9},{9,8},{10,11... | collective-permute-start | bytes 1572872 | tf_op jit(solution)/shard_map/ppermute | solution.py:308
  113.7 5.6 %collective-permute-start.15 = (bf16[2,2,128,128]{3,2,1,0:T(8,128)(2,1)S(1)}, bf16[2,2,128,128]{3,2,1,0:T(8,128)(2,1)S(1)}, u32[]{:S(2)}, u32[]{:S(2)}) collective-permute-start(bf16[2,2,128,128]{3,2,1,0:T(8,128)(2,1)S(1)} %fusion.1), channel_id=1, source_target_pairs={{0,4},{1,5},{2,6},{3,7},{4,0},{5,1},{6,2},{7,3},{8,12},{9,13},{10,... | collective-permute-start | bytes 393224 | tf_op jit(solution)/shard_map/ppermute | solution.py:308
  115.2 6.7 %collective-permute-start.12 = (bf16[2,2,128,128]{3,2,1,0:T(8,128)(2,1)S(1)}, bf16[2,2,128,128]{3,2,1,0:T(8,128)(2,1)S(1)}, u32[]{:S(2)}, u32[]{:S(2)}) collective-permute-start(bf16[2,2,128,128]{3,2,1,0:T(8,128)(2,1)S(1)} %fusion), channel_id=1, source_target_pairs={{0,2},{1,3},{2,0},{3,1},{4,6},{5,7},{6,4},{7,5},{8,10},{9,11},{10,... | collective-permute-start | bytes 393224 | tf_op jit(solution)/shard_map/ppermute | solution.py:308
  119.4 5.5 %collective-permute-start.16 = (f32[2,128,128]{2,1,0:T(8,128)S(1)}, f32[2,128,128]{2,1,0:T(8,128)S(1)}, u32[]{:S(2)}, u32[]{:S(2)}) collective-permute-start(f32[2,128,128]{2,1,0:T(8,128)S(1)} %dynamic-slice_bitcast_fusion.2), channel_id=1, source_target_pairs={{0,2},{1,3},{2,0},{3,1},{4,6},{5,7},{6,4},{7,5},{8,10},{9,11},{10,... | collective-permute-start | bytes 393224 | tf_op jit(solution)/shard_map/ppermute | solution.py:308
  122.0 5.1 %collective-permute-start.13 = (f32[2,128,128]{2,1,0:T(8,128)S(1)}, f32[2,128,128]{2,1,0:T(8,128)S(1)}, u32[]{:S(2)}, u32[]{:S(2)}) collective-permute-start(f32[2,128,128]{2,1,0:T(8,128)S(1)} %dynamic-slice_bitcast_fusion.3), channel_id=1, source_target_pairs={{0,4},{1,5},{2,6},{3,7},{4,0},{5,1},{6,2},{7,3},{8,12},{9,13},{10,... | collective-permute-start | bytes 393224 | tf_op jit(solution)/shard_map/ppermute | solution.py:308
  127.1 7.4 %collective-permute-start.17 = (f32[2,128,128]{2,1,0:T(8,128)S(1)}, f32[2,128,128]{2,1,0:T(8,128)S(1)}, u32[]{:S(2)}, u32[]{:S(2)}) collective-permute-start(f32[2,128,128]{2,1,0:T(8,128)S(1)} %fusion.3), channel_id=1, source_target_pairs={{0,8},{1,9},{2,10},{3,11},{4,12},{5,13},{6,14},{7,15},{8,0},{9,1},... | collective-permute-start | bytes 393224 | tf_op jit(solution)/shard_map/ppermute | solution.py:308

commit v6 on v5

--- a/solution.py
+++ b/solution.py
@@ -141,12 +141,11 @@
     )(me.reshape(1), where, *sources)
 
 
-def score_kernel(which, per_device, me_ref, rows, train, first, extra, keep, send):
+def score_kernel(per_device, me_ref, rows, train, first, extra, keep, send):
     core = me_ref[0] & 1
     devices = first.shape[0]
 
-    def tile(device):
-        pair = device * per_device + which
+    def tile(pair):
         slot = rows[1, pair]
         a = first[jnp.minimum(slot, devices - 1)]
         b = extra[jnp.maximum(slot - devices, 0)]
@@ -154,19 +153,20 @@
         return mm(train[rows[0, pair]], q)
 
     def step(h, carry):
-        keep[h] = tile(2 * h + core)
-        send[h] = tile(2 * h + 1 - core)
+        base = h // per_device * (2 * per_device) + h % per_device
+        keep[h] = tile(base + core * per_device)
+        send[h] = tile(base + (1 - core) * per_device)
         return carry
 
     lax.fori_loop(0, keep.shape[0], step, 0, unroll=4)
 
 
-def partial_scores(which, per_device, me, rows, train, first, extra):
-    half = rows.shape[1] // (2 * per_device)
+def partial_scores(per_device, me, rows, train, first, extra):
+    half = rows.shape[1] // 2
     tiles = jax.ShapeDtypeStruct((half, COLS, COLS), f32)
     whole = pl.BlockSpec(memory_space=pltpu.VMEM)
     return pl.pallas_call(
-        functools.partial(score_kernel, which, per_device),
+        functools.partial(score_kernel, per_device),
         out_shape=(tiles, tiles),
         in_specs=[pl.BlockSpec(memory_space=pltpu.SMEM)] * 2 + [whole] * 3,
         out_specs=(whole, whole),
@@ -367,10 +367,12 @@
             chain[:3] = parts[rank][0], others[rank], chain[3][k]
     extra_share = jnp.concatenate([arrived(hots[r], chain[2], chain[0], chain[1]) for r, chain in enumerate(chains)])
 
+    keep, send = partial_scores(per_device, me, rows, train_share, first_share, extra_share)
+    tiles = (keep + across(send, 0)).reshape((2,) * (bits - 1) + (per_device, COLS, COLS))
+
     sums, middle = [], list(range(1, bits - 1))
     for pair in range(per_device):
-        keep, send = partial_scores(pair, per_device, me, rows, train_share, first_share, extra_share)
-        x, left = (keep + across(send, 0)).reshape((2,) * (bits - 1) + (COLS, COLS)), list(range(1, bits))
+        x, left = tiles[..., pair, :, :], list(range(1, bits))
         turn = pair % 2
         for k, b in enumerate(middle[turn:] + middle[:turn]):
             axis = sorted(left, reverse=True).index(b)

time: 136 us -> 136 us (level)
  waiting for transfers between devices: 69.4 us -> 77.3 us
  local copies, waits for them, and re-layouts: 7.16 us -> 3.94 us
  starting transfers between devices: 36 us -> 33.7 us
    ppermute x18 -> x17, waiting for transfers between devices: 62.9 us -> 67.6 us  [across(): return lax.ppermute(x, 'dp', [(d, d ^ 1 << b) for d in range(devices)])]
    all_to_all x2, waiting for transfers between devices: 6.46 us -> 9.67 us  [to_all(): return lax.all_to_all(x, 'dp', split_axis=0, concat_axis=0, tiled=True)]
    ppermute x18 -> x17, starting transfers between devices: 22.9 us -> 20.5 us  [across(): return lax.ppermute(x, 'dp', [(d, d ^ 1 << b) for d in range(devices)])]
    unnamed x21 -> x25, local copies, waits for them, and re-layouts: 4.42 us -> 2.64 us
    pallas_call x1, Pallas kernels: 3.28 us -> 1.92 us  [pick(): pl.pallas_call(functools.partial(pick_kernel, plan_of), out_shape=shapes,...]
  transfers between devices with their start and end apart: 20 -> 19, of which waited for: 16 -> 15; matrix products, arithmetic and copies ran while one was open for 3% -> 2% of each run, Pallas kernels for 7% -> 6%
where the time goes in v6:
time: 136 us; the launch traced here: 135 us
  waiting for transfers between devices  77.3 us (57%)
  starting transfers between devices  33.7 us (25%)
  Pallas kernels  14.7 us (11%)
  local copies, waits for them, and re-layouts  3.94 us (3%)
  other arithmetic  3.36 us (2%)
  between operations  2.35 us (2%)
    ppermute x17, waiting for transfers between devices, across(): return lax.ppermute(x, 'dp', [(d, d ^ 1 << b) for d in range(devices)])  67.6 us
    ppermute x17, starting transfers between devices, across(): return lax.ppermute(x, 'dp', [(d, d ^ 1 << b) for d in range(devices)])  20.5 us
    all_to_all x2, starting transfers between devices, to_all(): return lax.all_to_all(x, 'dp', split_axis=0, concat_axis=0, tiled=True)  13.3 us
    all_to_all x2, waiting for transfers between devices, to_all(): return lax.all_to_all(x, 'dp', split_axis=0, concat_axis=0, tiled=True)  9.67 us
    pallas_call x1, Pallas kernels, precondition(): pl.pallas_call(precondition_kernel, out_shape=jax.ShapeDtypeStruct((chunk...  5.65 us
    pallas_call x1, Pallas kernels, plan(): pl.pallas_call(plan_kernel, out_shape=(jax.ShapeDtypeStruct((2, pairs.sha...  4.54 us
  transfers between devices with their start and end apart: 19, of which 15 were waited for; matrix products, arithmetic and copies ran while one was open for 2% of the time, Pallas kernels for 6%

profile of v6, /device:TPU:0, one launch (start us, length us, event | category | flops | bytes accessed | tf_op | source)
XLA Modules:
  0.0 135.3 jit_solution(1989309507371297250)
XLA Ops:
  0.0 0.8 copy.20
  0.8 0.5 collective-permute-start
  1.2 0.8 collective-permute-done
  2.0 0.1 add_select_fusion
  2.1 2.8 %collective-permute-start.1 = (s32[4,2]{0,1:T(2,128)S(1)}, s32[4,2]{0,1:T(2,128)S(1)}, u32[]{:S(2)}, u32[]{:S(2)}) collective-permute-start(s32[4,2]{0,1:T(2,128)S(1)} %add_select_fusion), channel_id=1, source_target_pairs={{0,2},{1,3},{2,0},{3,1},{4,6},{5,7},{6,4},{7,5},{8,10},{9,11},{10,... | collective-permute-start | bytes 104 | tf_op jit(solution)/shard_map/ppermute | solution.py:308
  5.0 1.5 %collective-permute-done.1 = s32[4,2]{0,1:T(2,128)S(1)} collective-permute-done((s32[4,2]{0,1:T(2,128)S(1)}, s32[4,2]{0,1:T(2,128)S(1)}, u32[]{:S(2)}, u32[]{:S(2)}) %collective-permute-start.1) | collective-permute-done | bytes 64 | tf_op jit(solution)/shard_map/ppermute | solution.py:308
  6.6 2.1 %collective-permute-start.2 = (s32[8,2]{0,1:T(2,128)S(1)}, s32[8,2]{0,1:T(2,128)S(1)}, u32[]{:S(2)}, u32[]{:S(2)}) collective-permute-start(s32[8,2]{0,1:T(2,128)S(1)} %add_select_fusion.1), channel_id=1, source_target_pairs={{0,4},{1,5},{2,6},{3,7},{4,0},{5,1},{6,2},{7,3},{8,12},{9,13},{10,... | collective-permute-start | bytes 200 | tf_op jit(solution)/shard_map/ppermute | solution.py:308
  8.7 1.5 %collective-permute-done.2 = s32[8,2]{0,1:T(2,128)S(1)} collective-permute-done((s32[8,2]{0,1:T(2,128)S(1)}, s32[8,2]{0,1:T(2,128)S(1)}, u32[]{:S(2)}, u32[]{:S(2)}) %collective-permute-start.2) | collective-permute-done | bytes 96 | tf_op jit(solution)/shard_map/ppermute | solution.py:308
  10.3 3.0 %collective-permute-start.3 = (s32[16,2]{0,1:T(2,128)S(1)}, s32[16,2]{0,1:T(2,128)S(1)}, u32[]{:S(2)}, u32[]{:S(2)}) collective-permute-start(s32[16,2]{0,1:T(2,128)S(1)} %add_select_fusion.2), channel_id=1, source_target_pairs={{0,8},{1,9},{2,10},{3,11},{4,12},{5,13},{6,14},{7,15},{8,0},{9,1},... | collective-permute-start | bytes 392 | tf_op jit(solution)/shard_map/ppermute | solution.py:308
  13.3 1.5 %collective-permute-done.3 = s32[16,2]{0,1:T(2,128)S(1)} collective-permute-done((s32[16,2]{0,1:T(2,128)S(1)}, s32[16,2]{0,1:T(2,128)S(1)}, u32[]{:S(2)}, u32[]{:S(2)}) %collective-permute-start.3) | collective-permute-done | bytes 160 | tf_op jit(solution)/shard_map/ppermute | solution.py:308
  14.9 0.1 copy.22
  15.0 0.1 copy.23
  15.1 0.6 broadcast_select_fusion.2.pairs
  15.7 4.5 %plan.1 = (s32[2,32]{1,0:T(2,128)}, s32[2]{0:T(128)}, bf16[8,2,256,128]{3,2,1,0:T(8,128)(2,1)}, bf16[3,8,256,128]{3,2,1,0:T(8,128)(2,1)}, bf16[3,8,256,128]{3,2,1,0:T(8,128)(2,1)}) custom-call(s32[1]{0:T(128)} %bitcast.me_ref.me, s32[32,2]{1,0:T(8,128)} %broadcast_select_fusion.2.pairs, bf16[8,2,256,1024]{3,2,1,0:T(8,128)(2,1)} %bitcast.73), custom_call_target="tpu_custom_call" | custom-call | tf_op jit(solution)/shard_map/plan/pallas_call | solution.py:275
  20.4 6.6 %all-to-all-start = ((bf16[16,256,128]{2,1,0:T(8,128)(2,1)}), bf16[16,256,128]{2,1,0:T(8,128)(2,1)}, u32[]{:S(2)}, u32[]{:S(2)}) async-start(bf16[16,256,128]{2,1,0:T(8,128)(2,1)} %bitcast.75), calls=%async_computation | async-start | bytes 2097152 | tf_op jit(solution)/shard_map/all_to_all | solution.py:311
  27.0 0.1 reshape.48
  27.1 0.1 copy.24
  27.9 0.1 add_divide_fusion
  28.0 1.9 %pick.1 = (bf16[12,256,128]{2,1,0:T(8,128)(2,1)S(1)}, bf16[12,256,128]{2,1,0:T(8,128)(2,1)}, bf16[6,512,128]{2,1,0:T(8,128)(2,1)S(1)}, bf16[6,512,128]{2,1,0:T(8,128)(2,1)}) custom-call(s32[1]{0:T(128)} %bitcast.me_ref.me, s32[2]{0:T(128)S(1)} %copy-done.5, bf16[12,2,256,128]{3,2,1,0:T(8,128)(2,1)S(1)} %bitcast.66, bf16[12,2,256,128]{3,2,1,0:T(8,128)(2,1)S(1)} %bitcast.68, ...), custom_call_target="tpu_custom_call" | custom-call | tf_op jit(solution)/shard_map/pick/pallas_call | solution.py:134
  29.9 0.9 copy-done.1
  30.9 0.9 copy-done.3
  31.8 1.9 %collective-permute-start.5 = (bf16[3,2,2,256,128]{4,3,2,1,0:T(8,128)(2,1)}, bf16[3,2,2,256,128]{4,3,2,1,0:T(8,128)(2,1)}, u32[]{:S(2)}, u32[]{:S(2)}) collective-permute-start(bf16[3,2,2,256,128]{4,3,2,1,0:T(8,128)(2,1)} %bitcast.7), channel_id=1, source_target_pairs={{0,2},{1,3},{2,0},{3,1},{4,6},{5,7},{6,4},{7,5},{8,10},{9,11},{10,... | collective-permute-start | bytes 2359304 | tf_op jit(solution)/shard_map/ppermute | solution.py:308
  33.6 1.5 %collective-permute-start.6 = (bf16[3,2,2,256,128]{4,3,2,1,0:T(8,128)(2,1)}, bf16[3,2,2,256,128]{4,3,2,1,0:T(8,128)(2,1)}, u32[]{:S(2)}, u32[]{:S(2)}) collective-permute-start(bf16[3,2,2,256,128]{4,3,2,1,0:T(8,128)(2,1)} %bitcast.8), channel_id=1, source_target_pairs={{0,4},{1,5},{2,6},{3,7},{4,0},{5,1},{6,2},{7,3},{8,12},{9,13},{10,... | collective-permute-start | bytes 2359304 | tf_op jit(solution)/shard_map/ppermute | solution.py:308
  35.1 5.6 %precondition.1 = bf16[16,128,256]{2,1,0:T(8,128)(2,1)} custom-call(bf16[4096,128]{1,0:T(8,128)(2,1)S(1)} %copy-done.7, f32[64,64]{1,0:T(8,128)S(1)} %copy-done.8, f32[64,64]{1,0:T(8,128)S(1)} %copy-done.9, f32[256,16]{1,0:T(8,128)S(1)} %bitcast.72), custom_call_target="tpu_custom_call" | custom-call | flops 3000000000 | bytes 2097152 | tf_op jit(solution)/shard_map/precondition/pallas_call | solution.py:99
  40.8 9.7 %all-to-all-done.first = bf16[16,256,128]{2,1,0:T(8,128)(2,1)} async-done(((bf16[16,256,128]{2,1,0:T(8,128)(2,1)}), bf16[16,256,128]{2,1,0:T(8,128)(2,1)}, u32[]{:S(2)}, u32[]{:S(2)}) %all-to-all-start) | async-done | bytes 1048608 | tf_op jit(solution)/shard_map/all_to_all | solution.py:311
  50.4 6.7 %all-to-all-start.1 = ((bf16[16,128,256]{2,1,0:T(8,128)(2,1)}), bf16[16,128,256]{2,1,0:T(8,128)(2,1)S(1)}, u32[]{:S(2)}, u32[]{:S(2)}) async-start(bf16[16,128,256]{2,1,0:T(8,128)(2,1)} %precondition.1), calls=%async_computation.1 | async-start | bytes 2097152 | tf_op jit(solution)/shard_map/all_to_all | solution.py:311
  57.1 0.6 fusion.10
  59.0 11.0 %collective-permute-done.6 = bf16[3,2,2,256,128]{4,3,2,1,0:T(8,128)(2,1)} collective-permute-done((bf16[3,2,2,256,128]{4,3,2,1,0:T(8,128)(2,1)}, bf16[3,2,2,256,128]{4,3,2,1,0:T(8,128)(2,1)}, u32[]{:S(2)}, u32[]{:S(2)}) %collective-permute-start.6) | collective-permute-done | bytes 786464 | tf_op jit(solution)/shard_map/ppermute | solution.py:308
  70.0 1.3 broadcast_select_fusion
  71.4 0.4 collective-permute-start.8
  72.0 13.8 %collective-permute-done.8 = bf16[3,2,256,128]{3,2,0,1:T(8,128)(2,1)S(1)} collective-permute-done((bf16[3,2,256,128]{3,2,0,1:T(8,128)(2,1)S(1)}, bf16[3,2,256,128]{3,2,0,1:T(8,128)(2,1)S(1)}, u32[]{:S(2)}, u32[]{:S(2)}) %collective-permute-start.8) | collective-permute-done | bytes 393248 | tf_op jit(solution)/shard_map/ppermute | solution.py:308
  85.7 3.3 %collective-permute-done.7 = bf16[3,2,256,128]{3,2,0,1:T(8,128)(2,1)S(1)} collective-permute-done((bf16[3,2,256,128]{3,2,0,1:T(8,128)(2,1)S(1)}, bf16[3,2,256,128]{3,2,0,1:T(8,128)(2,1)S(1)}, u32[]{:S(2)}, u32[]{:S(2)}) %collective-permute-start.7) | collective-permute-done | bytes 393248 | tf_op jit(solution)/shard_map/ppermute | solution.py:308
  89.3 2.6 %collective-permute-start.10 = (bf16[3,256,128]{2,1,0:T(8,128)(2,1)S(1)}, bf16[3,256,128]{2,1,0:T(8,128)(2,1)S(1)}, u32[]{:S(2)}, u32[]{:S(2)}) collective-permute-start(bf16[3,256,128]{2,1,0:T(8,128)(2,1)S(1)} %dynamic-slice_bitcast_fusion), channel_id=1, source_target_pairs={{0,8},{1,9},{2,10},{3,11},{4,12},{5,13},{6,14},{7,15},{8,0},{9,1},... | collective-permute-start | bytes 589832 | tf_op jit(solution)/shard_map/ppermute | solution.py:308
  91.9 0.4 collective-permute-start.9
  92.2 13.6 %collective-permute-done.10 = bf16[3,256,128]{2,1,0:T(8,128)(2,1)S(1)} collective-permute-done((bf16[3,256,128]{2,1,0:T(8,128)(2,1)S(1)}, bf16[3,256,128]{2,1,0:T(8,128)(2,1)S(1)}, u32[]{:S(2)}, u32[]{:S(2)}) %collective-permute-start.10) | collective-permute-done | bytes 196640 | tf_op jit(solution)/shard_map/ppermute | solution.py:308
  105.9 3.4 %collective-permute-done.9 = bf16[3,256,128]{2,1,0:T(8,128)(2,1)S(1)} collective-permute-done((bf16[3,256,128]{2,1,0:T(8,128)(2,1)S(1)}, bf16[3,256,128]{2,1,0:T(8,128)(2,1)S(1)}, u32[]{:S(2)}, u32[]{:S(2)}) %collective-permute-start.9) | collective-permute-done | bytes 196640 | tf_op jit(solution)/shard_map/ppermute | solution.py:308
  109.4 2.6 %partial_scores.1 = (f32[16,128,128]{2,1,0:T(8,128)S(1)}, f32[16,128,128]{2,1,0:T(8,128)S(1)}) custom-call(s32[1]{0:T(128)} %bitcast.me_ref.me, s32[2,32]{1,0:T(2,128)S(1)} %copy-done.6, bf16[16,128,256]{2,1,0:T(8,128)(2,1)S(1)} %all-to-all-done.1.train, bf16[16,256,128]{2,1,0:T(8,128)(2,1)} %all-to-all-done.first, ...), custom_call_target="tpu_custom_call" | custom-call | tf_op jit(solution)/shard_map/partial_scores/pallas_call | solution.py:168
  112.1 2.6 %collective-permute-done.11 = f32[16,128,128]{2,1,0:T(8,128)S(1)} collective-permute-done((f32[16,128,128]{2,1,0:T(8,128)S(1)}, f32[16,128,128]{2,1,0:T(8,128)S(1)}, u32[]{:S(2)}, u32[]{:S(2)}) %collective-permute-start.11) | collective-permute-done | bytes 1048608 | tf_op jit(solution)/shard_map/ppermute | solution.py:308
  114.7 0.1 add.71
  115.1 1.6 %collective-permute-start.12 = (bf16[2,2,128,128]{3,2,1,0:T(8,128)(2,1)S(1)}, bf16[2,2,128,128]{3,2,1,0:T(8,128)(2,1)S(1)}, u32[]{:S(2)}, u32[]{:S(2)}) collective-permute-start(bf16[2,2,128,128]{3,2,1,0:T(8,128)(2,1)S(1)} %fusion), channel_id=1, source_target_pairs={{0,2},{1,3},{2,0},{3,1},{4,6},{5,7},{6,4},{7,5},{8,10},{9,11},{10,... | collective-permute-start | bytes 393224 | tf_op jit(solution)/shard_map/ppermute | solution.py:308
  116.6 3.9 %collective-permute-done.14 = bf16[2,2,128,128]{3,2,1,0:T(8,128)(2,1)S(1)} collective-permute-done((bf16[2,2,128,128]{3,2,1,0:T(8,128)(2,1)S(1)}, bf16[2,2,128,128]{3,2,1,0:T(8,128)(2,1)S(1)}, u32[]{:S(2)}, u32[]{:S(2)}) %collective-permute-start.14) | collective-permute-done | bytes 131104 | tf_op jit(solution)/shard_map/ppermute | solution.py:308
  120.6 1.6 %collective-permute-start.15 = (f32[2,128,128]{2,1,0:T(8,128)S(1)}, f32[2,128,128]{2,1,0:T(8,128)S(1)}, u32[]{:S(2)}, u32[]{:S(2)}) collective-permute-start(f32[2,128,128]{2,1,0:T(8,128)S(1)} %dynamic-slice_bitcast_fusion.2), channel_id=1, source_target_pairs={{0,2},{1,3},{2,0},{3,1},{4,6},{5,7},{6,4},{7,5},{8,10},{9,11},{10,... | collective-permute-start | bytes 393224 | tf_op jit(solution)/shard_map/ppermute | solution.py:308
  122.2 0.4 collective-permute-start.13
  122.6 3.1 %collective-permute-done.15 = f32[2,128,128]{2,1,0:T(8,128)S(1)} collective-permute-done((f32[2,128,128]{2,1,0:T(8,128)S(1)}, f32[2,128,128]{2,1,0:T(8,128)S(1)}, u32[]{:S(2)}, u32[]{:S(2)}) %collective-permute-start.15) | collective-permute-done | bytes 131104 | tf_op jit(solution)/shard_map/ppermute | solution.py:308
  125.7 1.6 %collective-permute-done.13 = f32[2,128,128]{2,1,0:T(8,128)S(1)} collective-permute-done((f32[2,128,128]{2,1,0:T(8,128)S(1)}, f32[2,128,128]{2,1,0:T(8,128)S(1)}, u32[]{:S(2)}, u32[]{:S(2)}) %collective-permute-start.13) | collective-permute-done | bytes 131104 | tf_op jit(solution)/shard_map/ppermute | solution.py:308
  127.3 1.6 %collective-permute-start.16 = (f32[2,128,128]{2,1,0:T(8,128)S(1)}, f32[2,128,128]{2,1,0:T(8,128)S(1)}, u32[]{:S(2)}, u32[]{:S(2)}) collective-permute-start(f32[2,128,128]{2,1,0:T(8,128)S(1)} %fusion.3), channel_id=1, source_target_pairs={{0,8},{1,9},{2,10},{3,11},{4,12},{5,13},{6,14},{7,15},{8,0},{9,1},... | collective-permute-start | bytes 393224 | tf_op jit(solution)/shard_map/ppermute | solution.py:308
  128.9 5.7 %collective-permute-done.16 = f32[2,128,128]{2,1,0:T(8,128)S(1)} collective-permute-done((f32[2,128,128]{2,1,0:T(8,128)S(1)}, f32[2,128,128]{2,1,0:T(8,128)S(1)}, u32[]{:S(2)}, u32[]{:S(2)}) %collective-permute-start.16) | collective-permute-done | bytes 131104 | tf_op jit(solution)/shard_map/ppermute | solution.py:308
  134.6 0.7 fusion.6
  (54 shorter events, 1.2 us)
Async XLA Ops:
  0.8 1.3 collective-permute-start
  2.1 4.4 %collective-permute-start.1 = (s32[4,2]{0,1:T(2,128)S(1)}, s32[4,2]{0,1:T(2,128)S(1)}, u32[]{:S(2)}, u32[]{:S(2)}) collective-permute-start(s32[4,2]{0,1:T(2,128)S(1)} %add_select_fusion), channel_id=1, source_target_pairs={{0,2},{1,3},{2,0},{3,1},{4,6},{5,7},{6,4},{7,5},{8,10},{9,11},{10,... | collective-permute-start | bytes 104 | tf_op jit(solution)/shard_map/ppermute | solution.py:308
  6.6 3.6 %collective-permute-start.2 = (s32[8,2]{0,1:T(2,128)S(1)}, s32[8,2]{0,1:T(2,128)S(1)}, u32[]{:S(2)}, u32[]{:S(2)}) collective-permute-start(s32[8,2]{0,1:T(2,128)S(1)} %add_select_fusion.1), channel_id=1, source_target_pairs={{0,4},{1,5},{2,6},{3,7},{4,0},{5,1},{6,2},{7,3},{8,12},{9,13},{10,... | collective-permute-start | bytes 200 | tf_op jit(solution)/shard_map/ppermute | solution.py:308
  10.3 4.6 %collective-permute-start.3 = (s32[16,2]{0,1:T(2,128)S(1)}, s32[16,2]{0,1:T(2,128)S(1)}, u32[]{:S(2)}, u32[]{:S(2)}) collective-permute-start(s32[16,2]{0,1:T(2,128)S(1)} %add_select_fusion.2), channel_id=1, source_target_pairs={{0,8},{1,9},{2,10},{3,11},{4,12},{5,13},{6,14},{7,15},{8,0},{9,1},... | collective-permute-start | bytes 392 | tf_op jit(solution)/shard_map/ppermute | solution.py:308
  20.3 6.7 %copy-start.11 = (f32[64]{0:T(128)S(1)}, f32[64]{0:T(128)}, u32[]{:S(2)}) copy-start(f32[64]{0:T(128)} %param.14) | copy-start | bytes 772
  20.3 7.6 %copy-start.10 = (f32[64]{0:T(128)S(1)}, f32[64]{0:T(128)}, u32[]{:S(2)}) copy-start(f32[64]{0:T(128)} %param.13) | copy-start | bytes 772
  20.3 7.7 %copy-start = (bf16[3,8,256,128]{3,2,1,0:T(8,128)(2,1)S(1)}, bf16[3,8,256,128]{3,2,1,0:T(8,128)(2,1)}, u32[]{:S(2)}) copy-start(bf16[3,8,256,128]{3,2,1,0:T(8,128)(2,1)} %get-tuple-element.32) | copy-start | bytes 4718596
  20.3 7.7 %copy-start.5 = (s32[2]{0:T(128)S(1)}, s32[2]{0:T(128)}, u32[]{:S(2)}) copy-start(s32[2]{0:T(128)} %get-tuple-element.31.where) | copy-start | bytes 28
  20.3 7.6 %collective-permute-start.4 = (bf16[3,8,256,128]{3,2,1,0:T(8,128)(2,1)}, bf16[3,8,256,128]{3,2,1,0:T(8,128)(2,1)S(1)}, u32[]{:S(2)}, u32[]{:S(2)}) collective-permute-start(bf16[3,8,256,128]{3,2,1,0:T(8,128)(2,1)} %get-tuple-element.33), channel_id=1, source_target_pairs={{0,1},{1,0},{2,3},{3,2},{4,5},{5,4},{6,7},{7,6},{8,9},{9,8},{10,11... | collective-permute-start | bytes 4718600 | tf_op jit(solution)/shard_map/ppermute | solution.py:308
  20.4 30.0 %all-to-all-start = ((bf16[16,256,128]{2,1,0:T(8,128)(2,1)}), bf16[16,256,128]{2,1,0:T(8,128)(2,1)}, u32[]{:S(2)}, u32[]{:S(2)}) async-start(bf16[16,256,128]{2,1,0:T(8,128)(2,1)} %bitcast.75), calls=%async_computation | async-start | bytes 2097152 | tf_op jit(solution)/shard_map/all_to_all | solution.py:311
  28.0 7.1 %copy-start.7 = (bf16[4096,128]{1,0:T(8,128)(2,1)S(1)}, bf16[4096,128]{1,0:T(8,128)(2,1)}, u32[]{:S(2)}) copy-start(bf16[4096,128]{1,0:T(8,128)(2,1)} %train.1) | copy-start | bytes 3145732
  28.0 7.1 %copy-start.8 = (f32[64,64]{1,0:T(8,128)S(1)}, f32[64,64]{1,0:T(8,128)}, u32[]{:S(2)}) copy-start(f32[64,64]{1,0:T(8,128)} %basis_in.1) | copy-start | bytes 49156
  28.0 7.1 %copy-start.9 = (f32[64,64]{1,0:T(8,128)S(1)}, f32[64,64]{1,0:T(8,128)}, u32[]{:S(2)}) copy-start(f32[64,64]{1,0:T(8,128)} %basis_out.1) | copy-start | bytes 49156
  29.9 0.9 copy-start.1
  30.9 0.9 copy-start.3
  31.8 27.2 %collective-permute-start.5 = (bf16[3,2,2,256,128]{4,3,2,1,0:T(8,128)(2,1)}, bf16[3,2,2,256,128]{4,3,2,1,0:T(8,128)(2,1)}, u32[]{:S(2)}, u32[]{:S(2)}) collective-permute-start(bf16[3,2,2,256,128]{4,3,2,1,0:T(8,128)(2,1)} %bitcast.7), channel_id=1, source_target_pairs={{0,2},{1,3},{2,0},{3,1},{4,6},{5,7},{6,4},{7,5},{8,10},{9,11},{10,... | collective-permute-start | bytes 2359304 | tf_op jit(solution)/shard_map/ppermute | solution.py:308
  33.6 36.3 %collective-permute-start.6 = (bf16[3,2,2,256,128]{4,3,2,1,0:T(8,128)(2,1)}, bf16[3,2,2,256,128]{4,3,2,1,0:T(8,128)(2,1)}, u32[]{:S(2)}, u32[]{:S(2)}) collective-permute-start(bf16[3,2,2,256,128]{4,3,2,1,0:T(8,128)(2,1)} %bitcast.8), channel_id=1, source_target_pairs={{0,4},{1,5},{2,6},{3,7},{4,0},{5,1},{6,2},{7,3},{8,12},{9,13},{10,... | collective-permute-start | bytes 2359304 | tf_op jit(solution)/shard_map/ppermute | solution.py:308
  40.8 29.2 %copy-start.2 = (bf16[12,256,128]{2,1,0:T(8,128)(2,1)S(1)}, bf16[12,256,128]{2,1,0:T(8,128)(2,1)}, u32[]{:S(2)}) copy-start(bf16[12,256,128]{2,1,0:T(8,128)(2,1)} %copy-done.1) | copy-start | bytes 2359300
  40.8 29.2 %copy-start.4 = (bf16[6,512,128]{2,1,0:T(8,128)(2,1)S(1)}, bf16[6,512,128]{2,1,0:T(8,128)(2,1)}, u32[]{:S(2)}) copy-start(bf16[6,512,128]{2,1,0:T(8,128)(2,1)} %copy-done.3) | copy-start | bytes 2359300
  50.4 38.8 %all-to-all-start.1 = ((bf16[16,128,256]{2,1,0:T(8,128)(2,1)}), bf16[16,128,256]{2,1,0:T(8,128)(2,1)S(1)}, u32[]{:S(2)}, u32[]{:S(2)}) async-start(bf16[16,128,256]{2,1,0:T(8,128)(2,1)} %precondition.1), calls=%async_computation.1 | async-start | bytes 2097152 | tf_op jit(solution)/shard_map/all_to_all | solution.py:311
  71.4 14.3 %collective-permute-start.8 = (bf16[3,2,256,128]{3,2,0,1:T(8,128)(2,1)S(1)}, bf16[3,2,256,128]{3,2,0,1:T(8,128)(2,1)S(1)}, u32[]{:S(2)}, u32[]{:S(2)}) collective-permute-start(bf16[3,2,256,128]{3,2,0,1:T(8,128)(2,1)S(1)} %bitcast.76), channel_id=1, source_target_pairs={{0,2},{1,3},{2,0},{3,1},{4,6},{5,7},{6,4},{7,5},{8,10},{9,11},{10,... | collective-permute-start | bytes 1179656 | tf_op jit(solution)/shard_map/ppermute | solution.py:308
  71.9 17.2 %collective-permute-start.7 = (bf16[3,2,256,128]{3,2,0,1:T(8,128)(2,1)S(1)}, bf16[3,2,256,128]{3,2,0,1:T(8,128)(2,1)S(1)}, u32[]{:S(2)}, u32[]{:S(2)}) collective-permute-start(bf16[3,2,256,128]{3,2,0,1:T(8,128)(2,1)S(1)} %bitcast.77), channel_id=1, source_target_pairs={{0,4},{1,5},{2,6},{3,7},{4,0},{5,1},{6,2},{7,3},{8,12},{9,13},{10,... | collective-permute-start | bytes 1179656 | tf_op jit(solution)/shard_map/ppermute | solution.py:308
  89.2 20.3 %copy-start.6 = (s32[2,32]{1,0:T(2,128)S(1)}, s32[2,32]{1,0:T(2,128)}, u32[]{:S(2)}) copy-start(s32[2,32]{1,0:T(2,128)} %get-tuple-element.30.rows) | copy-start | bytes 772
  89.3 16.6 %collective-permute-start.10 = (bf16[3,256,128]{2,1,0:T(8,128)(2,1)S(1)}, bf16[3,256,128]{2,1,0:T(8,128)(2,1)S(1)}, u32[]{:S(2)}, u32[]{:S(2)}) collective-permute-start(bf16[3,256,128]{2,1,0:T(8,128)(2,1)S(1)} %dynamic-slice_bitcast_fusion), channel_id=1, source_target_pairs={{0,8},{1,9},{2,10},{3,11},{4,12},{5,13},{6,14},{7,15},{8,0},{9,1},... | collective-permute-start | bytes 589832 | tf_op jit(solution)/shard_map/ppermute | solution.py:308
  91.9 17.4 %collective-permute-start.9 = (bf16[3,256,128]{2,1,0:T(8,128)(2,1)S(1)}, bf16[3,256,128]{2,1,0:T(8,128)(2,1)S(1)}, u32[]{:S(2)}, u32[]{:S(2)}) collective-permute-start(bf16[3,256,128]{2,1,0:T(8,128)(2,1)S(1)} %dynamic-slice_bitcast_fusion.1), channel_id=1, source_target_pairs={{0,8},{1,9},{2,10},{3,11},{4,12},{5,13},{6,14},{7,15},{8,0},{9,1},... | collective-permute-start | bytes 589832 | tf_op jit(solution)/shard_map/ppermute | solution.py:308
  112.0 2.7 %collective-permute-start.11 = (f32[16,128,128]{2,1,0:T(8,128)S(1)}, f32[16,128,128]{2,1,0:T(8,128)S(1)}, u32[]{:S(2)}, u32[]{:S(2)}) collective-permute-start(f32[16,128,128]{2,1,0:T(8,128)S(1)} %get-tuple-element.54), channel_id=1, source_target_pairs={{0,1},{1,0},{2,3},{3,2},{4,5},{5,4},{6,7},{7,6},{8,9},{9,8},{10,11... | collective-permute-start | bytes 3145736 | tf_op jit(solution)/shard_map/ppermute | solution.py:308
  114.9 5.6 %collective-permute-start.14 = (bf16[2,2,128,128]{3,2,1,0:T(8,128)(2,1)S(1)}, bf16[2,2,128,128]{3,2,1,0:T(8,128)(2,1)S(1)}, u32[]{:S(2)}, u32[]{:S(2)}) collective-permute-start(bf16[2,2,128,128]{3,2,1,0:T(8,128)(2,1)S(1)} %fusion.1), channel_id=1, source_target_pairs={{0,4},{1,5},{2,6},{3,7},{4,0},{5,1},{6,2},{7,3},{8,12},{9,13},{10,... | collective-permute-start | bytes 393224 | tf_op jit(solution)/shard_map/ppermute | solution.py:308
  115.1 7.1 %collective-permute-start.12 = (bf16[2,2,128,128]{3,2,1,0:T(8,128)(2,1)S(1)}, bf16[2,2,128,128]{3,2,1,0:T(8,128)(2,1)S(1)}, u32[]{:S(2)}, u32[]{:S(2)}) collective-permute-start(bf16[2,2,128,128]{3,2,1,0:T(8,128)(2,1)S(1)} %fusion), channel_id=1, source_target_pairs={{0,2},{1,3},{2,0},{3,1},{4,6},{5,7},{6,4},{7,5},{8,10},{9,11},{10,... | collective-permute-start | bytes 393224 | tf_op jit(solution)/shard_map/ppermute | solution.py:308
  120.6 5.0 %collective-permute-start.15 = (f32[2,128,128]{2,1,0:T(8,128)S(1)}, f32[2,128,128]{2,1,0:T(8,128)S(1)}, u32[]{:S(2)}, u32[]{:S(2)}) collective-permute-start(f32[2,128,128]{2,1,0:T(8,128)S(1)} %dynamic-slice_bitcast_fusion.2), channel_id=1, source_target_pairs={{0,2},{1,3},{2,0},{3,1},{4,6},{5,7},{6,4},{7,5},{8,10},{9,11},{10,... | collective-permute-start | bytes 393224 | tf_op jit(solution)/shard_map/ppermute | solution.py:308
  122.2 5.0 %collective-permute-start.13 = (f32[2,128,128]{2,1,0:T(8,128)S(1)}, f32[2,128,128]{2,1,0:T(8,128)S(1)}, u32[]{:S(2)}, u32[]{:S(2)}) collective-permute-start(f32[2,128,128]{2,1,0:T(8,128)S(1)} %dynamic-slice_bitcast_fusion.3), channel_id=1, source_target_pairs={{0,4},{1,5},{2,6},{3,7},{4,0},{5,1},{6,2},{7,3},{8,12},{9,13},{10,... | collective-permute-start | bytes 393224 | tf_op jit(solution)/shard_map/ppermute | solution.py:308
  127.3 7.3 %collective-permute-start.16 = (f32[2,128,128]{2,1,0:T(8,128)S(1)}, f32[2,128,128]{2,1,0:T(8,128)S(1)}, u32[]{:S(2)}, u32[]{:S(2)}) collective-permute-start(f32[2,128,128]{2,1,0:T(8,128)S(1)} %fusion.3), channel_id=1, source_target_pairs={{0,8},{1,9},{2,10},{3,11},{4,12},{5,13},{6,14},{7,15},{8,0},{9,1},... | collective-permute-start | bytes 393224 | tf_op jit(solution)/shard_map/ppermute | solution.py:308
